TPU v7x, 256 devices: a whole 4x4x8 slice. The times are simulated.
256 devices in a mesh: ctx: 64 (over x, z, core), head: 4 (over y).
Axes of the slice: x: 4, y: 4, z: 8, core: 2. Of those that a mesh axis runs over, the one named last changes fastest.
Arguments:
- queries: bfloat16 [8192, 6144], P('ctx', 'head'), may hold values from -2 to 2
- keys_in: bfloat16 [8192, 6144], P('ctx', 'head'), may hold values from -2 to 2
- values_in: bfloat16 [8192, 6144], P('ctx', 'head'), may hold values from -26 to 26
- out_grad: bfloat16 [8192, 6144], P('ctx', 'head'), may hold values from -6 to 6
- gated_fading_logarithms: float32 [64, 8192], P('head', 'ctx'), may hold values from -1 to 0
- norm_gain: float32 [6144], P('head'), may hold values from 0.1 to 1.9
Outputs:
- grad_queries: bfloat16 [8192, 6144], P('ctx', 'head')
- grad_keys: bfloat16 [8192, 6144], P('ctx', 'head')
- grad_values: bfloat16 [8192, 6144], P('ctx', 'head')
All inputs are finite; a program needn't handle non-finite values.
Results may differ from a plain program's by a relative error of at most 0.0051.
Values sent between devices are 32-bit elements; how exact they have to be, the bound alone decides.
No kernel may reach another device: no remote copies, remote signals or barrier semaphores. Data moves between devices by JAX's collectives and lax.ppermute only.
A program may use at most 256 MiB of HBM per device.

v0:
```python
import jax
import jax.numpy as jnp
from jax import lax
from jax.sharding import PartitionSpec as P

HEADS = 64
HEAD_DIM = 96
BLOCK = 128


PRECISE_MODE = lax.Precision.HIGHEST


def prefix(value, axis, join, neutral, backward):
    count, mine = (lax.axis_size(axis), lax.axis_index(axis))
    pieces = jax.tree.map(lambda part: lax.all_gather(part, axis), value)
    if backward:
        pieces = jax.tree.map(lambda part: part[::-1], pieces)
        mine = count - 1 - mine
    running = jax.tree.map(
        lambda part, zero: jnp.full_like(part, 0) + jnp.asarray(zero, part.dtype), value, neutral
    )

    def step(position, running):
        longer = join(running, jax.tree.map(lambda part: part[position], pieces))
        return jax.tree.map(lambda new, old: jnp.where(position < mine, new, old), longer, running)

    return lax.fori_loop(0, count - 1, step, running)


def block_weight(decays):
    accum = jnp.cumsum(decays, axis=1)
    span = decays.shape[1]
    rows = lax.broadcasted_iota(jnp.int32, (span, span), 0)
    cols = lax.broadcasted_iota(jnp.int32, (span, span), 1)
    lower = (cols <= rows)[None]
    spread = accum[:, :, None] - accum[:, None, :]
    weight = jnp.where(lower, jnp.exp(jnp.where(lower, spread, 0.0)), 0.0)
    return (accum, weight)


def join_forward(early, late):
    return (early[0] * late[1][:, None, None] + late[0], early[1] * late[1])


def join_backward(early, late):
    return (late[0] + late[1][:, None, None] * early[0], early[1] * late[1])


def local(queries, keys_in, values_in, out_grad, gated_fading_logarithms, norm_gain):
    length = queries.shape[0]
    heads = gated_fading_logarithms.shape[0]
    width = heads * HEAD_DIM
    count = length // BLOCK
    gain = norm_gain.reshape(heads, HEAD_DIM)
    empty = jnp.zeros((heads, HEAD_DIM, HEAD_DIM), jnp.float32)
    unity = jnp.ones((heads,), jnp.float32)
    local_state = empty
    local_decay = unity
    block_queries = queries.reshape(BLOCK, heads, HEAD_DIM)
    segment_lookup_vectors = keys_in.reshape(BLOCK, heads, HEAD_DIM)
    block_values = values_in.reshape(BLOCK, heads, HEAD_DIM)
    grad_block = out_grad.reshape(BLOCK, heads, HEAD_DIM)
    accum, weight = block_weight(gated_fading_logarithms)
    last_position = accum[:, -1]
    scores = jnp.einsum(
        "thd,shd->hts", block_queries, segment_lookup_vectors, preferred_element_type=jnp.float32
    )
    qk_weights = (scores * weight).astype(jnp.bfloat16)
    inner = jnp.einsum("hts,shd->thd", qk_weights, block_values, preferred_element_type=jnp.float32)
    block_start = jnp.exp(accum).T[:, :, None]
    tail_decay = jnp.exp(last_position[:, None] - accum).T[:, :, None]
    block_state_matrix = jnp.einsum(
        "rpz,rpb->pzb",
        segment_lookup_vectors.astype(jnp.float32) * tail_decay,
        block_values.astype(jnp.float32),
        precision=PRECISE_MODE,
    )
    growth = jnp.exp(last_position)
    local_state = growth[:, None, None] * local_state + block_state_matrix
    local_decay = local_decay * growth
    pieces = [
        (
            block_queries,
            segment_lookup_vectors,
            block_values,
            grad_block,
            weight,
            qk_weights,
            inner,
            block_start,
            tail_decay,
            growth,
            block_state_matrix,
        )
    ]
    entering_decay = prefix((local_state, local_decay), "ctx", join_forward, (empty, unity), False)[
        0
    ]
    block_index = 0
    (
        block_queries,
        segment_lookup_vectors,
        block_values,
        grad_block,
        weight,
        qk_weights,
        inner,
        block_start,
        tail_decay,
        growth,
        block_state_matrix,
    ) = pieces[block_index]
    outer_product = block_start * jnp.einsum(
        "zmo,mol->zml", block_queries.astype(jnp.float32), entering_decay, precision=PRECISE_MODE
    )
    attention = inner + outer_product
    scaled = gain[None] * grad_block.astype(jnp.float32)
    square_parts = jnp.sum(attention * attention, axis=(1, 2))
    cross_parts = jnp.sum(scaled * attention, axis=(1, 2))
    attentions = [attention]
    prior_states = [entering_decay]
    squares, crossed = lax.psum((square_parts, cross_parts), "head")
    root = jnp.sqrt(squares / (HEADS * HEAD_DIM) + 1e-05)
    factor = crossed / (HEADS * HEAD_DIM * root**3)
    local_back = empty
    block_index = 0
    (
        block_queries,
        segment_lookup_vectors,
        block_values,
        grad_block,
        weight,
        qk_weights,
        inner,
        block_start,
        tail_decay,
        growth,
        block_state_matrix,
    ) = pieces[block_index]
    block_root = root[:, None, None]
    block_factor = factor[:, None, None]
    scaled = gain[None] * grad_block.astype(jnp.float32)
    norm_back = (scaled / block_root - attentions[block_index] * block_factor).astype(jnp.bfloat16)
    back_scores = jnp.einsum(
        "thd,shd->hts", norm_back, block_values, preferred_element_type=jnp.float32
    )
    back_weights = (back_scores * weight).astype(jnp.bfloat16)
    back_grad_wide = norm_back.astype(jnp.float32)
    query_gradient = jnp.einsum(
        "hts,shd->thd", back_weights, segment_lookup_vectors, preferred_element_type=jnp.float32
    )
    query_gradient = query_gradient + block_start * jnp.einsum(
        "bsp,snp->bsn", back_grad_wide, prior_states[block_index], precision=PRECISE_MODE
    )
    grad_qs = query_gradient.astype(jnp.bfloat16).reshape(BLOCK, width)
    backs = [norm_back]
    back_weight_list = [back_weights]
    back_terms = [
        jnp.einsum(
            "rua,rus->uas",
            block_queries.astype(jnp.float32) * block_start,
            back_grad_wide,
            precision=PRECISE_MODE,
        )
    ]
    block_index = 0
    local_back = back_terms[block_index] + pieces[block_index][9][:, None, None] * local_back
    leaving_decay = prefix((local_back, local_decay), "ctx", join_backward, (empty, unity), True)[0]
    grad_ks = [None] * count
    grad_vs = [None] * count
    block_index = 0
    (
        block_queries,
        segment_lookup_vectors,
        block_values,
        grad_block,
        weight,
        qk_weights,
        inner,
        block_start,
        tail_decay,
        growth,
        block_state_matrix,
    ) = pieces[block_index]
    key_gradient = jnp.einsum(
        "hts,thd->shd",
        back_weight_list[block_index],
        block_queries,
        preferred_element_type=jnp.float32,
    )
    key_gradient = key_gradient + tail_decay * jnp.einsum(
        "baz,aiz->bai", block_values.astype(jnp.float32), leaving_decay, precision=PRECISE_MODE
    )
    value_gradient = jnp.einsum(
        "hts,thd->shd", qk_weights, backs[block_index], preferred_element_type=jnp.float32
    )
    value_gradient = value_gradient + tail_decay * jnp.einsum(
        "tpa,pao->tpo",
        segment_lookup_vectors.astype(jnp.float32),
        leaving_decay,
        precision=PRECISE_MODE,
    )
    grad_ks[block_index] = key_gradient.astype(jnp.bfloat16).reshape(BLOCK, width)
    grad_vs[block_index] = value_gradient.astype(jnp.bfloat16).reshape(BLOCK, width)
    return (grad_qs, grad_ks[0], grad_vs[0])


def solution(mesh):
    in_specs = (
        P("ctx", "head"),
        P("ctx", "head"),
        P("ctx", "head"),
        P("ctx", "head"),
        P("head", "ctx"),
        P("head"),
    )
    out_specs = (P("ctx", "head"), P("ctx", "head"), P("ctx", "head"))
    return jax.shard_map(local, mesh=mesh, in_specs=in_specs, out_specs=out_specs, check_vma=False)
```

profile of v0, /device:TPU:1, one launch (start us, length us, event | category | flops | bytes accessed | tf_op | source)
XLA Modules:
  0.0 619.2 jit_solution(11615444361685317476)
XLA Ops:
  10.9 1.8 convolution_add_fusion.1
  15.0 130.1 %all-reduce = f32[1024]{0:T(1024)S(1)} all-reduce(f32[1024]{0:T(1024)S(1)} %dynamic-update-slice), channel_id=2, replica_groups=mesh['ctx'=64,'head'=4] {'ctx'}, use_global_device_ids=true, to_apply=%add | all-reduce | flops 1024 | bytes 8192
  148.5 1.3 fusion.10
  149.9 54.0 %all-gather.6.cloned.1.call-done = f32[1024,96,96]{2,1,0:T(8,128)} async-done(((f32[16,96,96]{2,1,0:T(8,128)}), f32[1024,96,96]{2,1,0:T(8,128)}) %all-gather.6.cloned.1.call-update) | async-done | bytes 37748752 | tf_op jit(solution)/shard_map/all_gather | solution.py:16
  203.9 84.5 %while.28 = (s32[]{:T(128)}, f32[16,96,96]{2,1,0:T(8,128)S(1)}, s32[]{:T(128)}, f32[64,16]{1,0:T(8,128)S(1)}, f32[64,16,96,96]{3,2,1,0:T(8,128)}, /*index=5*/s32[]{:T(128)}, s32[]{:T(128)}) while((s32[]{:T(128)}, f32[16,96,96]{2,1,0:T(8,128)S(1)}, s32[]{:T(128)}, f32[64,16]{1,0:T(8,128)S(1)}, f32[64,16,96,96]{3,2,1,0:T(8,128)}, ...), condition=%wide.region_2.3_spmd.clone, body=%wide.region_1.2_spmd.clone.sunk | while | flops 589828 | bytes 1769769 | solution.py:28
  205.3 1.3 fusion.47
  209.3 1.3 fusion.47
  214.7 1.3 fusion.47
  220.0 1.3 fusion.47
  225.4 1.3 fusion.47
  229.4 1.3 fusion.47
  234.8 1.3 fusion.47
  240.2 1.3 fusion.47
  245.5 1.3 fusion.47
  250.9 1.3 fusion.47
  254.9 1.3 fusion.47
  260.3 1.3 fusion.47
  265.7 1.3 fusion.47
  271.0 1.3 fusion.47
  276.4 1.3 fusion.47
  280.4 1.3 fusion.47
  285.8 1.3 fusion.47
  289.3 2.4 multiply_reduce_fusion.1
  291.7 8.4 %all-reduce.1 = (f32[128]{0:T(128)S(1)}, f32[128]{0:T(128)S(1)}) all-reduce(f32[128]{0:T(128)S(1)} %get-tuple-element.239, f32[128]{0:T(128)S(1)} %get-tuple-element.238), channel_id=1, replica_groups=mesh['ctx'=64,'head'=4] {'head'}, use_global_device_ids=true, to_apply=%region_6.7 | all-reduce | flops 256 | bytes 2048 | tf_op jit(solution)/shard_map/psum | solution.py:123
  300.1 1.4 subtract_convert_fusion
  301.5 1.8 convolution_add_fusion
  305.9 180.6 %all-gather.8.cloned.1.call-done = f32[1024,96,96]{2,1,0:T(8,128)} async-done(((f32[16,96,96]{2,1,0:T(8,128)}), f32[1024,96,96]{2,1,0:T(8,128)}) %all-gather.8.cloned.1.call-update) | async-done | bytes 37748752 | tf_op jit(solution)/shard_map/all_gather | solution.py:16
  486.5 35.5 %rev.6 = f32[64,16,96,96]{3,2,1,0:T(8,128)} reverse(f32[64,16,96,96]{3,2,1,0:T(8,128)} %bitcast.94), dimensions={0} | reverse | bytes 75497472 | tf_op jit(solution)/shard_map/rev | solution.py:18
  522.0 84.6 %while.29 = (s32[]{:T(128)}, f32[16,96,96]{2,1,0:T(8,128)S(1)}, s32[]{:T(128)}, f32[64,16,96,96]{3,2,1,0:T(8,128)}, f32[64,16]{1,0:T(8,128)S(1)}, /*index=5*/s32[]{:T(128)}, s32[]{:T(128)}) while((s32[]{:T(128)}, f32[16,96,96]{2,1,0:T(8,128)S(1)}, s32[]{:T(128)}, f32[64,16,96,96]{3,2,1,0:T(8,128)}, f32[64,16]{1,0:T(8,128)S(1)}, ...), condition=%wide.region_8.9_spmd.clone, body=%wide.region_7.8_spmd.clone.sunk | while | flops 589828 | bytes 1769769 | solution.py:28
  523.3 1.3 fusion.48
  526.0 1.3 fusion.48
  532.7 1.3 fusion.48
  539.4 1.3 fusion.48
  542.1 1.3 fusion.48
  548.8 1.3 fusion.48
  551.5 1.3 fusion.48
  558.2 1.3 fusion.48
  564.9 1.3 fusion.48
  567.6 1.3 fusion.48
  574.3 1.3 fusion.48
  577.0 1.3 fusion.48
  583.7 1.3 fusion.48
  590.4 1.3 fusion.48
  593.1 1.3 fusion.48
  599.8 1.3 fusion.48
  602.5 1.3 fusion.48
  607.8 1.3 fusion.13
  610.1 1.3 fusion.12
  (251 shorter events, 136.1 us)
Async XLA Ops:
  7.2 196.8 %all-gather.6.cloned.1.call-start = ((), (), s32[]{:S(2)}) async-start(), calls=%async_computation | async-start | bytes 51118080 | tf_op jit(solution)/shard_map/all_gather | solution.py:16
  12.8 473.7 %all-gather.8.cloned.1.call-start = ((), (), s32[]{:S(2)}) async-start(), calls=%async_computation.1 | async-start | bytes 51118080 | tf_op jit(solution)/shard_map/all_gather | solution.py:16
  303.9 1.0 copy-start
Sparse Core Ops, SparseCore 0:
  12.9 191.0 all-gather.5
  303.5 182.9 all-gather.7
where the time goes:
time: 625 us; the launch traced here: 619 us
  waiting for transfers between devices  235 us (38%)
  other arithmetic  167 us (27%)
  blocking collectives  139 us (22%)
  local copies, waits for them, and re-layouts  47 us (8%)
  between operations  14.9 us (2%)
  matrix products  13.7 us (2%)
    all_gather x2, waiting for transfers between devices, prefix(): pieces = jax.tree.map(lambda part: lax.all_gather(part, axis), value)  235 us
    select_n x126, other arithmetic, step(): jnp.where(position < mine, new, old)  164 us
    unnamed x1, blocking collectives  130 us
    rev x2, local copies, waits for them, and re-layouts, prefix(): pieces = jax.tree.map(lambda part: part[::-1], pieces)  35.5 us
  transfers between devices with their start and end apart: 2, of which 2 were waited for; matrix products, arithmetic and copies ran while one was open for 1% of the time, Pallas kernels for 0%

commit v1 on v0

v1 whole, which is shorter than its diff:
```python
import jax
import jax.numpy as jnp
from jax import lax
from jax.experimental import pallas as pl
from jax.experimental.pallas import tpu as pltpu
from jax.sharding import Mesh, PartitionSpec as P

HEADS = 64
HEAD_DIM = 96
TOKENS = 128
LOCAL_HEADS = 16
HALF = 8
WIDTH = LOCAL_HEADS * HEAD_DIM
LANES = 128
PACK = 72
CHIPS = 32
PART = 18
FWD_PART = 20
ROWS = LOCAL_HEADS * PACK
HALF_ROWS = HALF * PACK
VMEM = 48 * 1024 * 1024

F32 = jnp.float32
BF16 = jnp.bfloat16

START = (0, 0, 128, 256)
SPAN = (128, 256, 256, 128)
FIRST = (0, 96, 64, 32)
FREE = (3, 2, 1, 0)


def lanes_of(shape):
    return lax.broadcasted_iota(jnp.int32, shape, len(shape) - 1)


def rows_of(shape):
    return lax.broadcasted_iota(jnp.int32, shape, len(shape) - 2)


def dot_nn(a, b):
    return lax.dot_general(a, b, (((1,), (0,)), ((), ())), preferred_element_type=F32)


def dot_nt(a, b):
    return lax.dot_general(a, b, (((1,), (1,)), ((), ())), preferred_element_type=F32)


def two(x):
    high = x.astype(BF16)
    return high, (x - high.astype(F32)).astype(BF16)


def head_tiles(value, g, j, masked):
    part = value[:, 384 * g + START[j] : 384 * g + START[j] + SPAN[j]]
    if masked:
        lane = lanes_of(part.shape)
        part = jnp.where((lane >= FIRST[j]) & (lane < FIRST[j] + HEAD_DIM), part, jnp.zeros_like(part))
    return part


def merge(tiles):
    return tiles if tiles.shape[1] == LANES else tiles[:, :LANES] + tiles[:, LANES:]


def pack(square, j):
    lane = lanes_of((24, LANES))
    free = lane // 32 == FREE[j]
    extra = square[PACK:]
    others = [c for c in range(4) if c != FREE[j]]
    return [
        jnp.where(free, pltpu.roll(extra, (32 * (FREE[j] - c)) % LANES, 1), square[24 * i : 24 * i + 24])
        for i, c in enumerate(others)
    ]


def unpack(packed, j):
    lane = lanes_of((24, LANES))
    others = [c for c in range(4) if c != FREE[j]]
    extra = jnp.zeros((24, LANES), F32)
    for i, c in enumerate(others):
        moved = pltpu.roll(packed[24 * i : 24 * i + 24], (32 * (c - FREE[j])) % LANES, 1)
        extra = jnp.where(lane // 32 == c, moved, extra)
    return jnp.concatenate([packed, extra], axis=0)


def spread(square, j):
    lane = lanes_of(square.shape)
    zero = jnp.zeros_like(square)
    if j == 0:
        tiles = (jnp.where(lane < 96, square, zero), zero, zero)
    elif j == 1:
        tiles = (jnp.where(lane >= 96, square, zero), jnp.where(lane < 64, square, zero), zero)
    elif j == 2:
        tiles = (zero, jnp.where(lane >= 64, square, zero), jnp.where(lane < 32, square, zero))
    else:
        tiles = (zero, zero, jnp.where(lane >= 32, square, zero))
    return jnp.concatenate(tiles, axis=1)


def block_diagonal(ref, g):
    rows = []
    for j in range(4):
        h = 4 * g + j
        rows.append(spread(unpack(ref[PACK * h : PACK * h + PACK, :], j), j))
    return two(jnp.concatenate(rows, axis=0))


def running(logs):
    lane = lanes_of(logs.shape)
    total = logs
    for k in (1, 2, 4, 8, 16, 32, 64):
        total = total + jnp.where(lane >= k, pltpu.roll(total, k, 1), 0.0)
    return total


def columns(rows):
    filler = jnp.zeros((LANES - rows.shape[0], LANES), F32)
    return jnp.concatenate([rows, filler], axis=0).T


def wide_column(cols, h):
    return jnp.broadcast_to(cols[:, h : h + 1], (TOKENS, LANES))


def group_columns(cols, g):
    lane = lanes_of((TOKENS, LANES))
    c = [wide_column(cols, 4 * g + j) for j in range(4)]
    return jnp.concatenate(
        [jnp.where(lane < 96, c[0], c[1]), jnp.where(lane < 64, c[1], c[2]), jnp.where(lane < 32, c[2], c[3])],
        axis=1,
    )


def weight_of(accum, cols, h):
    row = accum[h : h + 1, :]
    spread_by = wide_column(cols, h) - row
    shape = (TOKENS, LANES)
    keep = lanes_of(shape) <= rows_of(shape)
    return jnp.where(keep, jnp.exp(jnp.where(keep, spread_by, 0.0)), 0.0)


def weight_turned(accum, cols, h):
    spread_by = accum[h : h + 1, :] - wide_column(cols, h)
    shape = (TOKENS, LANES)
    keep = rows_of(shape) <= lanes_of(shape)
    return jnp.where(keep, jnp.exp(jnp.where(keep, spread_by, 0.0)), 0.0)


def outer_states(left_ref, scale, right, out_ref):
    for g in range(4):
        turned = left_ref[:, 384 * g : 384 * g + 384].astype(F32).T
        for j in range(4):
            h = 4 * g + j
            high, low = two(turned[96 * j : 96 * j + 96, :] * scale[h : h + 1, :])
            both = dot_nn(jnp.concatenate([high, low], axis=0), head_tiles(right, g, j, True))
            square = merge(both[:96] + both[96:])
            for i, piece in enumerate(pack(square, j)):
                out_ref[PACK * h + 24 * i : PACK * h + 24 * i + 24, :] = piece


def state_kernel(k_ref, v_ref, logs_ref, x_ref):
    accum = running(logs_ref[...])
    last = accum[:, LANES - 1 :]
    outer_states(k_ref, jnp.exp(last - accum), v_ref, x_ref)
    x_ref[ROWS : ROWS + LOCAL_HEADS, :] = jnp.broadcast_to(jnp.exp(last), (LOCAL_HEADS, LANES))


def combine_forward_kernel(core_ref, own_ref, got_ref, out_ref, own_decay_ref, got_decay_ref):
    core = core_ref[0]
    own_decay_ref[...] = own_ref[ROWS : ROWS + LOCAL_HEADS, :]
    got_decay_ref[...] = got_ref[ROWS : ROWS + LOCAL_HEADS, :]
    first = core == 0
    at = pl.multiple_of(ROWS + HALF * core, 8)
    own_decay = own_ref[pl.ds(at, HALF), :]
    got_decay = got_ref[pl.ds(at, HALF), :]
    late_decay = jnp.where(first, got_decay, own_decay)
    both_decay = own_decay * got_decay
    for h in range(HALF):
        at = pl.multiple_of(HALF_ROWS * core + PACK * h, 8)
        own = own_ref[pl.ds(at, PACK), :]
        got = got_ref[pl.ds(at, PACK), :]
        early = jnp.where(first, own, got)
        late = jnp.where(first, got, own)
        total = early * late_decay[h : h + 1, :] + late
        for quarter in range(4):
            to = FWD_PART * (4 * h + quarter)
            out_ref[to : to + PART, :] = total[PART * quarter : PART * quarter + PART, :]
            out_ref[to + PART : to + FWD_PART, :] = jnp.broadcast_to(both_decay[h : h + 1, :], (2, LANES))


def combine_backward_kernel(core_ref, own_ref, got_ref, own_decay_ref, got_decay_ref, out_ref):
    core = core_ref[0]
    first = core == 0
    at = pl.multiple_of(HALF * core, 8)
    early_decay = jnp.where(first, own_decay_ref[pl.ds(at, HALF), :], got_decay_ref[pl.ds(at, HALF), :])
    for h in range(HALF):
        at = pl.multiple_of(HALF_ROWS * core + PACK * h, 8)
        own = own_ref[pl.ds(at, PACK), :]
        got = got_ref[pl.ds(at, PACK), :]
        early = jnp.where(first, own, got)
        late = jnp.where(first, got, own)
        out_ref[PACK * h : PACK * h + PACK, :] = late * early_decay[h : h + 1, :] + early


def scan_forward_kernel(in_ref, out_ref, decay_ref):
    state = jnp.zeros((PART, LANES), F32)
    for c in range(CHIPS):
        out_ref[PART * c : PART * c + PART, :] = state
        at = FWD_PART * c
        decay = in_ref[at + PART : at + PART + 1, :]
        decay_ref[c : c + 1, :] = decay
        state = state * decay + in_ref[at : at + PART, :]


def scan_backward_kernel(in_ref, decay_ref, out_ref):
    state = jnp.zeros((PART, LANES), F32)
    for c in reversed(range(CHIPS)):
        out_ref[PART * c : PART * c + PART, :] = state
        state = state * decay_ref[c : c + 1, :] + in_ref[PART * c : PART * c + PART, :]


def finish_states(mine, other, add_ref, decay, own_ref, got_ref, out_ref):
    for h in range(LOCAL_HEADS):
        at = PACK * (h % HALF)
        own = own_ref[at : at + PACK, :]
        got = got_ref[at : at + PACK, :]
        state = jnp.where(mine, own, got) if h < HALF else jnp.where(mine, got, own)
        stepped = state * decay[h : h + 1, :] + add_ref[PACK * h : PACK * h + PACK, :]
        out_ref[PACK * h : PACK * h + PACK, :] = jnp.where(other, stepped, state)


def inner_kernel(q_ref, k_ref, v_ref, logs_ref, inner_ref):
    accum = running(logs_ref[...])
    cols = columns(accum)
    for g in range(4):
        tiles = [None] * 3
        for j in range(4):
            h = 4 * g + j
            scores = dot_nt(head_tiles(q_ref, g, j, True), head_tiles(k_ref, g, j, False))
            weights = (scores * weight_of(accum, cols, h)).astype(BF16)
            part = dot_nn(weights, head_tiles(v_ref, g, j, True))
            for i in range(SPAN[j] // LANES):
                t = START[j] // LANES + i
                piece = part[:, LANES * i : LANES * i + LANES]
                tiles[t] = piece if tiles[t] is None else tiles[t] + piece
        for t in range(3):
            inner_ref[:, 384 * g + LANES * t : 384 * g + LANES * t + LANES] = tiles[t]


def attention_kernel(
    core_ref, q_ref, y_ref, gain_ref, logs_ref, inner_ref, own_ref, got_ref, got_state_ref, o_ref, state_ref, sums_ref
):
    core = core_ref[0]
    decay = got_state_ref[ROWS : ROWS + LOCAL_HEADS, :]
    finish_states(core == 0, core == 1, got_state_ref, decay, own_ref, got_ref, state_ref)
    start = jnp.exp(columns(running(logs_ref[...])))
    squares = jnp.zeros((TOKENS, LANES), F32)
    crossed = jnp.zeros((TOKENS, LANES), F32)
    for g in range(4):
        high, low = block_diagonal(state_ref, g)
        at = slice(384 * g, 384 * g + 384)
        q = q_ref[:, at]
        attention = inner_ref[:, at] + group_columns(start, g) * (dot_nn(q, high) + dot_nn(q, low))
        o_ref[:, at] = attention
        scaled = gain_ref[:, at] * y_ref[:, at].astype(F32)
        both = scaled * attention
        square = attention * attention
        for t in range(3):
            squares = squares + square[:, LANES * t : LANES * t + LANES]
            crossed = crossed + both[:, LANES * t : LANES * t + LANES]
    sums_ref[0:1, :] = jnp.sum(squares.T, axis=0, keepdims=True)
    sums_ref[1:2, :] = jnp.sum(crossed.T, axis=0, keepdims=True)


def norm_kernel(q_ref, y_ref, gain_ref, logs_ref, o_ref, sums_ref, back_ref, c_ref):
    accum = running(logs_ref[...])
    root = jnp.sqrt(sums_ref[0:1, :] / (HEADS * HEAD_DIM) + 1e-05)
    factor = sums_ref[1:2, :] / (HEADS * HEAD_DIM * root * root * root)
    cols = columns(jnp.concatenate([1.0 / root, factor], axis=0))
    inverse = jnp.broadcast_to(cols[:, 0:1], (TOKENS, 384))
    factor = jnp.broadcast_to(cols[:, 1:2], (TOKENS, 384))
    for g in range(4):
        at = slice(384 * g, 384 * g + 384)
        scaled = gain_ref[:, at] * y_ref[:, at].astype(F32)
        back_ref[:, at] = (scaled * inverse - o_ref[:, at] * factor).astype(BF16)
    outer_states(q_ref, jnp.exp(accum), back_ref, c_ref)


def middle_kernel(q_ref, k_ref, v_ref, back_ref, logs_ref, state_ref, gq_ref, gk_ref, gv_ref):
    accum = running(logs_ref[...])
    cols = columns(accum)
    start = jnp.exp(cols)
    for g in range(4):
        high, low = block_diagonal(state_ref, g)
        at = slice(384 * g, 384 * g + 384)
        back = back_ref[:, at]
        gq = group_columns(start, g) * (dot_nt(back, high) + dot_nt(back, low))
        gq = [gq[:, LANES * t : LANES * t + LANES] for t in range(3)]
        gk = [None] * 3
        gv = [None] * 3
        for j in range(4):
            h = 4 * g + j
            q = head_tiles(q_ref, g, j, True)
            k = head_tiles(k_ref, g, j, True)
            v = head_tiles(v_ref, g, j, False)
            d = head_tiles(back_ref, g, j, True)
            weight = weight_of(accum, cols, h)
            turned = weight_turned(accum, cols, h)
            weights = (dot_nt(d, v) * weight).astype(BF16)
            weights_t = (dot_nt(v, d) * turned).astype(BF16)
            qk_t = (dot_nt(k, q) * turned).astype(BF16)
            to_q = dot_nn(weights, k)
            to_k = dot_nn(weights_t, q)
            to_v = dot_nn(qk_t, d)
            for i in range(SPAN[j] // LANES):
                t = START[j] // LANES + i
                lane = slice(LANES * i, LANES * i + LANES)
                gq[t] = gq[t] + to_q[:, lane]
                gk[t] = to_k[:, lane] if gk[t] is None else gk[t] + to_k[:, lane]
                gv[t] = to_v[:, lane] if gv[t] is None else gv[t] + to_v[:, lane]
        for t in range(3):
            lane = slice(384 * g + LANES * t, 384 * g + LANES * t + LANES)
            gq_ref[:, lane] = gq[t].astype(BF16)
            gk_ref[:, lane] = gk[t]
            gv_ref[:, lane] = gv[t]


def last_kernel(
    core_ref, k_ref, v_ref, logs_ref, gk0_ref, gv0_ref, own_ref, got_ref, got_c_ref, got_decay_ref, gk_ref, gv_ref, carry_ref
):
    core = core_ref[0]
    finish_states(core == 0, core == 0, got_c_ref, got_decay_ref[...], own_ref, got_ref, carry_ref)
    accum = running(logs_ref[...])
    tail = columns(jnp.exp(accum[:, LANES - 1 :] - accum))
    for g in range(4):
        high, low = block_diagonal(carry_ref, g)
        at = slice(384 * g, 384 * g + 384)
        k = k_ref[:, at]
        v = v_ref[:, at]
        wide = group_columns(tail, g)
        gk_ref[:, at] = (gk0_ref[:, at] + wide * (dot_nt(v, high) + dot_nt(v, low))).astype(BF16)
        gv_ref[:, at] = (gv0_ref[:, at] + wide * (dot_nn(k, high) + dot_nn(k, low))).astype(BF16)


def call(kernel, outs, smem, *args, scratch=(), flops=0):
    specs = []
    for i, arg in enumerate(args):
        if i < smem:
            specs.append(pl.BlockSpec(memory_space=pltpu.SMEM))
        else:
            specs.append(pl.BlockSpec(memory_space=pltpu.VMEM))
    shapes = [jax.ShapeDtypeStruct(s, d) for s, d in outs]
    moved = sum(a.size * a.dtype.itemsize for a in args) + sum(s.size * s.dtype.itemsize for s in shapes)
    out = pl.pallas_call(
        kernel,
        out_shape=shapes,
        in_specs=specs,
        out_specs=[pl.BlockSpec(memory_space=pltpu.VMEM)] * len(shapes),
        scratch_shapes=scratch,
        compiler_params=pltpu.CompilerParams(vmem_limit_bytes=VMEM),
        cost_estimate=pl.CostEstimate(flops=flops, bytes_accessed=moved, transcendentals=0),
        name=kernel.__name__,
    )(*args)
    return out[0] if len(out) == 1 else out


SWAP = [(0, 1), (1, 0)]
CHIP_AXES = ("x", "z")


def swap(value):
    return lax.ppermute(value, "core", SWAP)


def exchange(value):
    flat = lax.all_to_all(value.reshape(-1), CHIP_AXES, 0, 0, tiled=True)
    return flat.reshape(value.shape)


def local(q, k, v, y, logs, gain):
    core = lax.axis_index("core").astype(jnp.int32).reshape(1)
    gain = gain.reshape(1, WIDTH)
    wide = (TOKENS, WIDTH)
    x = call(state_kernel, [((ROWS + LOCAL_HEADS, LANES), F32)], 0, k, v, logs, flops=2 * 10**8)
    got_x = swap(x)
    decay = ((LOCAL_HEADS, LANES), F32)
    payload, own_decay, got_decay = call(
        combine_forward_kernel, [((CHIPS * FWD_PART, LANES), F32), decay, decay], 1, core, x, got_x
    )
    payload = exchange(payload)
    inner = call(inner_kernel, [(wide, F32)], 0, q, k, v, logs, flops=4 * 10**8)
    entering, decays = call(scan_forward_kernel, [((HALF_ROWS, LANES), F32), ((CHIPS, LANES), F32)], 0, payload)
    entering = exchange(entering)
    got_entering = swap(entering)
    attention, state, sums = call(
        attention_kernel,
        [(wide, F32), ((ROWS, LANES), F32), ((2, LANES), F32)],
        1, core, q, y, gain, logs, inner, entering, got_entering, got_x,
        flops=4 * 10**8,
    )
    sums = lax.psum(sums, "head")
    back, c = call(norm_kernel, [(wide, BF16), ((ROWS, LANES), F32)], 0, q, y, gain, logs, attention, sums, flops=2 * 10**8)
    got_c = swap(c)
    payload = call(
        combine_backward_kernel, [((HALF_ROWS, LANES), F32)], 1, core, c, got_c, own_decay, got_decay
    )
    payload = exchange(payload)
    gq, gk0, gv0 = call(
        middle_kernel, [(wide, BF16), (wide, F32), (wide, F32)], 0, q, k, v, back, logs, state, flops=10**9
    )
    leaving = call(scan_backward_kernel, [((HALF_ROWS, LANES), F32)], 0, payload, decays)
    leaving = exchange(leaving)
    got_leaving = swap(leaving)
    gk, gv = call(
        last_kernel,
        [(wide, BF16), (wide, BF16)],
        1, core, k, v, logs, gk0, gv0, leaving, got_leaving, got_c, got_decay,
        scratch=[pltpu.VMEM((ROWS, LANES), F32)],
        flops=4 * 10**8,
    )
    return gq, gk, gv


def solution(mesh):
    grid = Mesh(mesh.devices.reshape(4, 8, 2, 4), ("x", "z", "core", "head"))
    tokens = ("x", "z", "core")
    rows = P(tokens, "head")
    return jax.shard_map(
        local,
        mesh=grid,
        in_specs=(rows, rows, rows, rows, P("head", tokens), P("head")),
        out_specs=(rows, rows, rows),
        check_vma=False,
    )
```

time: 625 us -> 112 us (0.18)
  waiting for transfers between devices: 235 us -> 3.28 us
  other arithmetic: 167 us -> 0 us
  blocking collectives: 139 us -> 76.9 us
  local copies, waits for them, and re-layouts: 47 us -> 3.55 us
  between operations: 14.9 us -> 0.77 us
  starting transfers between devices: 0.08 us -> 14.1 us
  matrix products: 13.7 us -> 0 us
  Pallas kernels: 0 us -> 12.8 us
    all_gather x2 -> x0, waiting for transfers between devices: 235 us -> none  [prefix(): pieces = jax.tree.map(lambda part: lax.all_gather(part, axis), value)]
    select_n x126 -> x0, other arithmetic: 164 us -> none  [step(): jnp.where(position < mine, new, old)]
    unnamed x1 -> x0, blocking collectives: 130 us -> none
    all_to_all x0 -> x4, blocking collectives: none -> 68.2 us  [exchange(): flat = lax.all_to_all(value.reshape(-1), CHIP_AXES, 0, 0, tiled=True)]
    rev x2 -> x0, local copies, waits for them, and re-layouts: 35.5 us -> none  [prefix(): pieces = jax.tree.map(lambda part: part[::-1], pieces)]
    ppermute x0 -> x4, starting transfers between devices: none -> 14.1 us  [swap(): return lax.ppermute(value, 'core', SWAP)]
    dot_general x12 -> x0, matrix products: 13.7 us -> none  [the longest x1 2.4 us: local(): jnp.einsum('hts,shd->thd', qk_weights, block_values, preferred_element_ty...]
    pallas_call x0 -> x10, Pallas kernels: none -> 12.8 us  [call(): pl.pallas_call(kernel, out_shape=shapes, in_specs=specs, out_specs=[pl.Bl...]
  transfers between devices with their start and end apart: 2 -> 4, of which waited for: 2 -> 2; matrix products, arithmetic and copies ran while one was open for 1% -> 0% of each run, Pallas kernels for 0% -> 6%
where the time goes in v1:
time: 112 us; the launch traced here: 111 us
  blocking collectives  76.9 us (69%)
  starting transfers between devices  14.1 us (13%)
  Pallas kernels  12.8 us (11%)
  local copies, waits for them, and re-layouts  3.55 us (3%)
  waiting for transfers between devices  3.28 us (3%)
    all_to_all x4, blocking collectives, exchange(): flat = lax.all_to_all(value.reshape(-1), CHIP_AXES, 0, 0, tiled=True)  68.2 us
    ppermute x4, starting transfers between devices, swap(): return lax.ppermute(value, 'core', SWAP)  14.1 us
    pallas_call x10, Pallas kernels, call(): pl.pallas_call(kernel, out_shape=shapes, in_specs=specs, out_specs=[pl.Bl...  12.8 us
    psum x1, blocking collectives, local(): sums = lax.psum(sums, 'head')  8.69 us
    unnamed x22, local copies, waits for them, and re-layouts  3.54 us
    ppermute x4, waiting for transfers between devices, swap(): return lax.ppermute(value, 'core', SWAP)  3.28 us
  transfers between devices with their start and end apart: 4, of which 2 were waited for; matrix products, arithmetic and copies ran while one was open for 0% of the time, Pallas kernels for 6%

profile of v1, /device:TPU:1, one launch (start us, length us, event | category | flops | bytes accessed | tf_op | source)
XLA Modules:
  0.0 111.3 jit_solution(5586399552033787044)
XLA Ops:
  0.6 0.0 copy-start.1
  0.6 1.0 copy-done.1
  1.6 0.0 copy-start.3
  1.6 1.0 copy-done.3
  2.6 0.0 copy-start.6
  2.6 0.7 copy-done.6
  3.3 1.2 %state_kernel.1.own_ref = f32[1168,128]{1,0:T(8,128)S(1)} custom-call(bf16[128,1536]{1,0:T(8,128)(2,1)S(1)} %copy-done.1, bf16[128,1536]{1,0:T(8,128)(2,1)S(1)} %copy-done.3, f32[16,128]{1,0:T(8,128)S(1)} %copy-done.6), custom_call_target="tpu_custom_call" | custom-call | flops 200000000 | bytes 1392640 | tf_op jit(solution)/shard_map/state_kernel/pallas_call | solution.py:354
  4.5 3.3 %collective-permute-start = (f32[1168,128]{1,0:T(8,128)S(1)}, f32[1168,128]{1,0:T(8,128)S(1)}, u32[]{:S(2)}, u32[]{:S(2)}) collective-permute-start(f32[1168,128]{1,0:T(8,128)S(1)} %state_kernel.1.own_ref), channel_id=1, source_target_pairs={{0,4},{4,0},{1,5},{5,1},{2,6},{6,2},{3,7},{7,3},{8,12},{12,8},{9,1... | collective-permute-start | bytes 1794056 | tf_op jit(solution)/shard_map/ppermute | solution.py:372
  7.9 1.6 %collective-permute-done.got_ref.got_state_ref = f32[1168,128]{1,0:T(8,128)S(1)} collective-permute-done((f32[1168,128]{1,0:T(8,128)S(1)}, f32[1168,128]{1,0:T(8,128)S(1)}, u32[]{:S(2)}, u32[]{:S(2)}) %collective-permute-start) | collective-permute-done | bytes 598048 | tf_op jit(solution)/shard_map/ppermute | solution.py:372
  9.5 0.1 combine_forward_kernel.1
  9.5 0.0 copy-start.4
  9.6 19.7 %all_to_all.36 = f32[32,2560,1]{1,2,0:T(1,128)S(1)} all-to-all(f32[32,2560,1]{1,2,0:T(1,128)S(1)} %bitcast.17), channel_id=1, replica_groups=mesh['x'=4,'z'=8,'core'=2,'head'=4] {'x','z'}, dimensions={0} | all-to-all | bytes 655360 | tf_op jit(solution)/shard_map/all_to_all | solution.py:376
  29.3 0.0 copy-start
  29.3 0.0 copy-start.2
  29.3 0.1 scan_forward_kernel.1
  29.3 0.0 copy-start.10
  29.4 17.3 %all_to_all.37 = f32[32,2304,1]{1,2,0:T(1,128)S(1)} all-to-all(f32[32,2304,1]{1,2,0:T(1,128)S(1)} %bitcast.18), channel_id=1, replica_groups=mesh['x'=4,'z'=8,'core'=2,'head'=4] {'x','z'}, dimensions={0} | all-to-all | bytes 589824 | tf_op jit(solution)/shard_map/all_to_all | solution.py:376
  46.6 0.0 copy-start.7
  46.7 4.0 %collective-permute-start.1 = (f32[576,128]{1,0:T(8,128)S(1)}, f32[576,128]{1,0:T(8,128)S(1)}, u32[]{:S(2)}, u32[]{:S(2)}) collective-permute-start(f32[576,128]{1,0:T(8,128)S(1)} %bitcast.14), channel_id=1, source_target_pairs={{0,4},{4,0},{1,5},{5,1},{2,6},{6,2},{3,7},{7,3},{8,12},{12,8},{9,1... | collective-permute-start | bytes 884744 | tf_op jit(solution)/shard_map/ppermute | solution.py:372
  50.6 0.0 copy-done.10
  50.6 0.0 copy-done.4
  50.7 0.0 copy-done
  50.7 0.0 copy-done.2
  50.7 0.0 copy-done.7
  50.7 0.0 copy-start.5
  50.7 2.0 %inner_kernel.1.inner_ref = f32[128,1536]{1,0:T(8,128)S(1)} custom-call(bf16[128,1536]{1,0:T(8,128)(2,1)S(1)} %copy-done, bf16[128,1536]{1,0:T(8,128)(2,1)S(1)} %copy-done.2, bf16[128,1536]{1,0:T(8,128)(2,1)S(1)} %copy-done.4, f32[16,128]{1,0:T(8,128)S(1)} %copy-done.7), custom_call_target="tpu_custom_call" | custom-call | flops 400000000 | bytes 1974272 | tf_op jit(solution)/shard_map/inner_kernel/pallas_call | solution.py:354
  52.7 0.0 collective-permute-done.1.got_ref
  52.7 0.0 copy-done.5
  52.7 1.2 %attention_kernel.1 = (f32[128,1536]{1,0:T(8,128)S(1)}, f32[1152,128]{1,0:T(8,128)S(1)}, f32[2,128]{1,0:T(2,128)S(1)}) custom-call(s32[1]{0:T(128)} %bitcast.core_ref, bf16[128,1536]{1,0:T(8,128)(2,1)S(1)} %copy-done, bf16[128,1536]{1,0:T(8,128)(2,1)S(1)} %copy-done.5, f32[1,1536]{1,0:T(1,128)S(1)} %reshape.44.gain_ref, f32[16,128]{1,0:T(8,128)S(1)} %copy-done.7, ...), custom_call_target="tpu_custom_call" | custom-call | flops 400000000 | bytes 4152324 | tf_op jit(solution)/shard_map/attention_kernel/pallas_call | solution.py:354
  53.9 0.0 copy-start.8
  53.9 0.8 copy-done.8
  54.7 8.7 %psum.7.sums_ref = f32[2,128]{1,0:T(2,128)S(1)} all-reduce(f32[2,128]{1,0:T(2,128)S(1)} %get-tuple-element.21), channel_id=1, replica_groups=mesh['x'=4,'z'=8,'core'=2,'head'=4] {'head'}, use_global_device_ids=true, to_apply=%region_0.0 | all-reduce | flops 256 | bytes 2048 | tf_op jit(solution)/shard_map/psum | solution.py:401
  63.4 1.3 %norm_kernel.1 = (bf16[128,1536]{1,0:T(8,128)(2,1)S(1)}, f32[1152,128]{1,0:T(8,128)S(1)}) custom-call(bf16[128,1536]{1,0:T(8,128)(2,1)S(1)} %copy-done, bf16[128,1536]{1,0:T(8,128)(2,1)S(1)} %copy-done.5, f32[1,1536]{1,0:T(1,128)S(1)} %reshape.44.gain_ref, f32[16,128]{1,0:T(8,128)S(1)} %copy-done.7, f32[128,1536]{1,0:T(8,128)S(1)} %get-tuple-element.20.o_ref, ...), custom_call_target="tpu_custom_call" | custom-call | flops 200000000 | bytes 2571264 | tf_op jit(solution)/shard_map/norm_kernel/pallas_call | solution.py:354
  64.7 2.7 %collective-permute-start.2 = (f32[1152,128]{1,0:T(8,128)S(1)}, f32[1152,128]{1,0:T(8,128)S(1)}, u32[]{:S(2)}, u32[]{:S(2)}) collective-permute-start(f32[1152,128]{1,0:T(8,128)S(1)} %get-tuple-element.27.own_ref), channel_id=1, source_target_pairs={{0,4},{4,0},{1,5},{5,1},{2,6},{6,2},{3,7},{7,3},{8,12},{12,8},{9,1... | collective-permute-start | bytes 1769480 | tf_op jit(solution)/shard_map/ppermute | solution.py:372
  67.4 1.6 %collective-permute-done.2.got_ref.got_c_ref = f32[1152,128]{1,0:T(8,128)S(1)} collective-permute-done((f32[1152,128]{1,0:T(8,128)S(1)}, f32[1152,128]{1,0:T(8,128)S(1)}, u32[]{:S(2)}, u32[]{:S(2)}) %collective-permute-start.2) | collective-permute-done | bytes 589856 | tf_op jit(solution)/shard_map/ppermute | solution.py:372
  69.1 0.1 combine_backward_kernel.1
  69.1 14.4 %all_to_all.38 = f32[32,2304,1]{1,2,0:T(1,128)S(1)} all-to-all(f32[32,2304,1]{1,2,0:T(1,128)S(1)} %bitcast.16), channel_id=1, replica_groups=mesh['x'=4,'z'=8,'core'=2,'head'=4] {'x','z'}, dimensions={0} | all-to-all | bytes 589824 | tf_op jit(solution)/shard_map/all_to_all | solution.py:376
  83.5 0.0 copy-start.9
  83.5 0.1 scan_backward_kernel.1
  83.6 16.8 %all_to_all.39 = f32[32,2304,1]{1,2,0:T(1,128)S(1)} all-to-all(f32[32,2304,1]{1,2,0:T(1,128)S(1)} %bitcast.11), channel_id=1, replica_groups=mesh['x'=4,'z'=8,'core'=2,'head'=4] {'x','z'}, dimensions={0} | all-to-all | bytes 589824 | tf_op jit(solution)/shard_map/all_to_all | solution.py:376
  100.4 4.0 %collective-permute-start.3 = (f32[576,128]{1,0:T(8,128)S(1)}, f32[576,128]{1,0:T(8,128)S(1)}, u32[]{:S(2)}, u32[]{:S(2)}) collective-permute-start(f32[576,128]{1,0:T(8,128)S(1)} %bitcast.12), channel_id=1, source_target_pairs={{0,4},{4,0},{1,5},{5,1},{2,6},{6,2},{3,7},{7,3},{8,12},{12,8},{9,1... | collective-permute-start | bytes 884744 | tf_op jit(solution)/shard_map/ppermute | solution.py:372
  104.4 0.0 copy-done.9
  104.4 4.6 %middle_kernel.1 = (bf16[128,1536]{1,0:T(8,128)(2,1)}, f32[128,1536]{1,0:T(8,128)S(1)}, f32[128,1536]{1,0:T(8,128)S(1)}) custom-call(bf16[128,1536]{1,0:T(8,128)(2,1)S(1)} %copy-done, bf16[128,1536]{1,0:T(8,128)(2,1)S(1)} %copy-done.2, bf16[128,1536]{1,0:T(8,128)(2,1)S(1)} %copy-done.4, bf16[128,1536]{1,0:T(8,128)(2,1)S(1)} %get-tuple-element.22.back_ref, ...), custom_call_target="tpu_custom_call" | custom-call | flops 1000000000 | bytes 4136960 | tf_op jit(solution)/shard_map/middle_kernel/pallas_call | solution.py:354
  109.0 0.0 collective-permute-done.3.got_ref
  109.0 2.4 %last_kernel.1 = (bf16[128,1536]{1,0:T(8,128)(2,1)}, bf16[128,1536]{1,0:T(8,128)(2,1)}) custom-call(s32[1]{0:T(128)} %bitcast.core_ref, bf16[128,1536]{1,0:T(8,128)(2,1)S(1)} %copy-done.2, bf16[128,1536]{1,0:T(8,128)(2,1)S(1)} %copy-done.4, f32[16,128]{1,0:T(8,128)S(1)} %copy-done.7, f32[128,1536]{1,0:T(8,128)S(1)} %get-tuple-element.25.gk0_ref, ...), custom_call_target="tpu_custom_call" | custom-call | flops 400000000 | bytes 4341764 | tf_op jit(solution)/shard_map/last_kernel/pallas_call | solution.py:354
  (1 shorter events, 0.0 us)
Async XLA Ops:
  0.6 1.0 copy-start.1
  1.6 1.0 copy-start.3
  2.6 0.7 copy-start.6
  4.5 5.0 %collective-permute-start = (f32[1168,128]{1,0:T(8,128)S(1)}, f32[1168,128]{1,0:T(8,128)S(1)}, u32[]{:S(2)}, u32[]{:S(2)}) collective-permute-start(f32[1168,128]{1,0:T(8,128)S(1)} %state_kernel.1.own_ref), channel_id=1, source_target_pairs={{0,4},{4,0},{1,5},{5,1},{2,6},{6,2},{3,7},{7,3},{8,12},{12,8},{9,1... | collective-permute-start | bytes 1794056 | tf_op jit(solution)/shard_map/ppermute | solution.py:372
  9.5 41.1 %copy-start.4 = (bf16[128,1536]{1,0:T(8,128)(2,1)S(1)}, bf16[128,1536]{1,0:T(8,128)(2,1)}, u32[]{:S(2)}) copy-start(bf16[128,1536]{1,0:T(8,128)(2,1)} %v_ref.7) | copy-start | bytes 1179652
  29.3 21.4 %copy-start = (bf16[128,1536]{1,0:T(8,128)(2,1)S(1)}, bf16[128,1536]{1,0:T(8,128)(2,1)}, u32[]{:S(2)}) copy-start(bf16[128,1536]{1,0:T(8,128)(2,1)} %q_ref.7) | copy-start | bytes 1179652
  29.3 21.4 %copy-start.2 = (bf16[128,1536]{1,0:T(8,128)(2,1)S(1)}, bf16[128,1536]{1,0:T(8,128)(2,1)}, u32[]{:S(2)}) copy-start(bf16[128,1536]{1,0:T(8,128)(2,1)} %k_ref.7) | copy-start | bytes 1179652
  29.3 21.3 %copy-start.10 = (f32[1536]{0:T(1024)S(1)}, f32[1536]{0:T(1024)}, u32[]{:S(2)}) copy-start(f32[1536]{0:T(1024)} %param.11) | copy-start | bytes 18436
  46.6 4.0 %copy-start.7 = (f32[16,128]{1,0:T(8,128)S(1)}, f32[16,128]{1,0:T(8,128)}, u32[]{:S(2)}) copy-start(f32[16,128]{1,0:T(8,128)} %logs_ref.11) | copy-start | bytes 24580
  46.7 6.1 %collective-permute-start.1 = (f32[576,128]{1,0:T(8,128)S(1)}, f32[576,128]{1,0:T(8,128)S(1)}, u32[]{:S(2)}, u32[]{:S(2)}) collective-permute-start(f32[576,128]{1,0:T(8,128)S(1)} %bitcast.14), channel_id=1, source_target_pairs={{0,4},{4,0},{1,5},{5,1},{2,6},{6,2},{3,7},{7,3},{8,12},{12,8},{9,1... | collective-permute-start | bytes 884744 | tf_op jit(solution)/shard_map/ppermute | solution.py:372
  50.7 2.0 %copy-start.5 = (bf16[128,1536]{1,0:T(8,128)(2,1)S(1)}, bf16[128,1536]{1,0:T(8,128)(2,1)}, u32[]{:S(2)}) copy-start(bf16[128,1536]{1,0:T(8,128)(2,1)} %y_ref.3) | copy-start | bytes 1179652
  53.9 0.8 copy-start.8
  64.7 4.4 %collective-permute-start.2 = (f32[1152,128]{1,0:T(8,128)S(1)}, f32[1152,128]{1,0:T(8,128)S(1)}, u32[]{:S(2)}, u32[]{:S(2)}) collective-permute-start(f32[1152,128]{1,0:T(8,128)S(1)} %get-tuple-element.27.own_ref), channel_id=1, source_target_pairs={{0,4},{4,0},{1,5},{5,1},{2,6},{6,2},{3,7},{7,3},{8,12},{12,8},{9,1... | collective-permute-start | bytes 1769480 | tf_op jit(solution)/shard_map/ppermute | solution.py:372
  83.5 20.9 %copy-start.9 = (f32[1152,128]{1,0:T(8,128)S(1)}, f32[1152,128]{1,0:T(8,128)}, u32[]{:S(2)}) copy-start(f32[1152,128]{1,0:T(8,128)} %copy-done.8) | copy-start | bytes 1769476
  100.4 8.6 %collective-permute-start.3 = (f32[576,128]{1,0:T(8,128)S(1)}, f32[576,128]{1,0:T(8,128)S(1)}, u32[]{:S(2)}, u32[]{:S(2)}) collective-permute-start(f32[576,128]{1,0:T(8,128)S(1)} %bitcast.12), channel_id=1, source_target_pairs={{0,4},{4,0},{1,5},{5,1},{2,6},{6,2},{3,7},{7,3},{8,12},{12,8},{9,1... | collective-permute-start | bytes 884744 | tf_op jit(solution)/shard_map/ppermute | solution.py:372

commit v2 on v1

--- a/solution.py
+++ b/solution.py
@@ -18,7 +18,7 @@
 FWD_PART = 20
 ROWS = LOCAL_HEADS * PACK
 HALF_ROWS = HALF * PACK
-VMEM = 48 * 1024 * 1024
+VMEM = 12 * 1024 * 1024
 
 F32 = jnp.float32
 BF16 = jnp.bfloat16
@@ -146,22 +146,30 @@
     return jnp.where(keep, jnp.exp(jnp.where(keep, spread_by, 0.0)), 0.0)
 
 
-def outer_states(left_ref, scale, right, out_ref):
-    for g in range(4):
-        turned = left_ref[:, 384 * g : 384 * g + 384].astype(F32).T
+def turn_and_scale(left_ref, scale, g):
+    turned = left_ref[:, 384 * g : 384 * g + 384].astype(F32).T
+    return [
+        jnp.concatenate(two(turned[96 * j : 96 * j + 96, :] * scale[4 * g + j : 4 * g + j + 1, :]), axis=0)
+        for j in range(4)
+    ]
+
+
+def outer_states(left, right, out_ref):
+    for g in range(4):
         for j in range(4):
             h = 4 * g + j
-            high, low = two(turned[96 * j : 96 * j + 96, :] * scale[h : h + 1, :])
-            both = dot_nn(jnp.concatenate([high, low], axis=0), head_tiles(right, g, j, True))
+            both = dot_nn(left(h), head_tiles(right, g, j, True))
             square = merge(both[:96] + both[96:])
             for i, piece in enumerate(pack(square, j)):
                 out_ref[PACK * h + 24 * i : PACK * h + 24 * i + 24, :] = piece
 
 
-def state_kernel(k_ref, v_ref, logs_ref, x_ref):
+def state_kernel(kv_ref, logs_ref, x_ref):
     accum = running(logs_ref[...])
     last = accum[:, LANES - 1 :]
-    outer_states(k_ref, jnp.exp(last - accum), v_ref, x_ref)
+    tail = jnp.exp(last - accum)
+    turned = [both for g in range(4) for both in turn_and_scale(kv_ref[:TOKENS], tail, g)]
+    outer_states(lambda h: turned[h], kv_ref[TOKENS:], x_ref)
     x_ref[ROWS : ROWS + LOCAL_HEADS, :] = jnp.broadcast_to(jnp.exp(last), (LOCAL_HEADS, LANES))
 
 
@@ -202,25 +210,31 @@
         out_ref[PACK * h : PACK * h + PACK, :] = late * early_decay[h : h + 1, :] + early
 
 
+def turned_bits(c):
+    return sum(((c >> b) & 1) << (4 - b) for b in range(5))
+
+
 def scan_forward_kernel(in_ref, out_ref, decay_ref):
     state = jnp.zeros((PART, LANES), F32)
     for c in range(CHIPS):
-        out_ref[PART * c : PART * c + PART, :] = state
-        at = FWD_PART * c
+        place = turned_bits(c)
+        out_ref[PART * place : PART * place + PART, :] = state
+        at = FWD_PART * place
         decay = in_ref[at + PART : at + PART + 1, :]
         decay_ref[c : c + 1, :] = decay
         state = state * decay + in_ref[at : at + PART, :]
 
 
-def scan_backward_kernel(in_ref, decay_ref, out_ref):
+def scan_backward_kernel(in_ref, decay_ref, after_ref, out_ref):
     state = jnp.zeros((PART, LANES), F32)
     for c in reversed(range(CHIPS)):
-        out_ref[PART * c : PART * c + PART, :] = state
-        state = state * decay_ref[c : c + 1, :] + in_ref[PART * c : PART * c + PART, :]
-
-
-def finish_states(mine, other, add_ref, decay, own_ref, got_ref, out_ref):
-    for h in range(LOCAL_HEADS):
+        at = PART * turned_bits(c)
+        out_ref[at : at + PART, :] = state
+        state = state * decay_ref[c : c + 1, :] + in_ref[at : at + PART, :]
+
+
+def finish_states(g, mine, other, add_ref, decay, own_ref, got_ref, out_ref):
+    for h in range(4 * g, 4 * g + 4):
         at = PACK * (h % HALF)
         own = own_ref[at : at + PACK, :]
         got = got_ref[at : at + PACK, :]
@@ -229,6 +243,13 @@
         out_ref[PACK * h : PACK * h + PACK, :] = jnp.where(other, stepped, state)
 
 
+def add_tiles(tiles, part, j):
+    for i in range(SPAN[j] // LANES):
+        t = START[j] // LANES + i
+        piece = part[:, LANES * i : LANES * i + LANES]
+        tiles[t] = piece if tiles[t] is None else tiles[t] + piece
+
+
 def inner_kernel(q_ref, k_ref, v_ref, logs_ref, inner_ref):
     accum = running(logs_ref[...])
     cols = columns(accum)
@@ -238,11 +259,7 @@
             h = 4 * g + j
             scores = dot_nt(head_tiles(q_ref, g, j, True), head_tiles(k_ref, g, j, False))
             weights = (scores * weight_of(accum, cols, h)).astype(BF16)
-            part = dot_nn(weights, head_tiles(v_ref, g, j, True))
-            for i in range(SPAN[j] // LANES):
-                t = START[j] // LANES + i
-                piece = part[:, LANES * i : LANES * i + LANES]
-                tiles[t] = piece if tiles[t] is None else tiles[t] + piece
+            add_tiles(tiles, dot_nn(weights, head_tiles(v_ref, g, j, True)), j)
         for t in range(3):
             inner_ref[:, 384 * g + LANES * t : 384 * g + LANES * t + LANES] = tiles[t]
 
@@ -252,11 +269,11 @@
 ):
     core = core_ref[0]
     decay = got_state_ref[ROWS : ROWS + LOCAL_HEADS, :]
-    finish_states(core == 0, core == 1, got_state_ref, decay, own_ref, got_ref, state_ref)
     start = jnp.exp(columns(running(logs_ref[...])))
     squares = jnp.zeros((TOKENS, LANES), F32)
     crossed = jnp.zeros((TOKENS, LANES), F32)
     for g in range(4):
+        finish_states(g, core == 0, core == 1, got_state_ref, decay, own_ref, got_ref, state_ref)
         high, low = block_diagonal(state_ref, g)
         at = slice(384 * g, 384 * g + 384)
         q = q_ref[:, at]
@@ -272,10 +289,11 @@
     sums_ref[1:2, :] = jnp.sum(crossed.T, axis=0, keepdims=True)
 
 
-def norm_kernel(q_ref, y_ref, gain_ref, logs_ref, o_ref, sums_ref, back_ref, c_ref):
-    accum = running(logs_ref[...])
-    root = jnp.sqrt(sums_ref[0:1, :] / (HEADS * HEAD_DIM) + 1e-05)
-    factor = sums_ref[1:2, :] / (HEADS * HEAD_DIM * root * root * root)
+def norm_kernel(q_ref, y_ref, gain_ref, logs_ref, o_ref, sums_0, sums_1, sums_2, sums_3, back_ref, c_ref):
+    accum = running(logs_ref[...])
+    sums = (sums_0[...] + sums_1[...]) + (sums_2[...] + sums_3[...])
+    root = jnp.sqrt(sums[0:1, :] / (HEADS * HEAD_DIM) + 1e-05)
+    factor = sums[1:2, :] / (HEADS * HEAD_DIM * root * root * root)
     cols = columns(jnp.concatenate([1.0 / root, factor], axis=0))
     inverse = jnp.broadcast_to(cols[:, 0:1], (TOKENS, 384))
     factor = jnp.broadcast_to(cols[:, 1:2], (TOKENS, 384))
@@ -283,11 +301,14 @@
         at = slice(384 * g, 384 * g + 384)
         scaled = gain_ref[:, at] * y_ref[:, at].astype(F32)
         back_ref[:, at] = (scaled * inverse - o_ref[:, at] * factor).astype(BF16)
-    outer_states(q_ref, jnp.exp(accum), back_ref, c_ref)
-
-
-def middle_kernel(q_ref, k_ref, v_ref, back_ref, logs_ref, state_ref, gq_ref, gk_ref, gv_ref):
-    accum = running(logs_ref[...])
+    scale = jnp.exp(accum)
+    turned = [both for g in range(4) for both in turn_and_scale(q_ref, scale, g)]
+    outer_states(lambda h: turned[h], back_ref, c_ref)
+
+
+def middle_kernel(q_ref, k_ref, v_ref, back_ref, logs_ref, state_ref, gq_ref, gk_ref, done_ref):
+    accum = running(logs_ref[...])
+    done_ref[...] = accum[:8]
     cols = columns(accum)
     start = jnp.exp(cols)
     for g in range(4):
@@ -297,42 +318,47 @@
         gq = group_columns(start, g) * (dot_nt(back, high) + dot_nt(back, low))
         gq = [gq[:, LANES * t : LANES * t + LANES] for t in range(3)]
         gk = [None] * 3
-        gv = [None] * 3
         for j in range(4):
             h = 4 * g + j
             q = head_tiles(q_ref, g, j, True)
             k = head_tiles(k_ref, g, j, True)
             v = head_tiles(v_ref, g, j, False)
             d = head_tiles(back_ref, g, j, True)
-            weight = weight_of(accum, cols, h)
-            turned = weight_turned(accum, cols, h)
-            weights = (dot_nt(d, v) * weight).astype(BF16)
-            weights_t = (dot_nt(v, d) * turned).astype(BF16)
-            qk_t = (dot_nt(k, q) * turned).astype(BF16)
-            to_q = dot_nn(weights, k)
-            to_k = dot_nn(weights_t, q)
-            to_v = dot_nn(qk_t, d)
-            for i in range(SPAN[j] // LANES):
-                t = START[j] // LANES + i
-                lane = slice(LANES * i, LANES * i + LANES)
-                gq[t] = gq[t] + to_q[:, lane]
-                gk[t] = to_k[:, lane] if gk[t] is None else gk[t] + to_k[:, lane]
-                gv[t] = to_v[:, lane] if gv[t] is None else gv[t] + to_v[:, lane]
+            weights = (dot_nt(d, v) * weight_of(accum, cols, h)).astype(BF16)
+            weights_t = (dot_nt(v, d) * weight_turned(accum, cols, h)).astype(BF16)
+            add_tiles(gq, dot_nn(weights, k), j)
+            add_tiles(gk, dot_nn(weights_t, q), j)
         for t in range(3):
             lane = slice(384 * g + LANES * t, 384 * g + LANES * t + LANES)
             gq_ref[:, lane] = gq[t].astype(BF16)
             gk_ref[:, lane] = gk[t]
-            gv_ref[:, lane] = gv[t]
+
+
+def values_kernel(q_ref, k_ref, back_ref, logs_ref, gv_ref):
+    accum = running(logs_ref[...])
+    cols = columns(accum)
+    for g in range(4):
+        gv = [None] * 3
+        for j in range(4):
+            h = 4 * g + j
+            scores = dot_nt(head_tiles(k_ref, g, j, True), head_tiles(q_ref, g, j, False))
+            weights = (scores * weight_turned(accum, cols, h)).astype(BF16)
+            add_tiles(gv, dot_nn(weights, head_tiles(back_ref, g, j, True)), j)
+        for t in range(3):
+            gv_ref[:, 384 * g + LANES * t : 384 * g + LANES * t + LANES] = gv[t]
 
 
 def last_kernel(
-    core_ref, k_ref, v_ref, logs_ref, gk0_ref, gv0_ref, own_ref, got_ref, got_c_ref, got_decay_ref, gk_ref, gv_ref, carry_ref
+    core_ref, k_ref, v_ref, logs_ref, gk0_ref, gv0_ref, own_ref, got_ref, got_c_ref, got_decay_ref,
+    gk_hbm, gv_hbm, carry_ref, gk_ref, gv_ref, sems,
 ):
     core = core_ref[0]
-    finish_states(core == 0, core == 0, got_c_ref, got_decay_ref[...], own_ref, got_ref, carry_ref)
+    decay = got_decay_ref[...]
     accum = running(logs_ref[...])
     tail = columns(jnp.exp(accum[:, LANES - 1 :] - accum))
-    for g in range(4):
+    copies = []
+    for g in range(4):
+        finish_states(g, core == 0, core == 0, got_c_ref, decay, own_ref, got_ref, carry_ref)
         high, low = block_diagonal(carry_ref, g)
         at = slice(384 * g, 384 * g + 384)
         k = k_ref[:, at]
@@ -340,24 +366,28 @@
         wide = group_columns(tail, g)
         gk_ref[:, at] = (gk0_ref[:, at] + wide * (dot_nt(v, high) + dot_nt(v, low))).astype(BF16)
         gv_ref[:, at] = (gv0_ref[:, at] + wide * (dot_nn(k, high) + dot_nn(k, low))).astype(BF16)
-
-
-def call(kernel, outs, smem, *args, scratch=(), flops=0):
+        for i, (src, dst) in enumerate(((gk_ref, gk_hbm), (gv_ref, gv_hbm))):
+            copy = pltpu.make_async_copy(src.at[:, at], dst.at[:, at], sems.at[2 * g + i])
+            copy.start()
+            copies.append(copy)
+    for copy in copies:
+        copy.wait()
+
+
+def call(kernel, outs, smem, *args, hbm_in=(), hbm_out=(), scratch=(), flops=0, vmem=VMEM):
     specs = []
     for i, arg in enumerate(args):
-        if i < smem:
-            specs.append(pl.BlockSpec(memory_space=pltpu.SMEM))
-        else:
-            specs.append(pl.BlockSpec(memory_space=pltpu.VMEM))
+        space = pltpu.SMEM if i < smem else pltpu.HBM if i in hbm_in else pltpu.VMEM
+        specs.append(pl.BlockSpec(memory_space=space))
     shapes = [jax.ShapeDtypeStruct(s, d) for s, d in outs]
     moved = sum(a.size * a.dtype.itemsize for a in args) + sum(s.size * s.dtype.itemsize for s in shapes)
     out = pl.pallas_call(
         kernel,
         out_shape=shapes,
         in_specs=specs,
-        out_specs=[pl.BlockSpec(memory_space=pltpu.VMEM)] * len(shapes),
+        out_specs=[pl.BlockSpec(memory_space=pltpu.HBM if i in hbm_out else pltpu.VMEM) for i in range(len(shapes))],
         scratch_shapes=scratch,
-        compiler_params=pltpu.CompilerParams(vmem_limit_bytes=VMEM),
+        compiler_params=pltpu.CompilerParams(vmem_limit_bytes=vmem),
         cost_estimate=pl.CostEstimate(flops=flops, bytes_accessed=moved, transcendentals=0),
         name=kernel.__name__,
     )(*args)
@@ -365,7 +395,7 @@
 
 
 SWAP = [(0, 1), (1, 0)]
-CHIP_AXES = ("x", "z")
+CHIP_BITS = ("xh", "xl", "zh", "zm", "zl")
 
 
 def swap(value):
@@ -373,22 +403,28 @@
 
 
 def exchange(value):
-    flat = lax.all_to_all(value.reshape(-1), CHIP_AXES, 0, 0, tiled=True)
-    return flat.reshape(value.shape)
+    parts = value.reshape(CHIPS, -1, 2, LANES)
+    return lax.all_to_all(parts, CHIP_BITS[::-1], 0, 0, tiled=True).reshape(value.shape)
+
+
+def others(value):
+    return [lax.ppermute(value, "head", [(i, (i + k) % 4) for i in range(4)]) for k in (1, 2, 3)]
 
 
 def local(q, k, v, y, logs, gain):
     core = lax.axis_index("core").astype(jnp.int32).reshape(1)
     gain = gain.reshape(1, WIDTH)
     wide = (TOKENS, WIDTH)
-    x = call(state_kernel, [((ROWS + LOCAL_HEADS, LANES), F32)], 0, k, v, logs, flops=2 * 10**8)
+    narrow = pltpu.VMEM(wide, BF16)
+    decay = ((LOCAL_HEADS, LANES), F32)
+    x = call(state_kernel, [((ROWS + LOCAL_HEADS, LANES), F32)], 0, jnp.concatenate([k, v]), logs, flops=10**9)
     got_x = swap(x)
-    decay = ((LOCAL_HEADS, LANES), F32)
     payload, own_decay, got_decay = call(
         combine_forward_kernel, [((CHIPS * FWD_PART, LANES), F32), decay, decay], 1, core, x, got_x
     )
     payload = exchange(payload)
-    inner = call(inner_kernel, [(wide, F32)], 0, q, k, v, logs, flops=4 * 10**8)
+    token = ((8, LANES), F32)
+    inner = call(inner_kernel, [(wide, F32)], 0, q, k, v, logs, flops=2 * 10**9)
     entering, decays = call(scan_forward_kernel, [((HALF_ROWS, LANES), F32), ((CHIPS, LANES), F32)], 0, payload)
     entering = exchange(entering)
     got_entering = swap(entering)
@@ -396,34 +432,40 @@
         attention_kernel,
         [(wide, F32), ((ROWS, LANES), F32), ((2, LANES), F32)],
         1, core, q, y, gain, logs, inner, entering, got_entering, got_x,
-        flops=4 * 10**8,
-    )
-    sums = lax.psum(sums, "head")
-    back, c = call(norm_kernel, [(wide, BF16), ((ROWS, LANES), F32)], 0, q, y, gain, logs, attention, sums, flops=2 * 10**8)
+        flops=10**9,
+    )
+    back, c = call(
+        norm_kernel,
+        [(wide, BF16), ((ROWS, LANES), F32)],
+        0, q, y, gain, logs, attention, sums, *others(sums),
+        flops=10**9,
+    )
     got_c = swap(c)
     payload = call(
         combine_backward_kernel, [((HALF_ROWS, LANES), F32)], 1, core, c, got_c, own_decay, got_decay
     )
     payload = exchange(payload)
-    gq, gk0, gv0 = call(
-        middle_kernel, [(wide, BF16), (wide, F32), (wide, F32)], 0, q, k, v, back, logs, state, flops=10**9
-    )
-    leaving = call(scan_backward_kernel, [((HALF_ROWS, LANES), F32)], 0, payload, decays)
+    gq, gk0, middle_done = call(
+        middle_kernel, [(wide, BF16), (wide, F32), token], 0, q, k, v, back, logs, state, flops=4 * 10**9
+    )
+    leaving = call(scan_backward_kernel, [((HALF_ROWS, LANES), F32)], 0, payload, decays, middle_done)
     leaving = exchange(leaving)
     got_leaving = swap(leaving)
+    gv0 = call(values_kernel, [(wide, F32)], 0, q, k, back, logs, flops=2 * 10**9)
     gk, gv = call(
         last_kernel,
         [(wide, BF16), (wide, BF16)],
         1, core, k, v, logs, gk0, gv0, leaving, got_leaving, got_c, got_decay,
-        scratch=[pltpu.VMEM((ROWS, LANES), F32)],
-        flops=4 * 10**8,
+        hbm_out=(0, 1),
+        scratch=[pltpu.VMEM((ROWS, LANES), F32), narrow, narrow, pltpu.SemaphoreType.DMA((8,))],
+        flops=2 * 10**9,
     )
     return gq, gk, gv
 
 
 def solution(mesh):
-    grid = Mesh(mesh.devices.reshape(4, 8, 2, 4), ("x", "z", "core", "head"))
-    tokens = ("x", "z", "core")
+    tokens = (*CHIP_BITS, "core")
+    grid = Mesh(mesh.devices.reshape(2, 2, 2, 2, 2, 2, 4), (*tokens, "head"))
     rows = P(tokens, "head")
     return jax.shard_map(
         local,

time: 112 us -> 104 us (0.929)
  blocking collectives: 76.9 us -> 52.1 us
  waiting for transfers between devices: 3.28 us -> 12.4 us
  starting transfers between devices: 14.1 us -> 20.3 us
  local copies, waits for them, and re-layouts: 3.55 us -> 0.93 us
  Pallas kernels: 12.8 us -> 15.4 us
  other arithmetic: 0 us -> 1.17 us
    all_to_all x4 -> x3, blocking collectives: 68.2 us -> 52.1 us  [exchange(): lax.all_to_all(parts, CHIP_BITS[::-1], 0, 0, tiled=True)]
    psum x1 -> x0, blocking collectives: 8.69 us -> none  [local(): sums = lax.psum(sums, 'head')]
    all_to_all x0 -> x1, waiting for transfers between devices: none -> 6.19 us  [exchange(): lax.all_to_all(parts, CHIP_BITS[::-1], 0, 0, tiled=True)]
    all_to_all x0 -> x1, starting transfers between devices: none -> 4.81 us  [exchange(): lax.all_to_all(parts, CHIP_BITS[::-1], 0, 0, tiled=True)]
    ppermute x0 -> x3, starting transfers between devices: none -> 3.85 us  [others(): lax.ppermute(value, 'head', [(i, (i + k) % 4) for i in range(4)])]
    ppermute x0 -> x3, waiting for transfers between devices: none -> 2.94 us  [others(): lax.ppermute(value, 'head', [(i, (i + k) % 4) for i in range(4)])]
    unnamed x22 -> x16, local copies, waits for them, and re-layouts: 3.54 us -> 0.93 us
    pallas_call x10 -> x11, Pallas kernels: 12.8 us -> 15.4 us  [call(): pl.pallas_call(kernel, out_shape=shapes, in_specs=specs, out_specs=[pl.Bl...]
  transfers between devices with their start and end apart: 4 -> 8, of which waited for: 2 -> 5; matrix products, arithmetic and copies ran while one was open for 0% -> 0% of each run, Pallas kernels for 6% -> 8%
where the time goes in v2:
time: 104 us; the launch traced here: 103 us
  blocking collectives  52.1 us (50%)
  starting transfers between devices  20.3 us (20%)
  Pallas kernels  15.4 us (15%)
  waiting for transfers between devices  12.4 us (12%)
  other arithmetic  1.17 us (1%)
    all_to_all x3, blocking collectives, exchange(): lax.all_to_all(parts, CHIP_BITS[::-1], 0, 0, tiled=True)  52.1 us
    pallas_call x11, Pallas kernels, call(): pl.pallas_call(kernel, out_shape=shapes, in_specs=specs, out_specs=[pl.Bl...  15.4 us
    ppermute x4, starting transfers between devices, swap(): return lax.ppermute(value, 'core', SWAP)  11.7 us
    all_to_all x1, waiting for transfers between devices, exchange(): lax.all_to_all(parts, CHIP_BITS[::-1], 0, 0, tiled=True)  6.19 us
    all_to_all x1, starting transfers between devices, exchange(): lax.all_to_all(parts, CHIP_BITS[::-1], 0, 0, tiled=True)  4.81 us
    ppermute x3, starting transfers between devices, others(): lax.ppermute(value, 'head', [(i, (i + k) % 4) for i in range(4)])  3.85 us
    ppermute x4, waiting for transfers between devices, swap(): return lax.ppermute(value, 'core', SWAP)  3.28 us
    ppermute x3, waiting for transfers between devices, others(): lax.ppermute(value, 'head', [(i, (i + k) % 4) for i in range(4)])  2.94 us
  transfers between devices with their start and end apart: 8, of which 5 were waited for; matrix products, arithmetic and copies ran while one was open for 0% of the time, Pallas kernels for 8%

profile of v2, /device:TPU:1, one launch (start us, length us, event | category | flops | bytes accessed | tf_op | source)
XLA Modules:
  0.0 103.3 jit_solution(654773621893416415)
XLA Ops:
  0.6 0.0 copy-start.4
  0.6 1.2 %pad_maximum_fusion.kv_ref = bf16[256,1536]{1,0:T(8,128)(2,1)S(1)} fusion(bf16[128,1536]{1,0:T(8,128)(2,1)} %v_ref.5, bf16[128,1536]{1,0:T(8,128)(2,1)} %k_ref.7), kind=kLoop, calls=%fused_computation | loop fusion | flops 1572864 | bytes 1572864 | tf_op jit(solution)/shard_map/concatenate | solution.py:420
  1.8 0.0 copy-done.4
  1.8 1.2 %state_kernel.1.own_ref = f32[1168,128]{1,0:T(8,128)S(1)} custom-call(bf16[256,1536]{1,0:T(8,128)(2,1)S(1)} %pad_maximum_fusion.kv_ref, f32[16,128]{1,0:T(8,128)S(1)} %copy-done.4), custom_call_target="tpu_custom_call" | custom-call | flops 1000000000 | bytes 1392640 | tf_op jit(solution)/shard_map/state_kernel/pallas_call | solution.py:384
  3.0 3.3 %collective-permute-start = (f32[1168,128]{1,0:T(8,128)S(1)}, f32[1168,128]{1,0:T(8,128)S(1)}, u32[]{:S(2)}, u32[]{:S(2)}) collective-permute-start(f32[1168,128]{1,0:T(8,128)S(1)} %state_kernel.1.own_ref), channel_id=1, source_target_pairs={{0,4},{4,0},{1,5},{5,1},{2,6},{6,2},{3,7},{7,3},{8,12},{12,8},{9,1... | collective-permute-start | bytes 1794056 | tf_op jit(solution)/shard_map/ppermute | solution.py:402
  6.4 1.6 %collective-permute-done.got_ref.got_state_ref = f32[1168,128]{1,0:T(8,128)S(1)} collective-permute-done((f32[1168,128]{1,0:T(8,128)S(1)}, f32[1168,128]{1,0:T(8,128)S(1)}, u32[]{:S(2)}, u32[]{:S(2)}) %collective-permute-start) | collective-permute-done | bytes 598048 | tf_op jit(solution)/shard_map/ppermute | solution.py:402
  8.0 0.1 combine_forward_kernel.1
  8.1 0.0 copy-start.7
  8.1 0.0 copy-start
  8.1 0.0 copy-start.1
  8.1 0.0 copy-start.3
  8.1 21.5 %all_to_all.20 = f32[32,10,2,128]{3,2,1,0:T(2,128)S(1)} all-to-all(f32[32,10,2,128]{3,2,1,0:T(2,128)S(1)} %bitcast.12), channel_id=1, replica_groups=mesh['xh'=2,'xl'=2,'zh'=2,'zm'=2,'zl'=2,'core'=2,'head'=4] {'zl','zm','z..., dimensions={0} | all-to-all | bytes 655360 | tf_op jit(solution)/shard_map/all_to_all | solution.py:407
  29.6 0.1 scan_forward_kernel.1
  29.7 15.4 %all_to_all.21 = f32[32,9,2,128]{3,2,1,0:T(2,128)S(1)} all-to-all(f32[32,9,2,128]{3,2,1,0:T(2,128)S(1)} %bitcast.17), channel_id=1, replica_groups=mesh['xh'=2,'xl'=2,'zh'=2,'zm'=2,'zl'=2,'core'=2,'head'=4] {'zl','zm','z..., dimensions={0} | all-to-all | bytes 589824 | tf_op jit(solution)/shard_map/all_to_all | solution.py:407
  45.1 3.2 %collective-permute-start.1 = (f32[576,128]{1,0:T(8,128)S(1)}, f32[576,128]{1,0:T(8,128)S(1)}, u32[]{:S(2)}, u32[]{:S(2)}) collective-permute-start(f32[576,128]{1,0:T(8,128)S(1)} %bitcast.15), channel_id=1, source_target_pairs={{0,4},{4,0},{1,5},{5,1},{2,6},{6,2},{3,7},{7,3},{8,12},{12,8},{9,1... | collective-permute-start | bytes 884744 | tf_op jit(solution)/shard_map/ppermute | solution.py:402
  48.3 0.0 copy-done.7
  48.3 0.0 copy-done
  48.3 0.0 copy-done.1
  48.3 0.0 copy-done.3
  48.3 0.0 copy-start.2
  48.3 2.0 %inner_kernel.1.inner_ref = f32[128,1536]{1,0:T(8,128)S(1)} custom-call(bf16[128,1536]{1,0:T(8,128)(2,1)S(1)} %copy-done.3, bf16[128,1536]{1,0:T(8,128)(2,1)S(1)} %copy-done, bf16[128,1536]{1,0:T(8,128)(2,1)S(1)} %copy-done.1, f32[16,128]{1,0:T(8,128)S(1)} %copy-done.4), custom_call_target="tpu_custom_call" | custom-call | flops 2000000000 | bytes 1974272 | tf_op jit(solution)/shard_map/inner_kernel/pallas_call | solution.py:384
  50.4 0.0 collective-permute-done.1.got_ref
  50.4 0.0 copy-done.2
  50.4 1.2 %attention_kernel.1 = (f32[128,1536]{1,0:T(8,128)S(1)}, f32[1152,128]{1,0:T(8,128)S(1)}, f32[2,128]{1,0:T(2,128)S(1)}) custom-call(s32[1]{0:T(128)} %bitcast.core_ref, bf16[128,1536]{1,0:T(8,128)(2,1)S(1)} %copy-done.3, bf16[128,1536]{1,0:T(8,128)(2,1)S(1)} %copy-done.2, f32[1,1536]{1,0:T(1,128)S(1)} %reshape.36.gain_ref, f32[16,128]{1,0:T(8,128)S(1)} %copy-done.4, ...), custom_call_target="tpu_custom_call" | custom-call | flops 1000000000 | bytes 4152324 | tf_op jit(solution)/shard_map/attention_kernel/pallas_call | solution.py:384
  51.6 2.8 %collective-permute-start.4 = (f32[2,128]{1,0:T(2,128)S(1)}, f32[2,128]{1,0:T(2,128)S(1)}, u32[]{:S(2)}, u32[]{:S(2)}) collective-permute-start(f32[2,128]{1,0:T(2,128)S(1)} %get-tuple-element.21.sums_0), channel_id=1, source_target_pairs={{0,3},{1,0},{2,1},{3,2},{4,7},{5,4},{6,5},{7,6},{8,11},{9,8},{10,9... | collective-permute-start | bytes 3080 | tf_op jit(solution)/shard_map/ppermute | solution.py:411
  54.4 0.4 collective-permute-start.3
  54.7 0.7 collective-permute-start.2
  55.4 0.0 collective-permute-done.4.sums_3
  55.4 2.9 %collective-permute-done.3.sums_2 = f32[2,128]{1,0:T(2,128)S(1)} collective-permute-done((f32[2,128]{1,0:T(2,128)S(1)}, f32[2,128]{1,0:T(2,128)S(1)}, u32[]{:S(2)}, u32[]{:S(2)}) %collective-permute-start.3) | collective-permute-done | bytes 1056 | tf_op jit(solution)/shard_map/ppermute | solution.py:411
  58.3 0.1 collective-permute-done.2.sums_1
  58.3 1.2 %norm_kernel.1 = (bf16[128,1536]{1,0:T(8,128)(2,1)S(1)}, f32[1152,128]{1,0:T(8,128)S(1)}) custom-call(bf16[128,1536]{1,0:T(8,128)(2,1)S(1)} %copy-done.3, bf16[128,1536]{1,0:T(8,128)(2,1)S(1)} %copy-done.2, f32[1,1536]{1,0:T(1,128)S(1)} %reshape.36.gain_ref, f32[16,128]{1,0:T(8,128)S(1)} %copy-done.4, f32[128,1536]{1,0:T(8,128)S(1)} %get-tuple-element.20.o_ref, ...), custom_call_target="tpu_custom_call" | custom-call | flops 1000000000 | bytes 2574336 | tf_op jit(solution)/shard_map/norm_kernel/pallas_call | solution.py:384
  59.6 1.8 %collective-permute-start.5 = (f32[1152,128]{1,0:T(8,128)S(1)}, f32[1152,128]{1,0:T(8,128)S(1)}, u32[]{:S(2)}, u32[]{:S(2)}) collective-permute-start(f32[1152,128]{1,0:T(8,128)S(1)} %get-tuple-element.26.own_ref), channel_id=1, source_target_pairs={{0,4},{4,0},{1,5},{5,1},{2,6},{6,2},{3,7},{7,3},{8,12},{12,8},{9,1... | collective-permute-start | bytes 1769480 | tf_op jit(solution)/shard_map/ppermute | solution.py:402
  61.4 1.6 %collective-permute-done.5.got_ref.got_c_ref = f32[1152,128]{1,0:T(8,128)S(1)} collective-permute-done((f32[1152,128]{1,0:T(8,128)S(1)}, f32[1152,128]{1,0:T(8,128)S(1)}, u32[]{:S(2)}, u32[]{:S(2)}) %collective-permute-start.5) | collective-permute-done | bytes 589856 | tf_op jit(solution)/shard_map/ppermute | solution.py:402
  63.0 0.8 combine_backward_kernel.1
  63.8 4.8 %all-to-all-start.2 = ((f32[32,9,2,128]{3,2,1,0:T(2,128)}), f32[32,9,2,128]{3,2,1,0:T(2,128)S(1)}, u32[]{:S(2)}, u32[]{:S(2)}) async-start(f32[32,9,2,128]{3,2,1,0:T(2,128)} %bitcast.5), calls=%async_computation.2 | async-start | bytes 589824 | tf_op jit(solution)/shard_map/all_to_all | solution.py:407
  68.6 4.4 %middle_kernel.1 = (bf16[128,1536]{1,0:T(8,128)(2,1)}, f32[128,1536]{1,0:T(8,128)S(1)}, f32[8,128]{1,0:T(8,128)S(1)}) custom-call(bf16[128,1536]{1,0:T(8,128)(2,1)S(1)} %copy-done.3, bf16[128,1536]{1,0:T(8,128)(2,1)S(1)} %copy-done, bf16[128,1536]{1,0:T(8,128)(2,1)S(1)} %copy-done.1, bf16[128,1536]{1,0:T(8,128)(2,1)S(1)} %get-tuple-element.22.back_ref, ...), custom_call_target="tpu_custom_call" | custom-call | flops 4000000000 | bytes 3354624 | tf_op jit(solution)/shard_map/middle_kernel/pallas_call | solution.py:384
  73.0 0.0 copy-start.5
  73.0 0.9 copy-done.5
  73.9 6.2 %all-to-all-done.2 = f32[32,9,2,128]{3,2,1,0:T(2,128)S(1)} async-done(((f32[32,9,2,128]{3,2,1,0:T(2,128)}), f32[32,9,2,128]{3,2,1,0:T(2,128)S(1)}, u32[]{:S(2)}, u32[]{:S(2)}) %all-to-all-start.2) | async-done | bytes 294944 | tf_op jit(solution)/shard_map/all_to_all | solution.py:407
  80.1 0.1 scan_backward_kernel.1
  80.2 15.2 %all_to_all.22 = f32[32,9,2,128]{3,2,1,0:T(2,128)S(1)} all-to-all(f32[32,9,2,128]{3,2,1,0:T(2,128)S(1)} %bitcast.11), channel_id=1, replica_groups=mesh['xh'=2,'xl'=2,'zh'=2,'zm'=2,'zl'=2,'core'=2,'head'=4] {'zl','zm','z..., dimensions={0} | all-to-all | bytes 589824 | tf_op jit(solution)/shard_map/all_to_all | solution.py:407
  95.4 0.0 copy-start.6
  95.4 3.4 %collective-permute-start.6 = (f32[576,128]{1,0:T(8,128)S(1)}, f32[576,128]{1,0:T(8,128)S(1)}, u32[]{:S(2)}, u32[]{:S(2)}) collective-permute-start(f32[576,128]{1,0:T(8,128)S(1)} %bitcast.13), channel_id=1, source_target_pairs={{0,4},{4,0},{1,5},{5,1},{2,6},{6,2},{3,7},{7,3},{8,12},{12,8},{9,1... | collective-permute-start | bytes 884744 | tf_op jit(solution)/shard_map/ppermute | solution.py:402
  98.8 2.0 %values_kernel.1.gv0_ref = f32[128,1536]{1,0:T(8,128)S(1)} custom-call(bf16[128,1536]{1,0:T(8,128)(2,1)S(1)} %copy-done.3, bf16[128,1536]{1,0:T(8,128)(2,1)S(1)} %copy-done, bf16[128,1536]{1,0:T(8,128)(2,1)S(1)} %get-tuple-element.22.back_ref, f32[16,128]{1,0:T(8,128)S(1)} %copy-done.4), custom_call_target="tpu_custom_call" | custom-call | flops 2000000000 | bytes 1974272 | tf_op jit(solution)/shard_map/values_kernel/pallas_call | solution.py:384
  100.8 0.0 collective-permute-done.6.got_ref
  100.8 0.0 copy-done.6
  100.8 2.4 %last_kernel.1 = (bf16[128,1536]{1,0:T(8,128)(2,1)}, bf16[128,1536]{1,0:T(8,128)(2,1)}) custom-call(s32[1]{0:T(128)} %bitcast.core_ref, bf16[128,1536]{1,0:T(8,128)(2,1)S(1)} %copy-done, bf16[128,1536]{1,0:T(8,128)(2,1)S(1)} %copy-done.1, f32[16,128]{1,0:T(8,128)S(1)} %copy-done.4, f32[128,1536]{1,0:T(8,128)S(1)} %copy-done.6, ...), custom_call_target="tpu_custom_call" | custom-call | flops 2000000000 | bytes 4341764 | tf_op jit(solution)/shard_map/last_kernel/pallas_call | solution.py:384
  (1 shorter events, 0.0 us)
Async XLA Ops:
  0.6 1.2 %copy-start.4 = (f32[16,128]{1,0:T(8,128)S(1)}, f32[16,128]{1,0:T(8,128)}, u32[]{:S(2)}) copy-start(f32[16,128]{1,0:T(8,128)} %logs_ref.13) | copy-start | bytes 24580
  3.0 5.0 %collective-permute-start = (f32[1168,128]{1,0:T(8,128)S(1)}, f32[1168,128]{1,0:T(8,128)S(1)}, u32[]{:S(2)}, u32[]{:S(2)}) collective-permute-start(f32[1168,128]{1,0:T(8,128)S(1)} %state_kernel.1.own_ref), channel_id=1, source_target_pairs={{0,4},{4,0},{1,5},{5,1},{2,6},{6,2},{3,7},{7,3},{8,12},{12,8},{9,1... | collective-permute-start | bytes 1794056 | tf_op jit(solution)/shard_map/ppermute | solution.py:402
  8.1 40.2 %copy-start.7 = (f32[1536]{0:T(1024)S(1)}, f32[1536]{0:T(1024)}, u32[]{:S(2)}) copy-start(f32[1536]{0:T(1024)} %param.11) | copy-start | bytes 18436
  8.1 40.2 %copy-start = (bf16[128,1536]{1,0:T(8,128)(2,1)S(1)}, bf16[128,1536]{1,0:T(8,128)(2,1)}, u32[]{:S(2)}) copy-start(bf16[128,1536]{1,0:T(8,128)(2,1)} %k_ref.7) | copy-start | bytes 1179652
  8.1 40.2 %copy-start.1 = (bf16[128,1536]{1,0:T(8,128)(2,1)S(1)}, bf16[128,1536]{1,0:T(8,128)(2,1)}, u32[]{:S(2)}) copy-start(bf16[128,1536]{1,0:T(8,128)(2,1)} %v_ref.5) | copy-start | bytes 1179652
  8.1 40.2 %copy-start.3 = (bf16[128,1536]{1,0:T(8,128)(2,1)S(1)}, bf16[128,1536]{1,0:T(8,128)(2,1)}, u32[]{:S(2)}) copy-start(bf16[128,1536]{1,0:T(8,128)(2,1)} %q_ref.9) | copy-start | bytes 1179652
  45.1 5.3 %collective-permute-start.1 = (f32[576,128]{1,0:T(8,128)S(1)}, f32[576,128]{1,0:T(8,128)S(1)}, u32[]{:S(2)}, u32[]{:S(2)}) collective-permute-start(f32[576,128]{1,0:T(8,128)S(1)} %bitcast.15), channel_id=1, source_target_pairs={{0,4},{4,0},{1,5},{5,1},{2,6},{6,2},{3,7},{7,3},{8,12},{12,8},{9,1... | collective-permute-start | bytes 884744 | tf_op jit(solution)/shard_map/ppermute | solution.py:402
  48.3 2.0 %copy-start.2 = (bf16[128,1536]{1,0:T(8,128)(2,1)S(1)}, bf16[128,1536]{1,0:T(8,128)(2,1)}, u32[]{:S(2)}) copy-start(bf16[128,1536]{1,0:T(8,128)(2,1)} %y_ref.3) | copy-start | bytes 1179652
  51.6 3.9 %collective-permute-start.4 = (f32[2,128]{1,0:T(2,128)S(1)}, f32[2,128]{1,0:T(2,128)S(1)}, u32[]{:S(2)}, u32[]{:S(2)}) collective-permute-start(f32[2,128]{1,0:T(2,128)S(1)} %get-tuple-element.21.sums_0), channel_id=1, source_target_pairs={{0,3},{1,0},{2,1},{3,2},{4,7},{5,4},{6,5},{7,6},{8,11},{9,8},{10,9... | collective-permute-start | bytes 3080 | tf_op jit(solution)/shard_map/ppermute | solution.py:411
  54.4 3.9 %collective-permute-start.3 = (f32[2,128]{1,0:T(2,128)S(1)}, f32[2,128]{1,0:T(2,128)S(1)}, u32[]{:S(2)}, u32[]{:S(2)}) collective-permute-start(f32[2,128]{1,0:T(2,128)S(1)} %get-tuple-element.21.sums_0), channel_id=1, source_target_pairs={{0,2},{1,3},{2,0},{3,1},{4,6},{5,7},{6,4},{7,5},{8,10},{9,11},{10,... | collective-permute-start | bytes 3080 | tf_op jit(solution)/shard_map/ppermute | solution.py:411
  54.7 3.6 %collective-permute-start.2 = (f32[2,128]{1,0:T(2,128)S(1)}, f32[2,128]{1,0:T(2,128)S(1)}, u32[]{:S(2)}, u32[]{:S(2)}) collective-permute-start(f32[2,128]{1,0:T(2,128)S(1)} %get-tuple-element.21.sums_0), channel_id=1, source_target_pairs={{0,1},{1,2},{2,3},{3,0},{4,5},{5,6},{6,7},{7,4},{8,9},{9,10},{10,1... | collective-permute-start | bytes 3080 | tf_op jit(solution)/shard_map/ppermute | solution.py:411
  59.6 3.4 %collective-permute-start.5 = (f32[1152,128]{1,0:T(8,128)S(1)}, f32[1152,128]{1,0:T(8,128)S(1)}, u32[]{:S(2)}, u32[]{:S(2)}) collective-permute-start(f32[1152,128]{1,0:T(8,128)S(1)} %get-tuple-element.26.own_ref), channel_id=1, source_target_pairs={{0,4},{4,0},{1,5},{5,1},{2,6},{6,2},{3,7},{7,3},{8,12},{12,8},{9,1... | collective-permute-start | bytes 1769480 | tf_op jit(solution)/shard_map/ppermute | solution.py:402
  63.8 16.3 %all-to-all-start.2 = ((f32[32,9,2,128]{3,2,1,0:T(2,128)}), f32[32,9,2,128]{3,2,1,0:T(2,128)S(1)}, u32[]{:S(2)}, u32[]{:S(2)}) async-start(f32[32,9,2,128]{3,2,1,0:T(2,128)} %bitcast.5), calls=%async_computation.2 | async-start | bytes 589824 | tf_op jit(solution)/shard_map/all_to_all | solution.py:407
  73.0 0.9 copy-start.5
  95.4 5.4 %copy-start.6 = (f32[128,1536]{1,0:T(8,128)S(1)}, f32[128,1536]{1,0:T(8,128)}, u32[]{:S(2)}) copy-start(f32[128,1536]{1,0:T(8,128)} %copy-done.5) | copy-start | bytes 2359300
  95.4 5.4 %collective-permute-start.6 = (f32[576,128]{1,0:T(8,128)S(1)}, f32[576,128]{1,0:T(8,128)S(1)}, u32[]{:S(2)}, u32[]{:S(2)}) collective-permute-start(f32[576,128]{1,0:T(8,128)S(1)} %bitcast.13), channel_id=1, source_target_pairs={{0,4},{4,0},{1,5},{5,1},{2,6},{6,2},{3,7},{7,3},{8,12},{12,8},{9,1... | collective-permute-start | bytes 884744 | tf_op jit(solution)/shard_map/ppermute | solution.py:402

commit v3 on v2

--- a/solution.py
+++ b/solution.py
@@ -50,8 +50,12 @@
     return high, (x - high.astype(F32)).astype(BF16)
 
 
+def at_lanes(base, start, size):
+    return pl.ds(base + start if isinstance(base, int) else pl.multiple_of(base + start, LANES), size)
+
+
 def head_tiles(value, g, j, masked):
-    part = value[:, 384 * g + START[j] : 384 * g + START[j] + SPAN[j]]
+    part = value[:, at_lanes(384 * g, START[j], SPAN[j])]
     if masked:
         lane = lanes_of(part.shape)
         part = jnp.where((lane >= FIRST[j]) & (lane < FIRST[j] + HEAD_DIM), part, jnp.zeros_like(part))
@@ -87,30 +91,46 @@
     lane = lanes_of(square.shape)
     zero = jnp.zeros_like(square)
     if j == 0:
-        tiles = (jnp.where(lane < 96, square, zero), zero, zero)
+        tiles = (jnp.where(lane < 96, square, zero), zero)
     elif j == 1:
-        tiles = (jnp.where(lane >= 96, square, zero), jnp.where(lane < 64, square, zero), zero)
+        tiles = (jnp.where(lane >= 96, square, zero), jnp.where(lane < 64, square, zero))
     elif j == 2:
-        tiles = (zero, jnp.where(lane >= 64, square, zero), jnp.where(lane < 32, square, zero))
+        tiles = (jnp.where(lane >= 64, square, zero), jnp.where(lane < 32, square, zero))
     else:
-        tiles = (zero, zero, jnp.where(lane >= 32, square, zero))
+        tiles = (zero, jnp.where(lane >= 32, square, zero))
     return jnp.concatenate(tiles, axis=1)
 
 
-def block_diagonal(ref, g):
-    rows = []
-    for j in range(4):
+def pair_states(ref, g, pair):
+    parts = []
+    for j in (2 * pair, 2 * pair + 1):
         h = 4 * g + j
-        rows.append(spread(unpack(ref[PACK * h : PACK * h + PACK, :], j), j))
-    return two(jnp.concatenate(rows, axis=0))
+        parts.append([spread(part, j) for part in two(unpack(ref[PACK * h : PACK * h + PACK, :], j))])
+    zero = jnp.zeros((64, 256), BF16)
+    out = []
+    for first, second in zip(*parts):
+        rows = [first, second, zero] if pair == 0 else [zero, first, second]
+        out.append(jnp.concatenate(rows, axis=0))
+    return out
+
+
+def times_states(values, pairs, dot):
+    left, right = (
+        dot(values[:, LANES * p : LANES * p + 256], pairs[p][0])
+        + dot(values[:, LANES * p : LANES * p + 256], pairs[p][1])
+        for p in range(2)
+    )
+    return jnp.concatenate([left[:, :LANES], left[:, LANES:] + right[:, :LANES], right[:, LANES:]], axis=1)
 
 
 def running(logs):
-    lane = lanes_of(logs.shape)
-    total = logs
-    for k in (1, 2, 4, 8, 16, 32, 64):
-        total = total + jnp.where(lane >= k, pltpu.roll(total, k, 1), 0.0)
-    return total
+    high = logs.astype(BF16)
+    rest = logs - high.astype(F32)
+    middle = rest.astype(BF16)
+    low = (rest - middle.astype(F32)).astype(BF16)
+    shape = (LANES, LANES)
+    upto = jnp.where(rows_of(shape) <= lanes_of(shape), 1.0, 0.0).astype(BF16)
+    return dot_nn(low, upto) + dot_nn(middle, upto) + dot_nn(high, upto)
 
 
 def columns(rows):
@@ -146,47 +166,49 @@
     return jnp.where(keep, jnp.exp(jnp.where(keep, spread_by, 0.0)), 0.0)
 
 
-def turn_and_scale(left_ref, scale, g):
-    turned = left_ref[:, 384 * g : 384 * g + 384].astype(F32).T
-    return [
-        jnp.concatenate(two(turned[96 * j : 96 * j + 96, :] * scale[4 * g + j : 4 * g + j + 1, :]), axis=0)
-        for j in range(4)
-    ]
-
-
-def outer_states(left, right, out_ref):
-    for g in range(4):
+def outer_states(half, left_ref, scale, right_ref, out_ref):
+    for i in range(2):
+        g = 2 * half + i
+        turned = left_ref[:, at_lanes(384 * g, 0, 384)].astype(F32).T
         for j in range(4):
-            h = 4 * g + j
-            both = dot_nn(left(h), head_tiles(right, g, j, True))
+            h = 4 * i + j
+            left = jnp.concatenate(two(turned[96 * j : 96 * j + 96, :] * scale[h : h + 1, :]), axis=0)
+            both = dot_nn(left, head_tiles(right_ref, g, j, True))
             square = merge(both[:96] + both[96:])
-            for i, piece in enumerate(pack(square, j)):
-                out_ref[PACK * h + 24 * i : PACK * h + 24 * i + 24, :] = piece
-
-
-def state_kernel(kv_ref, logs_ref, x_ref):
-    accum = running(logs_ref[...])
-    last = accum[:, LANES - 1 :]
-    tail = jnp.exp(last - accum)
-    turned = [both for g in range(4) for both in turn_and_scale(kv_ref[:TOKENS], tail, g)]
-    outer_states(lambda h: turned[h], kv_ref[TOKENS:], x_ref)
-    x_ref[ROWS : ROWS + LOCAL_HEADS, :] = jnp.broadcast_to(jnp.exp(last), (LOCAL_HEADS, LANES))
-
-
-def combine_forward_kernel(core_ref, own_ref, got_ref, out_ref, own_decay_ref, got_decay_ref):
-    core = core_ref[0]
-    own_decay_ref[...] = own_ref[ROWS : ROWS + LOCAL_HEADS, :]
-    got_decay_ref[...] = got_ref[ROWS : ROWS + LOCAL_HEADS, :]
-    first = core == 0
-    at = pl.multiple_of(ROWS + HALF * core, 8)
-    own_decay = own_ref[pl.ds(at, HALF), :]
-    got_decay = got_ref[pl.ds(at, HALF), :]
+            for n, piece in enumerate(pack(square, j)):
+                out_ref[PACK * h + 24 * n : PACK * h + 24 * n + 24, :] = piece
+
+
+def half_rows(ref, half):
+    return ref[pl.ds(pl.multiple_of(HALF * half, HALF), HALF), :]
+
+
+def state_half(half, kv_ref, accum_ref, out_ref):
+    accum = half_rows(accum_ref, half)
+    last = jnp.broadcast_to(accum[:, LANES - 1 :], (HALF, LANES))
+    out_ref[HALF_ROWS : HALF_ROWS + HALF, :] = jnp.exp(last)
+    keys, values = kv_ref.at[pl.ds(0, TOKENS)], kv_ref.at[pl.ds(TOKENS, TOKENS)]
+    outer_states(half, keys, jnp.exp(last - accum), values, out_ref)
+
+
+def state_send_kernel(core_ref, kv_ref, logs_ref, out_ref, accum_ref):
+    accum_ref[...] = running(logs_ref[...])
+    state_half(1 - core_ref[0], kv_ref, accum_ref, out_ref)
+
+
+def state_keep_kernel(core_ref, kv_ref, accum_ref, out_ref):
+    state_half(core_ref[0], kv_ref, accum_ref, out_ref)
+
+
+def combine_forward_kernel(core_ref, own_ref, got_ref, out_ref):
+    first = core_ref[0] == 0
+    own_decay = own_ref[HALF_ROWS : HALF_ROWS + HALF, :]
+    got_decay = got_ref[HALF_ROWS : HALF_ROWS + HALF, :]
     late_decay = jnp.where(first, got_decay, own_decay)
     both_decay = own_decay * got_decay
     for h in range(HALF):
-        at = pl.multiple_of(HALF_ROWS * core + PACK * h, 8)
-        own = own_ref[pl.ds(at, PACK), :]
-        got = got_ref[pl.ds(at, PACK), :]
+        own = own_ref[PACK * h : PACK * h + PACK, :]
+        got = got_ref[PACK * h : PACK * h + PACK, :]
         early = jnp.where(first, own, got)
         late = jnp.where(first, got, own)
         total = early * late_decay[h : h + 1, :] + late
@@ -196,15 +218,13 @@
             out_ref[to + PART : to + FWD_PART, :] = jnp.broadcast_to(both_decay[h : h + 1, :], (2, LANES))
 
 
-def combine_backward_kernel(core_ref, own_ref, got_ref, own_decay_ref, got_decay_ref, out_ref):
-    core = core_ref[0]
-    first = core == 0
-    at = pl.multiple_of(HALF * core, 8)
-    early_decay = jnp.where(first, own_decay_ref[pl.ds(at, HALF), :], got_decay_ref[pl.ds(at, HALF), :])
+def combine_backward_kernel(core_ref, own_ref, got_ref, own_x_ref, got_x_ref, out_ref):
+    first = core_ref[0] == 0
+    at = slice(HALF_ROWS, HALF_ROWS + HALF)
+    early_decay = jnp.where(first, own_x_ref[at, :], got_x_ref[at, :])
     for h in range(HALF):
-        at = pl.multiple_of(HALF_ROWS * core + PACK * h, 8)
-        own = own_ref[pl.ds(at, PACK), :]
-        got = got_ref[pl.ds(at, PACK), :]
+        own = own_ref[PACK * h : PACK * h + PACK, :]
+        got = got_ref[PACK * h : PACK * h + PACK, :]
         early = jnp.where(first, own, got)
         late = jnp.where(first, got, own)
         out_ref[PACK * h : PACK * h + PACK, :] = late * early_decay[h : h + 1, :] + early
@@ -233,14 +253,32 @@
         state = state * decay_ref[c : c + 1, :] + in_ref[at : at + PART, :]
 
 
-def finish_states(g, mine, other, add_ref, decay, own_ref, got_ref, out_ref):
+def step_kernel(core_ref, stepping, state_ref, add_ref, decay_ref, out_ref):
+    steps = core_ref[0] == stepping
+    for h in range(HALF):
+        at = slice(PACK * h, PACK * h + PACK)
+        state = state_ref[at, :]
+        stepped = state * decay_ref[HALF_ROWS + h : HALF_ROWS + h + 1, :] + add_ref[at, :]
+        out_ref[at, :] = jnp.where(steps, stepped, state)
+
+
+def step_forward_kernel(core_ref, state_ref, x_ref, out_ref):
+    step_kernel(core_ref, 0, state_ref, x_ref, x_ref, out_ref)
+
+
+def step_backward_kernel(core_ref, state_ref, c_ref, x_ref, out_ref):
+    step_kernel(core_ref, 1, state_ref, c_ref, x_ref, out_ref)
+
+
+def finish_states(g, core, late, own_ref, got_ref, add_ref, decay_ref, out_ref):
+    half = g // 2
     for h in range(4 * g, 4 * g + 4):
-        at = PACK * (h % HALF)
-        own = own_ref[at : at + PACK, :]
-        got = got_ref[at : at + PACK, :]
-        state = jnp.where(mine, own, got) if h < HALF else jnp.where(mine, got, own)
-        stepped = state * decay[h : h + 1, :] + add_ref[PACK * h : PACK * h + PACK, :]
-        out_ref[PACK * h : PACK * h + PACK, :] = jnp.where(other, stepped, state)
+        i = h % HALF
+        own = own_ref[PACK * i : PACK * i + PACK, :]
+        got = got_ref[PACK * i : PACK * i + PACK, :]
+        if half == late:
+            own = own * decay_ref[HALF_ROWS + i : HALF_ROWS + i + 1, :] + add_ref[PACK * i : PACK * i + PACK, :]
+        out_ref[PACK * h : PACK * h + PACK, :] = jnp.where(core == half, own, got)
 
 
 def add_tiles(tiles, part, j):
@@ -250,9 +288,11 @@
         tiles[t] = piece if tiles[t] is None else tiles[t] + piece
 
 
-def inner_kernel(q_ref, k_ref, v_ref, logs_ref, inner_ref):
-    accum = running(logs_ref[...])
+def inner_kernel(q_ref, k_ref, v_ref, accum_ref, inner_ref, start_ref, tail_ref):
+    accum = accum_ref[...]
     cols = columns(accum)
+    start_ref[...] = jnp.exp(cols)
+    tail_ref[...] = columns(jnp.exp(accum[:, LANES - 1 :] - accum))
     for g in range(4):
         tiles = [None] * 3
         for j in range(4):
@@ -265,19 +305,18 @@
 
 
 def attention_kernel(
-    core_ref, q_ref, y_ref, gain_ref, logs_ref, inner_ref, own_ref, got_ref, got_state_ref, o_ref, state_ref, sums_ref
+    core_ref, q_ref, y_ref, gain_ref, start_ref, inner_ref, own_ref, got_ref, got_x_ref,
+    o_ref, state_ref, sums_ref,
 ):
     core = core_ref[0]
-    decay = got_state_ref[ROWS : ROWS + LOCAL_HEADS, :]
-    start = jnp.exp(columns(running(logs_ref[...])))
+    start = start_ref[...]
     squares = jnp.zeros((TOKENS, LANES), F32)
     crossed = jnp.zeros((TOKENS, LANES), F32)
     for g in range(4):
-        finish_states(g, core == 0, core == 1, got_state_ref, decay, own_ref, got_ref, state_ref)
-        high, low = block_diagonal(state_ref, g)
+        finish_states(g, core, 1, own_ref, got_ref, got_x_ref, got_x_ref, state_ref)
+        pairs = [pair_states(state_ref, g, p) for p in range(2)]
         at = slice(384 * g, 384 * g + 384)
-        q = q_ref[:, at]
-        attention = inner_ref[:, at] + group_columns(start, g) * (dot_nn(q, high) + dot_nn(q, low))
+        attention = inner_ref[:, at] + group_columns(start, g) * times_states(q_ref[:, at], pairs, dot_nn)
         o_ref[:, at] = attention
         scaled = gain_ref[:, at] * y_ref[:, at].astype(F32)
         both = scaled * attention
@@ -289,8 +328,9 @@
     sums_ref[1:2, :] = jnp.sum(crossed.T, axis=0, keepdims=True)
 
 
-def norm_kernel(q_ref, y_ref, gain_ref, logs_ref, o_ref, sums_0, sums_1, sums_2, sums_3, back_ref, c_ref):
-    accum = running(logs_ref[...])
+def norm_kernel(
+    core_ref, q_ref, y_ref, gain_ref, accum_ref, o_ref, sums_0, sums_1, sums_2, sums_3, back_ref, c_ref
+):
     sums = (sums_0[...] + sums_1[...]) + (sums_2[...] + sums_3[...])
     root = jnp.sqrt(sums[0:1, :] / (HEADS * HEAD_DIM) + 1e-05)
     factor = sums[1:2, :] / (HEADS * HEAD_DIM * root * root * root)
@@ -301,21 +341,24 @@
         at = slice(384 * g, 384 * g + 384)
         scaled = gain_ref[:, at] * y_ref[:, at].astype(F32)
         back_ref[:, at] = (scaled * inverse - o_ref[:, at] * factor).astype(BF16)
-    scale = jnp.exp(accum)
-    turned = [both for g in range(4) for both in turn_and_scale(q_ref, scale, g)]
-    outer_states(lambda h: turned[h], back_ref, c_ref)
-
-
-def middle_kernel(q_ref, k_ref, v_ref, back_ref, logs_ref, state_ref, gq_ref, gk_ref, done_ref):
-    accum = running(logs_ref[...])
+    half = 1 - core_ref[0]
+    outer_states(half, q_ref, jnp.exp(half_rows(accum_ref, half)), back_ref, c_ref)
+
+
+def carry_keep_kernel(core_ref, q_ref, back_ref, accum_ref, c_ref):
+    half = core_ref[0]
+    outer_states(half, q_ref, jnp.exp(half_rows(accum_ref, half)), back_ref, c_ref)
+
+
+def middle_kernel(q_ref, k_ref, v_ref, back_ref, accum_ref, state_ref, gq_ref, gk_ref, done_ref):
+    accum = accum_ref[...]
     done_ref[...] = accum[:8]
     cols = columns(accum)
     start = jnp.exp(cols)
     for g in range(4):
-        high, low = block_diagonal(state_ref, g)
+        pairs = [pair_states(state_ref, g, p) for p in range(2)]
         at = slice(384 * g, 384 * g + 384)
-        back = back_ref[:, at]
-        gq = group_columns(start, g) * (dot_nt(back, high) + dot_nt(back, low))
+        gq = group_columns(start, g) * times_states(back_ref[:, at], pairs, dot_nt)
         gq = [gq[:, LANES * t : LANES * t + LANES] for t in range(3)]
         gk = [None] * 3
         for j in range(4):
@@ -334,8 +377,8 @@
             gk_ref[:, lane] = gk[t]
 
 
-def values_kernel(q_ref, k_ref, back_ref, logs_ref, gv_ref):
-    accum = running(logs_ref[...])
+def values_kernel(q_ref, k_ref, back_ref, accum_ref, gv_ref):
+    accum = accum_ref[...]
     cols = columns(accum)
     for g in range(4):
         gv = [None] * 3
@@ -349,23 +392,19 @@
 
 
 def last_kernel(
-    core_ref, k_ref, v_ref, logs_ref, gk0_ref, gv0_ref, own_ref, got_ref, got_c_ref, got_decay_ref,
+    core_ref, k_ref, v_ref, tail_ref, gk0_ref, gv0_ref, own_ref, got_ref, got_c_ref, got_x_ref,
     gk_hbm, gv_hbm, carry_ref, gk_ref, gv_ref, sems,
 ):
     core = core_ref[0]
-    decay = got_decay_ref[...]
-    accum = running(logs_ref[...])
-    tail = columns(jnp.exp(accum[:, LANES - 1 :] - accum))
+    tail = tail_ref[...]
     copies = []
     for g in range(4):
-        finish_states(g, core == 0, core == 0, got_c_ref, decay, own_ref, got_ref, carry_ref)
-        high, low = block_diagonal(carry_ref, g)
+        finish_states(g, core, 0, own_ref, got_ref, got_c_ref, got_x_ref, carry_ref)
+        pairs = [pair_states(carry_ref, g, p) for p in range(2)]
         at = slice(384 * g, 384 * g + 384)
-        k = k_ref[:, at]
-        v = v_ref[:, at]
         wide = group_columns(tail, g)
-        gk_ref[:, at] = (gk0_ref[:, at] + wide * (dot_nt(v, high) + dot_nt(v, low))).astype(BF16)
-        gv_ref[:, at] = (gv0_ref[:, at] + wide * (dot_nn(k, high) + dot_nn(k, low))).astype(BF16)
+        gk_ref[:, at] = (gk0_ref[:, at] + wide * times_states(v_ref[:, at], pairs, dot_nt)).astype(BF16)
+        gv_ref[:, at] = (gv0_ref[:, at] + wide * times_states(k_ref[:, at], pairs, dot_nn)).astype(BF16)
         for i, (src, dst) in enumerate(((gk_ref, gk_hbm), (gv_ref, gv_hbm))):
             copy = pltpu.make_async_copy(src.at[:, at], dst.at[:, at], sems.at[2 * g + i])
             copy.start()
@@ -416,46 +455,51 @@
     gain = gain.reshape(1, WIDTH)
     wide = (TOKENS, WIDTH)
     narrow = pltpu.VMEM(wide, BF16)
-    decay = ((LOCAL_HEADS, LANES), F32)
-    x = call(state_kernel, [((ROWS + LOCAL_HEADS, LANES), F32)], 0, jnp.concatenate([k, v]), logs, flops=10**9)
-    got_x = swap(x)
-    payload, own_decay, got_decay = call(
-        combine_forward_kernel, [((CHIPS * FWD_PART, LANES), F32), decay, decay], 1, core, x, got_x
-    )
+    half = ((HALF_ROWS, LANES), F32)
+    half_decay = ((HALF_ROWS + HALF, LANES), F32)
+    rows = ((LOCAL_HEADS, LANES), F32)
+    cols = ((TOKENS, LANES), F32)
+    kv = jnp.concatenate([k, v])
+    kv, logs = lax.optimization_barrier((kv, logs))
+    x_send, accum = call(state_send_kernel, [half_decay, rows], 1, core, kv, logs, flops=10**9)
+    got_x = swap(x_send)
+    x_keep = call(state_keep_kernel, [half_decay], 1, core, kv, accum, flops=10**9)
+    payload = call(combine_forward_kernel, [((CHIPS * FWD_PART, LANES), F32)], 1, core, x_keep, got_x)
     payload = exchange(payload)
-    token = ((8, LANES), F32)
-    inner = call(inner_kernel, [(wide, F32)], 0, q, k, v, logs, flops=2 * 10**9)
-    entering, decays = call(scan_forward_kernel, [((HALF_ROWS, LANES), F32), ((CHIPS, LANES), F32)], 0, payload)
+    inner, start, tail = call(inner_kernel, [(wide, F32), cols, cols], 0, q, k, v, accum, flops=2 * 10**9)
+    entering, decays = call(scan_forward_kernel, [half, ((CHIPS, LANES), F32)], 0, payload)
     entering = exchange(entering)
-    got_entering = swap(entering)
+    got_entering = swap(call(step_forward_kernel, [half], 1, core, entering, x_keep))
     attention, state, sums = call(
         attention_kernel,
         [(wide, F32), ((ROWS, LANES), F32), ((2, LANES), F32)],
-        1, core, q, y, gain, logs, inner, entering, got_entering, got_x,
+        1, core, q, y, gain, start, inner, entering, got_entering, got_x,
         flops=10**9,
     )
-    back, c = call(
+    back, c_send = call(
         norm_kernel,
-        [(wide, BF16), ((ROWS, LANES), F32)],
-        0, q, y, gain, logs, attention, sums, *others(sums),
+        [(wide, BF16), half],
+        1, core, q, y, gain, accum, attention, sums, *others(sums),
         flops=10**9,
     )
-    got_c = swap(c)
-    payload = call(
-        combine_backward_kernel, [((HALF_ROWS, LANES), F32)], 1, core, c, got_c, own_decay, got_decay
-    )
+    got_c = swap(c_send)
+    c_keep = call(carry_keep_kernel, [half], 1, core, q, back, accum, flops=10**9)
+    payload = call(combine_backward_kernel, [half], 1, core, c_keep, got_c, x_keep, got_x)
     payload = exchange(payload)
     gq, gk0, middle_done = call(
-        middle_kernel, [(wide, BF16), (wide, F32), token], 0, q, k, v, back, logs, state, flops=4 * 10**9
-    )
-    leaving = call(scan_backward_kernel, [((HALF_ROWS, LANES), F32)], 0, payload, decays, middle_done)
+        middle_kernel,
+        [(wide, BF16), (wide, F32), ((8, LANES), F32)],
+        0, q, k, v, back, accum, state,
+        flops=4 * 10**9,
+    )
+    leaving = call(scan_backward_kernel, [half], 0, payload, decays, middle_done)
     leaving = exchange(leaving)
-    got_leaving = swap(leaving)
-    gv0 = call(values_kernel, [(wide, F32)], 0, q, k, back, logs, flops=2 * 10**9)
+    got_leaving = swap(call(step_backward_kernel, [half], 1, core, leaving, c_keep, x_keep))
+    gv0 = call(values_kernel, [(wide, F32)], 0, q, k, back, accum, flops=2 * 10**9)
     gk, gv = call(
         last_kernel,
         [(wide, BF16), (wide, BF16)],
-        1, core, k, v, logs, gk0, gv0, leaving, got_leaving, got_c, got_decay,
+        1, core, k, v, tail, gk0, gv0, leaving, got_leaving, got_c, got_x,
         hbm_out=(0, 1),
         scratch=[pltpu.VMEM((ROWS, LANES), F32), narrow, narrow, pltpu.SemaphoreType.DMA((8,))],
         flops=2 * 10**9,

time: 104 us -> 100 us (0.962)
  Pallas kernels: 15.4 us -> 13 us
  waiting for transfers between devices: 12.4 us -> 10.2 us
    pallas_call x11 -> x15, Pallas kernels: 15.4 us -> 13 us  [call(): pl.pallas_call(kernel, out_shape=shapes, in_specs=specs, out_specs=[pl.Bl...]
    ppermute x4, waiting for transfers between devices: 3.28 us -> 1.49 us  [swap(): return lax.ppermute(value, 'core', SWAP)]
where the time goes in v3:
time: 100 us; the launch traced here: 99.9 us
  blocking collectives  52.1 us (52%)
  starting transfers between devices  20.5 us (20%)
  Pallas kernels  13 us (13%)
  waiting for transfers between devices  10.2 us (10%)
  local copies, waits for them, and re-layouts  1.94 us (2%)
  other arithmetic  1.17 us (1%)
  between operations  1.01 us (1%)
    all_to_all x3, blocking collectives, exchange(): lax.all_to_all(parts, CHIP_BITS[::-1], 0, 0, tiled=True)  52.1 us
    pallas_call x15, Pallas kernels, call(): pl.pallas_call(kernel, out_shape=shapes, in_specs=specs, out_specs=[pl.Bl...  13 us
    ppermute x4, starting transfers between devices, swap(): return lax.ppermute(value, 'core', SWAP)  11.9 us
    all_to_all x1, waiting for transfers between devices, exchange(): lax.all_to_all(parts, CHIP_BITS[::-1], 0, 0, tiled=True)  5.8 us
    all_to_all x1, starting transfers between devices, exchange(): lax.all_to_all(parts, CHIP_BITS[::-1], 0, 0, tiled=True)  4.81 us
    ppermute x3, starting transfers between devices, others(): lax.ppermute(value, 'head', [(i, (i + k) % 4) for i in range(4)])  3.85 us
    ppermute x3, waiting for transfers between devices, others(): lax.ppermute(value, 'head', [(i, (i + k) % 4) for i in range(4)])  2.94 us
  transfers between devices with their start and end apart: 8, of which 5 were waited for; matrix products, arithmetic and copies ran while one was open for 0% of the time, Pallas kernels for 8%

profile of v3, /device:TPU:1, one launch (start us, length us, event | category | flops | bytes accessed | tf_op | source)
XLA Modules:
  0.0 99.9 jit_solution(9598239554543304915)
XLA Ops:
  0.6 0.0 copy-start.4
  0.6 1.2 %pad_maximum_fusion.kv_ref = bf16[256,1536]{1,0:T(8,128)(2,1)S(1)} fusion(bf16[128,1536]{1,0:T(8,128)(2,1)} %v_ref.5, bf16[128,1536]{1,0:T(8,128)(2,1)} %k_ref.7), kind=kLoop, calls=%fused_computation | loop fusion | flops 1572864 | bytes 1572864 | tf_op jit(solution)/shard_map/concatenate | solution.py:462
  1.8 0.0 copy-done.4
  1.8 0.7 state_send_kernel.1
  2.5 3.3 %collective-permute-start = (f32[584,128]{1,0:T(8,128)S(1)}, f32[584,128]{1,0:T(8,128)S(1)}, u32[]{:S(2)}, u32[]{:S(2)}) collective-permute-start(f32[584,128]{1,0:T(8,128)S(1)} %get-tuple-element.27), channel_id=1, source_target_pairs={{0,4},{4,0},{1,5},{5,1},{2,6},{6,2},{3,7},{7,3},{8,12},{12,8},{9,1... | collective-permute-start | bytes 897032 | tf_op jit(solution)/shard_map/ppermute | solution.py:441
  5.8 0.5 state_keep_kernel.1.own_ref.x_ref.own_x_ref
  6.3 0.8 collective-permute-done.got_ref.got_x_ref
  7.0 0.1 combine_forward_kernel.1
  7.1 21.3 %all_to_all.20 = f32[32,10,2,128]{3,2,1,0:T(2,128)S(1)} all-to-all(f32[32,10,2,128]{3,2,1,0:T(2,128)S(1)} %bitcast.9), channel_id=1, replica_groups=mesh['xh'=2,'xl'=2,'zh'=2,'zm'=2,'zl'=2,'core'=2,'head'=4] {'zl','zm','z..., dimensions={0} | all-to-all | bytes 655360 | tf_op jit(solution)/shard_map/all_to_all | solution.py:446
  28.4 0.1 scan_forward_kernel.1
  28.5 0.0 copy-start.10
  28.5 0.0 copy-start
  28.5 0.0 copy-start.1
  28.5 0.0 copy-start.3
  28.5 15.5 %all_to_all.21 = f32[32,9,2,128]{3,2,1,0:T(2,128)S(1)} all-to-all(f32[32,9,2,128]{3,2,1,0:T(2,128)S(1)} %bitcast.17), channel_id=1, replica_groups=mesh['xh'=2,'xl'=2,'zh'=2,'zm'=2,'zl'=2,'core'=2,'head'=4] {'zl','zm','z..., dimensions={0} | all-to-all | bytes 589824 | tf_op jit(solution)/shard_map/all_to_all | solution.py:446
  44.1 3.3 %collective-permute-start.1 = (f32[576,128]{1,0:T(8,128)S(1)}, f32[576,128]{1,0:T(8,128)S(1)}, u32[]{:S(2)}, u32[]{:S(2)}) collective-permute-start(f32[576,128]{1,0:T(8,128)S(1)} %step_forward_kernel.1), channel_id=1, source_target_pairs={{0,4},{4,0},{1,5},{5,1},{2,6},{6,2},{3,7},{7,3},{8,12},{12,8},{9,1... | collective-permute-start | bytes 884744 | tf_op jit(solution)/shard_map/ppermute | solution.py:441
  47.5 0.0 copy-start.2
  47.5 1.5 %inner_kernel.1 = (f32[128,1536]{1,0:T(8,128)S(1)}, f32[128,128]{1,0:T(8,128)S(1)}, f32[128,128]{1,0:T(8,128)S(1)}) custom-call(bf16[128,1536]{1,0:T(8,128)(2,1)S(1)} %copy-done.3, bf16[128,1536]{1,0:T(8,128)(2,1)S(1)} %copy-done, bf16[128,1536]{1,0:T(8,128)(2,1)S(1)} %copy-done.1, f32[16,128]{1,0:T(8,128)S(1)} %get-tuple-element.24.accum_ref), custom_call_target="tpu_custom_call" | custom-call | flops 2000000000 | bytes 2105344 | tf_op jit(solution)/shard_map/inner_kernel/pallas_call | solution.py:423
  49.0 0.0 collective-permute-done.1.got_ref
  49.0 0.0 copy-done.2
  49.0 0.9 attention_kernel.1
  49.9 2.8 %collective-permute-start.4 = (f32[2,128]{1,0:T(2,128)S(1)}, f32[2,128]{1,0:T(2,128)S(1)}, u32[]{:S(2)}, u32[]{:S(2)}) collective-permute-start(f32[2,128]{1,0:T(2,128)S(1)} %get-tuple-element.30.sums_0), channel_id=1, source_target_pairs={{0,3},{1,0},{2,1},{3,2},{4,7},{5,4},{6,5},{7,6},{8,11},{9,8},{10,9... | collective-permute-start | bytes 3080 | tf_op jit(solution)/shard_map/ppermute | solution.py:450
  52.7 0.4 collective-permute-start.3
  53.1 0.7 collective-permute-start.2
  53.8 0.0 collective-permute-done.4.sums_3
  53.8 2.9 %collective-permute-done.3.sums_2 = f32[2,128]{1,0:T(2,128)S(1)} collective-permute-done((f32[2,128]{1,0:T(2,128)S(1)}, f32[2,128]{1,0:T(2,128)S(1)}, u32[]{:S(2)}, u32[]{:S(2)}) %collective-permute-start.3) | collective-permute-done | bytes 1056 | tf_op jit(solution)/shard_map/ppermute | solution.py:450
  56.7 0.1 collective-permute-done.2.sums_1
  56.7 0.7 norm_kernel.1
  57.4 0.0 copy-start.5
  57.5 1.8 %collective-permute-start.5 = (f32[576,128]{1,0:T(8,128)S(1)}, f32[576,128]{1,0:T(8,128)S(1)}, u32[]{:S(2)}, u32[]{:S(2)}) collective-permute-start(f32[576,128]{1,0:T(8,128)S(1)} %get-tuple-element.36), channel_id=1, source_target_pairs={{0,4},{4,0},{1,5},{5,1},{2,6},{6,2},{3,7},{7,3},{8,12},{12,8},{9,1... | collective-permute-start | bytes 884744 | tf_op jit(solution)/shard_map/ppermute | solution.py:441
  59.3 0.5 carry_keep_kernel.1.own_ref.c_ref
  59.8 0.7 collective-permute-done.5.got_ref.got_c_ref
  60.5 0.8 combine_backward_kernel.1
  61.2 4.8 %all-to-all-start.2 = ((f32[32,9,2,128]{3,2,1,0:T(2,128)}), f32[32,9,2,128]{3,2,1,0:T(2,128)S(1)}, u32[]{:S(2)}, u32[]{:S(2)}) async-start(f32[32,9,2,128]{3,2,1,0:T(2,128)} %bitcast.5), calls=%async_computation.2 | async-start | bytes 589824 | tf_op jit(solution)/shard_map/all_to_all | solution.py:446
  66.1 0.0 copy-start.6
  66.1 1.0 copy-done.6
  67.1 3.8 %middle_kernel.1 = (bf16[128,1536]{1,0:T(8,128)(2,1)}, f32[128,1536]{1,0:T(8,128)S(1)}, f32[8,128]{1,0:T(8,128)S(1)}) custom-call(bf16[128,1536]{1,0:T(8,128)(2,1)S(1)} %copy-done.3, bf16[128,1536]{1,0:T(8,128)(2,1)S(1)} %copy-done, bf16[128,1536]{1,0:T(8,128)(2,1)S(1)} %copy-done.1, bf16[128,1536]{1,0:T(8,128)(2,1)S(1)} %copy-done.6, ...), custom_call_target="tpu_custom_call" | custom-call | flops 4000000000 | bytes 3354624 | tf_op jit(solution)/shard_map/middle_kernel/pallas_call | solution.py:423
  70.9 0.9 copy-done.8
  71.8 5.8 %all-to-all-done.2 = f32[32,9,2,128]{3,2,1,0:T(2,128)S(1)} async-done(((f32[32,9,2,128]{3,2,1,0:T(2,128)}), f32[32,9,2,128]{3,2,1,0:T(2,128)S(1)}, u32[]{:S(2)}, u32[]{:S(2)}) %all-to-all-start.2) | async-done | bytes 294944 | tf_op jit(solution)/shard_map/all_to_all | solution.py:446
  77.6 0.1 scan_backward_kernel.1
  77.6 0.0 copy-start.7
  77.7 15.2 %all_to_all.22 = f32[32,9,2,128]{3,2,1,0:T(2,128)S(1)} all-to-all(f32[32,9,2,128]{3,2,1,0:T(2,128)S(1)} %bitcast.14), channel_id=1, replica_groups=mesh['xh'=2,'xl'=2,'zh'=2,'zm'=2,'zl'=2,'core'=2,'head'=4] {'zl','zm','z..., dimensions={0} | all-to-all | bytes 589824 | tf_op jit(solution)/shard_map/all_to_all | solution.py:446
  92.9 0.0 copy-start.9
  92.9 3.4 %collective-permute-start.6 = (f32[576,128]{1,0:T(8,128)S(1)}, f32[576,128]{1,0:T(8,128)S(1)}, u32[]{:S(2)}, u32[]{:S(2)}) collective-permute-start(f32[576,128]{1,0:T(8,128)S(1)} %step_backward_kernel.1), channel_id=1, source_target_pairs={{0,4},{4,0},{1,5},{5,1},{2,6},{6,2},{3,7},{7,3},{8,12},{12,8},{9,1... | collective-permute-start | bytes 884744 | tf_op jit(solution)/shard_map/ppermute | solution.py:441
  96.3 1.5 %values_kernel.1.gv0_ref = f32[128,1536]{1,0:T(8,128)S(1)} custom-call(bf16[128,1536]{1,0:T(8,128)(2,1)S(1)} %copy-done.3, bf16[128,1536]{1,0:T(8,128)(2,1)S(1)} %copy-done, bf16[128,1536]{1,0:T(8,128)(2,1)S(1)} %copy-done.7, f32[16,128]{1,0:T(8,128)S(1)} %get-tuple-element.24.accum_ref), custom_call_target="tpu_custom_call" | custom-call | flops 2000000000 | bytes 1974272 | tf_op jit(solution)/shard_map/values_kernel/pallas_call | solution.py:423
  97.9 0.0 collective-permute-done.6.got_ref
  97.9 0.0 copy-done.9
  97.9 1.9 %last_kernel.1 = (bf16[128,1536]{1,0:T(8,128)(2,1)}, bf16[128,1536]{1,0:T(8,128)(2,1)}) custom-call(s32[1]{0:T(128)} %bitcast.core_ref, bf16[128,1536]{1,0:T(8,128)(2,1)S(1)} %copy-done, bf16[128,1536]{1,0:T(8,128)(2,1)S(1)} %copy-done.1, f32[128,128]{1,0:T(8,128)S(1)} %get-tuple-element.34.tail_ref, f32[128,1536]{1,0:T(8,128)S(1)} %copy-done.9, ...), custom_call_target="tpu_custom_call" | custom-call | flops 2000000000 | bytes 4395012 | tf_op jit(solution)/shard_map/last_kernel/pallas_call | solution.py:423
  (10 shorter events, 0.1 us)
Async XLA Ops:
  0.6 1.2 %copy-start.4 = (f32[16,128]{1,0:T(8,128)S(1)}, f32[16,128]{1,0:T(8,128)}, u32[]{:S(2)}) copy-start(f32[16,128]{1,0:T(8,128)} %logs_ref) | copy-start | bytes 24580
  2.5 4.5 %collective-permute-start = (f32[584,128]{1,0:T(8,128)S(1)}, f32[584,128]{1,0:T(8,128)S(1)}, u32[]{:S(2)}, u32[]{:S(2)}) collective-permute-start(f32[584,128]{1,0:T(8,128)S(1)} %get-tuple-element.27), channel_id=1, source_target_pairs={{0,4},{4,0},{1,5},{5,1},{2,6},{6,2},{3,7},{7,3},{8,12},{12,8},{9,1... | collective-permute-start | bytes 897032 | tf_op jit(solution)/shard_map/ppermute | solution.py:441
  28.5 18.9 %copy-start.10 = (f32[1536]{0:T(1024)S(1)}, f32[1536]{0:T(1024)}, u32[]{:S(2)}) copy-start(f32[1536]{0:T(1024)} %param.11) | copy-start | bytes 18436
  28.5 18.9 %copy-start = (bf16[128,1536]{1,0:T(8,128)(2,1)S(1)}, bf16[128,1536]{1,0:T(8,128)(2,1)}, u32[]{:S(2)}) copy-start(bf16[128,1536]{1,0:T(8,128)(2,1)} %k_ref.7) | copy-start | bytes 1179652
  28.5 18.9 %copy-start.1 = (bf16[128,1536]{1,0:T(8,128)(2,1)S(1)}, bf16[128,1536]{1,0:T(8,128)(2,1)}, u32[]{:S(2)}) copy-start(bf16[128,1536]{1,0:T(8,128)(2,1)} %v_ref.5) | copy-start | bytes 1179652
  28.5 18.9 %copy-start.3 = (bf16[128,1536]{1,0:T(8,128)(2,1)S(1)}, bf16[128,1536]{1,0:T(8,128)(2,1)}, u32[]{:S(2)}) copy-start(bf16[128,1536]{1,0:T(8,128)(2,1)} %q_ref.11) | copy-start | bytes 1179652
  44.1 4.9 %collective-permute-start.1 = (f32[576,128]{1,0:T(8,128)S(1)}, f32[576,128]{1,0:T(8,128)S(1)}, u32[]{:S(2)}, u32[]{:S(2)}) collective-permute-start(f32[576,128]{1,0:T(8,128)S(1)} %step_forward_kernel.1), channel_id=1, source_target_pairs={{0,4},{4,0},{1,5},{5,1},{2,6},{6,2},{3,7},{7,3},{8,12},{12,8},{9,1... | collective-permute-start | bytes 884744 | tf_op jit(solution)/shard_map/ppermute | solution.py:441
  47.5 1.6 %copy-start.2 = (bf16[128,1536]{1,0:T(8,128)(2,1)S(1)}, bf16[128,1536]{1,0:T(8,128)(2,1)}, u32[]{:S(2)}) copy-start(bf16[128,1536]{1,0:T(8,128)(2,1)} %y_ref.3) | copy-start | bytes 1179652
  49.9 3.9 %collective-permute-start.4 = (f32[2,128]{1,0:T(2,128)S(1)}, f32[2,128]{1,0:T(2,128)S(1)}, u32[]{:S(2)}, u32[]{:S(2)}) collective-permute-start(f32[2,128]{1,0:T(2,128)S(1)} %get-tuple-element.30.sums_0), channel_id=1, source_target_pairs={{0,3},{1,0},{2,1},{3,2},{4,7},{5,4},{6,5},{7,6},{8,11},{9,8},{10,9... | collective-permute-start | bytes 3080 | tf_op jit(solution)/shard_map/ppermute | solution.py:450
  52.7 3.9 %collective-permute-start.3 = (f32[2,128]{1,0:T(2,128)S(1)}, f32[2,128]{1,0:T(2,128)S(1)}, u32[]{:S(2)}, u32[]{:S(2)}) collective-permute-start(f32[2,128]{1,0:T(2,128)S(1)} %get-tuple-element.30.sums_0), channel_id=1, source_target_pairs={{0,2},{1,3},{2,0},{3,1},{4,6},{5,7},{6,4},{7,5},{8,10},{9,11},{10,... | collective-permute-start | bytes 3080 | tf_op jit(solution)/shard_map/ppermute | solution.py:450
  53.1 3.6 %collective-permute-start.2 = (f32[2,128]{1,0:T(2,128)S(1)}, f32[2,128]{1,0:T(2,128)S(1)}, u32[]{:S(2)}, u32[]{:S(2)}) collective-permute-start(f32[2,128]{1,0:T(2,128)S(1)} %get-tuple-element.30.sums_0), channel_id=1, source_target_pairs={{0,1},{1,2},{2,3},{3,0},{4,5},{5,6},{6,7},{7,4},{8,9},{9,10},{10,1... | collective-permute-start | bytes 3080 | tf_op jit(solution)/shard_map/ppermute | solution.py:450
  57.4 2.3 %copy-start.5 = (bf16[128,1536]{1,0:T(8,128)(2,1)}, bf16[128,1536]{1,0:T(8,128)(2,1)S(1)}, u32[]{:S(2)}) copy-start(bf16[128,1536]{1,0:T(8,128)(2,1)S(1)} %get-tuple-element.31.back_ref) | copy-start | bytes 1179652
  57.5 3.0 %collective-permute-start.5 = (f32[576,128]{1,0:T(8,128)S(1)}, f32[576,128]{1,0:T(8,128)S(1)}, u32[]{:S(2)}, u32[]{:S(2)}) collective-permute-start(f32[576,128]{1,0:T(8,128)S(1)} %get-tuple-element.36), channel_id=1, source_target_pairs={{0,4},{4,0},{1,5},{5,1},{2,6},{6,2},{3,7},{7,3},{8,12},{12,8},{9,1... | collective-permute-start | bytes 884744 | tf_op jit(solution)/shard_map/ppermute | solution.py:441
  61.2 16.3 %all-to-all-start.2 = ((f32[32,9,2,128]{3,2,1,0:T(2,128)}), f32[32,9,2,128]{3,2,1,0:T(2,128)S(1)}, u32[]{:S(2)}, u32[]{:S(2)}) async-start(f32[32,9,2,128]{3,2,1,0:T(2,128)} %bitcast.5), calls=%async_computation.2 | async-start | bytes 589824 | tf_op jit(solution)/shard_map/all_to_all | solution.py:446
  66.1 1.0 copy-start.6
  70.9 0.9 copy-start.8
  77.6 18.7 %copy-start.7 = (bf16[128,1536]{1,0:T(8,128)(2,1)S(1)}, bf16[128,1536]{1,0:T(8,128)(2,1)}, u32[]{:S(2)}) copy-start(bf16[128,1536]{1,0:T(8,128)(2,1)} %copy-done.5) | copy-start | bytes 1179652
  92.9 5.0 %copy-start.9 = (f32[128,1536]{1,0:T(8,128)S(1)}, f32[128,1536]{1,0:T(8,128)}, u32[]{:S(2)}) copy-start(f32[128,1536]{1,0:T(8,128)} %copy-done.8) | copy-start | bytes 2359300
  92.9 5.0 %collective-permute-start.6 = (f32[576,128]{1,0:T(8,128)S(1)}, f32[576,128]{1,0:T(8,128)S(1)}, u32[]{:S(2)}, u32[]{:S(2)}) collective-permute-start(f32[576,128]{1,0:T(8,128)S(1)} %step_backward_kernel.1), channel_id=1, source_target_pairs={{0,4},{4,0},{1,5},{5,1},{2,6},{6,2},{3,7},{7,3},{8,12},{12,8},{9,1... | collective-permute-start | bytes 884744 | tf_op jit(solution)/shard_map/ppermute | solution.py:441

commit v4 on v3

--- a/solution.py
+++ b/solution.py
@@ -15,7 +15,7 @@
 PACK = 72
 CHIPS = 32
 PART = 18
-FWD_PART = 20
+FWD_PART = 19
 ROWS = LOCAL_HEADS * PACK
 HALF_ROWS = HALF * PACK
 VMEM = 12 * 1024 * 1024
@@ -215,7 +215,7 @@
         for quarter in range(4):
             to = FWD_PART * (4 * h + quarter)
             out_ref[to : to + PART, :] = total[PART * quarter : PART * quarter + PART, :]
-            out_ref[to + PART : to + FWD_PART, :] = jnp.broadcast_to(both_decay[h : h + 1, :], (2, LANES))
+            out_ref[to + PART : to + FWD_PART, :] = both_decay[h : h + 1, :]
 
 
 def combine_backward_kernel(core_ref, own_ref, got_ref, own_x_ref, got_x_ref, out_ref):
@@ -230,14 +230,14 @@
         out_ref[PACK * h : PACK * h + PACK, :] = late * early_decay[h : h + 1, :] + early
 
 
-def turned_bits(c):
-    return sum(((c >> b) & 1) << (4 - b) for b in range(5))
+def place_of(c):
+    return sum(((c >> (4 - CHIP_BITS.index(name))) & 1) << (4 - i) for i, name in enumerate(EXCHANGE))
 
 
 def scan_forward_kernel(in_ref, out_ref, decay_ref):
     state = jnp.zeros((PART, LANES), F32)
     for c in range(CHIPS):
-        place = turned_bits(c)
+        place = place_of(c)
         out_ref[PART * place : PART * place + PART, :] = state
         at = FWD_PART * place
         decay = in_ref[at + PART : at + PART + 1, :]
@@ -245,10 +245,10 @@
         state = state * decay + in_ref[at : at + PART, :]
 
 
-def scan_backward_kernel(in_ref, decay_ref, after_ref, out_ref):
+def scan_backward_kernel(in_ref, decay_ref, after_ref, after_too_ref, out_ref):
     state = jnp.zeros((PART, LANES), F32)
     for c in reversed(range(CHIPS)):
-        at = PART * turned_bits(c)
+        at = PART * place_of(c)
         out_ref[at : at + PART, :] = state
         state = state * decay_ref[c : c + 1, :] + in_ref[at : at + PART, :]
 
@@ -270,15 +270,12 @@
     step_kernel(core_ref, 1, state_ref, c_ref, x_ref, out_ref)
 
 
-def finish_states(g, core, late, own_ref, got_ref, add_ref, decay_ref, out_ref):
-    half = g // 2
-    for h in range(4 * g, 4 * g + 4):
-        i = h % HALF
-        own = own_ref[PACK * i : PACK * i + PACK, :]
-        got = got_ref[PACK * i : PACK * i + PACK, :]
-        if half == late:
-            own = own * decay_ref[HALF_ROWS + i : HALF_ROWS + i + 1, :] + add_ref[PACK * i : PACK * i + PACK, :]
-        out_ref[PACK * h : PACK * h + PACK, :] = jnp.where(core == half, own, got)
+def own_states(core, late, own_ref, add_ref, decay_ref, out_ref):
+    for h in range(HALF):
+        at = slice(PACK * h, PACK * h + PACK)
+        own = own_ref[at, :]
+        stepped = own * decay_ref[HALF_ROWS + h : HALF_ROWS + h + 1, :] + add_ref[at, :]
+        out_ref[at, :] = jnp.where(core == late, stepped, own)
 
 
 def add_tiles(tiles, part, j):
@@ -288,48 +285,79 @@
         tiles[t] = piece if tiles[t] is None else tiles[t] + piece
 
 
-def inner_kernel(q_ref, k_ref, v_ref, accum_ref, inner_ref, start_ref, tail_ref):
-    accum = accum_ref[...]
+def keys_of(kv_ref):
+    return kv_ref.at[pl.ds(0, TOKENS)]
+
+
+def values_of(kv_ref):
+    return kv_ref.at[pl.ds(TOKENS, TOKENS)]
+
+
+def group_lanes(half, i):
+    return at_lanes(384 * (2 * half + i), 0, 384)
+
+
+def inner_half(half, q_ref, kv_ref, accum_ref, inner_ref, start_ref, tail_ref):
+    accum = half_rows(accum_ref, half)
     cols = columns(accum)
     start_ref[...] = jnp.exp(cols)
     tail_ref[...] = columns(jnp.exp(accum[:, LANES - 1 :] - accum))
-    for g in range(4):
+    k_ref, v_ref = keys_of(kv_ref), values_of(kv_ref)
+    for i in range(2):
+        g = 2 * half + i
         tiles = [None] * 3
         for j in range(4):
-            h = 4 * g + j
             scores = dot_nt(head_tiles(q_ref, g, j, True), head_tiles(k_ref, g, j, False))
-            weights = (scores * weight_of(accum, cols, h)).astype(BF16)
+            weights = (scores * weight_of(accum, cols, 4 * i + j)).astype(BF16)
             add_tiles(tiles, dot_nn(weights, head_tiles(v_ref, g, j, True)), j)
         for t in range(3):
-            inner_ref[:, 384 * g + LANES * t : 384 * g + LANES * t + LANES] = tiles[t]
-
-
-def attention_kernel(
-    core_ref, q_ref, y_ref, gain_ref, start_ref, inner_ref, own_ref, got_ref, got_x_ref,
-    o_ref, state_ref, sums_ref,
+            inner_ref[:, 384 * i + LANES * t : 384 * i + LANES * t + LANES] = tiles[t]
+
+
+def inner_kernel(
+    core_ref, q_ref, kv_ref, accum_ref,
+    own_inner_ref, own_start_ref, own_tail_ref, inner_ref, start_ref, tail_ref,
 ):
     core = core_ref[0]
+    inner_half(core, q_ref, kv_ref, accum_ref, own_inner_ref, own_start_ref, own_tail_ref)
+    inner_half(1 - core, q_ref, kv_ref, accum_ref, inner_ref, start_ref, tail_ref)
+
+
+def attention_half(half, q_ref, y_ref, gain_ref, start_ref, inner_ref, state_ref, o_ref, squares, crossed):
     start = start_ref[...]
-    squares = jnp.zeros((TOKENS, LANES), F32)
-    crossed = jnp.zeros((TOKENS, LANES), F32)
-    for g in range(4):
-        finish_states(g, core, 1, own_ref, got_ref, got_x_ref, got_x_ref, state_ref)
-        pairs = [pair_states(state_ref, g, p) for p in range(2)]
-        at = slice(384 * g, 384 * g + 384)
-        attention = inner_ref[:, at] + group_columns(start, g) * times_states(q_ref[:, at], pairs, dot_nn)
+    for i in range(2):
+        pairs = [pair_states(state_ref, i, p) for p in range(2)]
+        lanes = group_lanes(half, i)
+        at = slice(384 * i, 384 * i + 384)
+        attention = inner_ref[:, at] + group_columns(start, i) * times_states(q_ref[:, lanes], pairs, dot_nn)
         o_ref[:, at] = attention
-        scaled = gain_ref[:, at] * y_ref[:, at].astype(F32)
-        both = scaled * attention
+        both = gain_ref[:, lanes] * y_ref[:, lanes].astype(F32) * attention
         square = attention * attention
         for t in range(3):
             squares = squares + square[:, LANES * t : LANES * t + LANES]
             crossed = crossed + both[:, LANES * t : LANES * t + LANES]
+    return squares, crossed
+
+
+def attention_kernel(
+    core_ref, q_ref, y_ref, gain_ref, own_start_ref, own_inner_ref, start_ref, inner_ref, own_ref, got_ref, got_x_ref,
+    own_o_ref, other_o_ref, sums_ref, state_ref,
+):
+    core = core_ref[0]
+    own_states(core, 1, own_ref, got_x_ref, got_x_ref, state_ref)
+    zero = jnp.zeros((TOKENS, LANES), F32)
+    squares, crossed = attention_half(
+        core, q_ref, y_ref, gain_ref, own_start_ref, own_inner_ref, state_ref, own_o_ref, zero, zero
+    )
+    squares, crossed = attention_half(
+        1 - core, q_ref, y_ref, gain_ref, start_ref, inner_ref, got_ref, other_o_ref, squares, crossed
+    )
     sums_ref[0:1, :] = jnp.sum(squares.T, axis=0, keepdims=True)
     sums_ref[1:2, :] = jnp.sum(crossed.T, axis=0, keepdims=True)
 
 
 def norm_kernel(
-    core_ref, q_ref, y_ref, gain_ref, accum_ref, o_ref, sums_0, sums_1, sums_2, sums_3, back_ref, c_ref
+    core_ref, q_ref, y_ref, gain_ref, accum_ref, own_o_ref, other_o_ref, sums_0, sums_1, sums_2, sums_3, back_ref, c_ref
 ):
     sums = (sums_0[...] + sums_1[...]) + (sums_2[...] + sums_3[...])
     root = jnp.sqrt(sums[0:1, :] / (HEADS * HEAD_DIM) + 1e-05)
@@ -337,11 +365,13 @@
     cols = columns(jnp.concatenate([1.0 / root, factor], axis=0))
     inverse = jnp.broadcast_to(cols[:, 0:1], (TOKENS, 384))
     factor = jnp.broadcast_to(cols[:, 1:2], (TOKENS, 384))
-    for g in range(4):
-        at = slice(384 * g, 384 * g + 384)
-        scaled = gain_ref[:, at] * y_ref[:, at].astype(F32)
-        back_ref[:, at] = (scaled * inverse - o_ref[:, at] * factor).astype(BF16)
-    half = 1 - core_ref[0]
+    core = core_ref[0]
+    for half, o_ref in ((1 - core, other_o_ref), (core, own_o_ref)):
+        for i in range(2):
+            lanes = group_lanes(half, i)
+            scaled = gain_ref[:, lanes] * y_ref[:, lanes].astype(F32)
+            back_ref[:, lanes] = (scaled * inverse - o_ref[:, 384 * i : 384 * i + 384] * factor).astype(BF16)
+    half = 1 - core
     outer_states(half, q_ref, jnp.exp(half_rows(accum_ref, half)), back_ref, c_ref)
 
 
@@ -350,19 +380,19 @@
     outer_states(half, q_ref, jnp.exp(half_rows(accum_ref, half)), back_ref, c_ref)
 
 
-def middle_kernel(q_ref, k_ref, v_ref, back_ref, accum_ref, state_ref, gq_ref, gk_ref, done_ref):
-    accum = accum_ref[...]
-    done_ref[...] = accum[:8]
+def middle_half(half, q_ref, kv_ref, back_ref, accum_ref, state_ref, gq_ref, gk_ref):
+    accum = half_rows(accum_ref, half)
     cols = columns(accum)
     start = jnp.exp(cols)
-    for g in range(4):
-        pairs = [pair_states(state_ref, g, p) for p in range(2)]
-        at = slice(384 * g, 384 * g + 384)
-        gq = group_columns(start, g) * times_states(back_ref[:, at], pairs, dot_nt)
+    k_ref, v_ref = keys_of(kv_ref), values_of(kv_ref)
+    for i in range(2):
+        g = 2 * half + i
+        pairs = [pair_states(state_ref, i, p) for p in range(2)]
+        gq = group_columns(start, i) * times_states(back_ref[:, group_lanes(half, i)], pairs, dot_nt)
         gq = [gq[:, LANES * t : LANES * t + LANES] for t in range(3)]
         gk = [None] * 3
         for j in range(4):
-            h = 4 * g + j
+            h = 4 * i + j
             q = head_tiles(q_ref, g, j, True)
             k = head_tiles(k_ref, g, j, True)
             v = head_tiles(v_ref, g, j, False)
@@ -372,48 +402,88 @@
             add_tiles(gq, dot_nn(weights, k), j)
             add_tiles(gk, dot_nn(weights_t, q), j)
         for t in range(3):
-            lane = slice(384 * g + LANES * t, 384 * g + LANES * t + LANES)
-            gq_ref[:, lane] = gq[t].astype(BF16)
-            gk_ref[:, lane] = gk[t]
-
-
-def values_kernel(q_ref, k_ref, back_ref, accum_ref, gv_ref):
-    accum = accum_ref[...]
+            gq_ref[:, at_lanes(384 * g, LANES * t, LANES)] = gq[t].astype(BF16)
+            gk_ref[:, 384 * i + LANES * t : 384 * i + LANES * t + LANES] = gk[t]
+
+
+def middle_kernel(
+    core_ref, q_ref, kv_ref, back_ref, accum_ref, own_ref, got_x_ref, other_state_ref,
+    gq_ref, own_gk_ref, other_gk_ref, done_ref, own_state_ref,
+):
+    done_ref[...] = accum_ref[0:8, :]
+    core = core_ref[0]
+    own_states(core, 1, own_ref, got_x_ref, got_x_ref, own_state_ref)
+    middle_half(core, q_ref, kv_ref, back_ref, accum_ref, own_state_ref, gq_ref, own_gk_ref)
+    middle_half(1 - core, q_ref, kv_ref, back_ref, accum_ref, other_state_ref, gq_ref, other_gk_ref)
+
+
+def values_half(half, q_ref, kv_ref, back_ref, accum_ref, gv_ref):
+    accum = half_rows(accum_ref, half)
     cols = columns(accum)
-    for g in range(4):
+    k_ref = keys_of(kv_ref)
+    for i in range(2):
+        g = 2 * half + i
         gv = [None] * 3
         for j in range(4):
-            h = 4 * g + j
             scores = dot_nt(head_tiles(k_ref, g, j, True), head_tiles(q_ref, g, j, False))
-            weights = (scores * weight_turned(accum, cols, h)).astype(BF16)
+            weights = (scores * weight_turned(accum, cols, 4 * i + j)).astype(BF16)
             add_tiles(gv, dot_nn(weights, head_tiles(back_ref, g, j, True)), j)
         for t in range(3):
-            gv_ref[:, 384 * g + LANES * t : 384 * g + LANES * t + LANES] = gv[t]
-
-
-def last_kernel(
-    core_ref, k_ref, v_ref, tail_ref, gk0_ref, gv0_ref, own_ref, got_ref, got_c_ref, got_x_ref,
-    gk_hbm, gv_hbm, carry_ref, gk_ref, gv_ref, sems,
+            gv_ref[:, 384 * i + LANES * t : 384 * i + LANES * t + LANES] = gv[t]
+
+
+def values_own_kernel(core_ref, q_ref, kv_ref, back_ref, accum_ref, gv_ref, done_ref):
+    done_ref[...] = accum_ref[0:8, :]
+    values_half(core_ref[0], q_ref, kv_ref, back_ref, accum_ref, gv_ref)
+
+
+def values_other_kernel(core_ref, q_ref, kv_ref, back_ref, accum_ref, gv_ref):
+    values_half(1 - core_ref[0], q_ref, kv_ref, back_ref, accum_ref, gv_ref)
+
+
+def last_group(half, i, kv_ref, tail, gk0_ref, gv0_ref, carry_ref, gk_ref, gv_ref):
+    pairs = [pair_states(carry_ref, i, p) for p in range(2)]
+    lanes = group_lanes(half, i)
+    at = slice(384 * i, 384 * i + 384)
+    wide = group_columns(tail, i)
+    k_ref, v_ref = keys_of(kv_ref), values_of(kv_ref)
+    gk_ref[:, at] = (gk0_ref[:, at] + wide * times_states(v_ref[:, lanes], pairs, dot_nt)).astype(BF16)
+    gv_ref[:, at] = (gv0_ref[:, at] + wide * times_states(k_ref[:, lanes], pairs, dot_nn)).astype(BF16)
+
+
+def last_own_kernel(
+    core_ref, kv_ref, tail_ref, gk0_ref, gv0_ref, own_ref, got_c_ref, got_x_ref, gk_ref, gv_ref, carry_ref
 ):
     core = core_ref[0]
-    tail = tail_ref[...]
+    own_states(core, 0, own_ref, got_c_ref, got_x_ref, carry_ref)
+    for i in range(2):
+        last_group(core, i, kv_ref, tail_ref[...], gk0_ref, gv0_ref, carry_ref, gk_ref, gv_ref)
+
+
+def last_other_kernel(
+    core_ref, kv_ref, tail_ref, gk0_ref, gv0_ref, carry_ref, own_gk_ref, own_gv_ref,
+    gk_hbm, gv_hbm, gk_ref, gv_ref, sems,
+):
+    core = core_ref[0]
     copies = []
-    for g in range(4):
-        finish_states(g, core, 0, own_ref, got_ref, got_c_ref, got_x_ref, carry_ref)
-        pairs = [pair_states(carry_ref, g, p) for p in range(2)]
-        at = slice(384 * g, 384 * g + 384)
-        wide = group_columns(tail, g)
-        gk_ref[:, at] = (gk0_ref[:, at] + wide * times_states(v_ref[:, at], pairs, dot_nt)).astype(BF16)
-        gv_ref[:, at] = (gv0_ref[:, at] + wide * times_states(k_ref[:, at], pairs, dot_nn)).astype(BF16)
-        for i, (src, dst) in enumerate(((gk_ref, gk_hbm), (gv_ref, gv_hbm))):
-            copy = pltpu.make_async_copy(src.at[:, at], dst.at[:, at], sems.at[2 * g + i])
+
+    def copy_out(half, i, gk, gv, first):
+        lanes = group_lanes(half, i)
+        for n, (src, dst) in enumerate(((gk, gk_hbm), (gv, gv_hbm))):
+            copy = pltpu.make_async_copy(src.at[:, pl.ds(384 * i, 384)], dst.at[:, lanes], sems.at[first + n])
             copy.start()
             copies.append(copy)
+
+    for i in range(2):
+        copy_out(core, i, own_gk_ref, own_gv_ref, 2 * i)
+    for i in range(2):
+        last_group(1 - core, i, kv_ref, tail_ref[...], gk0_ref, gv0_ref, carry_ref, gk_ref, gv_ref)
+        copy_out(1 - core, i, gk_ref, gv_ref, 4 + 2 * i)
     for copy in copies:
         copy.wait()
 
 
-def call(kernel, outs, smem, *args, hbm_in=(), hbm_out=(), scratch=(), flops=0, vmem=VMEM):
+def call(kernel, outs, smem, *args, hbm_in=(), hbm_out=(), scratch=(), flops=0):
     specs = []
     for i, arg in enumerate(args):
         space = pltpu.SMEM if i < smem else pltpu.HBM if i in hbm_in else pltpu.VMEM
@@ -426,7 +496,7 @@
         in_specs=specs,
         out_specs=[pl.BlockSpec(memory_space=pltpu.HBM if i in hbm_out else pltpu.VMEM) for i in range(len(shapes))],
         scratch_shapes=scratch,
-        compiler_params=pltpu.CompilerParams(vmem_limit_bytes=vmem),
+        compiler_params=pltpu.CompilerParams(vmem_limit_bytes=VMEM),
         cost_estimate=pl.CostEstimate(flops=flops, bytes_accessed=moved, transcendentals=0),
         name=kernel.__name__,
     )(*args)
@@ -435,6 +505,7 @@
 
 SWAP = [(0, 1), (1, 0)]
 CHIP_BITS = ("xh", "xl", "zh", "zm", "zl")
+EXCHANGE = ("zl", "zm", "xl", "xh", "zh")
 
 
 def swap(value):
@@ -442,8 +513,9 @@
 
 
 def exchange(value):
-    parts = value.reshape(CHIPS, -1, 2, LANES)
-    return lax.all_to_all(parts, CHIP_BITS[::-1], 0, 0, tiled=True).reshape(value.shape)
+    rows = value.shape[0] // CHIPS
+    parts = value.reshape(CHIPS, rows // 2, 2, LANES) if rows % 2 == 0 else value.reshape(-1)
+    return lax.all_to_all(parts, EXCHANGE, 0, 0, tiled=True).reshape(value.shape)
 
 
 def others(value):
@@ -453,56 +525,73 @@
 def local(q, k, v, y, logs, gain):
     core = lax.axis_index("core").astype(jnp.int32).reshape(1)
     gain = gain.reshape(1, WIDTH)
-    wide = (TOKENS, WIDTH)
-    narrow = pltpu.VMEM(wide, BF16)
     half = ((HALF_ROWS, LANES), F32)
     half_decay = ((HALF_ROWS + HALF, LANES), F32)
     rows = ((LOCAL_HEADS, LANES), F32)
     cols = ((TOKENS, LANES), F32)
-    kv = jnp.concatenate([k, v])
-    kv, logs = lax.optimization_barrier((kv, logs))
+    token = ((8, LANES), F32)
+    wide = (TOKENS, WIDTH)
+    half_wide = ((TOKENS, WIDTH // 2), F32)
+    narrow = pltpu.VMEM((TOKENS, WIDTH // 2), BF16)
+    kv, logs = lax.optimization_barrier((jnp.concatenate([k, v]), logs))
     x_send, accum = call(state_send_kernel, [half_decay, rows], 1, core, kv, logs, flops=10**9)
     got_x = swap(x_send)
     x_keep = call(state_keep_kernel, [half_decay], 1, core, kv, accum, flops=10**9)
-    payload = call(combine_forward_kernel, [((CHIPS * FWD_PART, LANES), F32)], 1, core, x_keep, got_x)
+    payload = call(
+        combine_forward_kernel, [((CHIPS * FWD_PART, LANES), F32)], 1, core, x_keep, got_x
+    )
     payload = exchange(payload)
-    inner, start, tail = call(inner_kernel, [(wide, F32), cols, cols], 0, q, k, v, accum, flops=2 * 10**9)
     entering, decays = call(scan_forward_kernel, [half, ((CHIPS, LANES), F32)], 0, payload)
     entering = exchange(entering)
     got_entering = swap(call(step_forward_kernel, [half], 1, core, entering, x_keep))
-    attention, state, sums = call(
+    own_inner, own_start, own_tail, inner, start, tail = call(
+        inner_kernel, [half_wide, cols, cols, half_wide, cols, cols], 1, core, q, kv, accum, flops=2 * 10**9
+    )
+    half_scratch = pltpu.VMEM((HALF_ROWS, LANES), F32)
+    own_o, other_o, sums = call(
         attention_kernel,
-        [(wide, F32), ((ROWS, LANES), F32), ((2, LANES), F32)],
-        1, core, q, y, gain, start, inner, entering, got_entering, got_x,
+        [half_wide, half_wide, ((2, LANES), F32)],
+        1, core, q, y, gain, own_start, own_inner, start, inner, entering, got_entering, got_x,
+        scratch=[half_scratch],
         flops=10**9,
     )
     back, c_send = call(
         norm_kernel,
         [(wide, BF16), half],
-        1, core, q, y, gain, accum, attention, sums, *others(sums),
+        1, core, q, y, gain, accum, own_o, other_o, sums, *others(sums),
         flops=10**9,
     )
     got_c = swap(c_send)
-    c_keep = call(carry_keep_kernel, [half], 1, core, q, back, accum, flops=10**9)
+    c_keep = call(carry_keep_kernel, [half], 1, core, q, back, accum, flops=5 * 10**8)
+    own_gv, values_done = call(values_own_kernel, [half_wide, token], 1, core, q, kv, back, accum, flops=10**9)
     payload = call(combine_backward_kernel, [half], 1, core, c_keep, got_c, x_keep, got_x)
     payload = exchange(payload)
-    gq, gk0, middle_done = call(
+    gq, own_gk, other_gk, middle_done = call(
         middle_kernel,
-        [(wide, BF16), (wide, F32), ((8, LANES), F32)],
-        0, q, k, v, back, accum, state,
+        [(wide, BF16), half_wide, half_wide, token],
+        1, core, q, kv, back, accum, entering, got_x, got_entering,
+        scratch=[half_scratch],
         flops=4 * 10**9,
     )
-    leaving = call(scan_backward_kernel, [half], 0, payload, decays, middle_done)
+    leaving = call(scan_backward_kernel, [half], 0, payload, decays, middle_done, values_done)
     leaving = exchange(leaving)
     got_leaving = swap(call(step_backward_kernel, [half], 1, core, leaving, c_keep, x_keep))
-    gv0 = call(values_kernel, [(wide, F32)], 0, q, k, back, accum, flops=2 * 10**9)
+    other_gv = call(values_other_kernel, [half_wide], 1, core, q, kv, back, accum, flops=10**9)
+    half_narrow = ((TOKENS, WIDTH // 2), BF16)
+    own_gk, own_gv = call(
+        last_own_kernel,
+        [half_narrow, half_narrow],
+        1, core, kv, own_tail, own_gk, own_gv, leaving, got_c, got_x,
+        scratch=[half_scratch],
+        flops=5 * 10**8,
+    )
     gk, gv = call(
-        last_kernel,
+        last_other_kernel,
         [(wide, BF16), (wide, BF16)],
-        1, core, k, v, tail, gk0, gv0, leaving, got_leaving, got_c, got_x,
+        1, core, kv, tail, other_gk, other_gv, got_leaving, own_gk, own_gv,
         hbm_out=(0, 1),
-        scratch=[pltpu.VMEM((ROWS, LANES), F32), narrow, narrow, pltpu.SemaphoreType.DMA((8,))],
-        flops=2 * 10**9,
+        scratch=[narrow, narrow, pltpu.SemaphoreType.DMA((8,))],
+        flops=5 * 10**8,
     )
     return gq, gk, gv
 

time: 100 us -> 99.3 us (level)
  waiting for transfers between devices: 10.2 us -> 6.3 us
  starting transfers between devices: 20.5 us -> 22.6 us
    all_to_all x1, waiting for transfers between devices: 5.8 us -> 3.45 us  [exchange(): lax.all_to_all(parts, EXCHANGE, 0, 0, tiled=True).reshape(value.shape)]
    ppermute x3, waiting for transfers between devices: 2.94 us -> 1.35 us  [others(): lax.ppermute(value, 'head', [(i, (i + k) % 4) for i in range(4)])]
    ppermute x4, starting transfers between devices: 11.9 us -> 13.2 us  [swap(): return lax.ppermute(value, 'core', SWAP)]
    ppermute x3, starting transfers between devices: 3.85 us -> 5.06 us  [others(): lax.ppermute(value, 'head', [(i, (i + k) % 4) for i in range(4)])]
    pallas_call x15 -> x17, Pallas kernels: 13 us -> 13.4 us  [call(): pl.pallas_call(kernel, out_shape=shapes, in_specs=specs, out_specs=[pl.Bl...]
    unnamed x22 -> x28, local copies, waits for them, and re-layouts: 1.93 us -> 2.13 us
  transfers between devices with their start and end apart: 8 -> 8, of which waited for: 5 -> 5; matrix products, arithmetic and copies ran while one was open for 0% -> 0% of each run, Pallas kernels for 8% -> 9%
where the time goes in v4:
time: 99.3 us; the launch traced here: 98.9 us
  blocking collectives  52.3 us (53%)
  starting transfers between devices  22.6 us (23%)
  Pallas kernels  13.4 us (13%)
  waiting for transfers between devices  6.3 us (6%)
  local copies, waits for them, and re-layouts  2.13 us (2%)
  other arithmetic  1.17 us (1%)
  between operations  1.02 us (1%)
    all_to_all x3, blocking collectives, exchange(): lax.all_to_all(parts, EXCHANGE, 0, 0, tiled=True).reshape(value.shape)  52.3 us
    pallas_call x17, Pallas kernels, call(): pl.pallas_call(kernel, out_shape=shapes, in_specs=specs, out_specs=[pl.Bl...  13.4 us
    ppermute x4, starting transfers between devices, swap(): return lax.ppermute(value, 'core', SWAP)  13.2 us
    ppermute x3, starting transfers between devices, others(): lax.ppermute(value, 'head', [(i, (i + k) % 4) for i in range(4)])  5.06 us
    all_to_all x1, starting transfers between devices, exchange(): lax.all_to_all(parts, EXCHANGE, 0, 0, tiled=True).reshape(value.shape)  4.32 us
    all_to_all x1, waiting for transfers between devices, exchange(): lax.all_to_all(parts, EXCHANGE, 0, 0, tiled=True).reshape(value.shape)  3.45 us
    unnamed x28, local copies, waits for them, and re-layouts  2.13 us
  transfers between devices with their start and end apart: 8, of which 5 were waited for; matrix products, arithmetic and copies ran while one was open for 0% of the time, Pallas kernels for 9%

profile of v4, /device:TPU:1, one launch (start us, length us, event | category | flops | bytes accessed | tf_op | source)
XLA Modules:
  0.0 98.9 jit_solution(4706166880672654902)
XLA Ops:
  0.6 1.2 %pad_maximum_fusion.kv_ref = bf16[256,1536]{1,0:T(8,128)(2,1)S(1)} fusion(bf16[128,1536]{1,0:T(8,128)(2,1)} %param.8, bf16[128,1536]{1,0:T(8,128)(2,1)} %param.7), kind=kLoop, calls=%fused_computation | loop fusion | flops 1572864 | bytes 1572864 | tf_op jit(solution)/shard_map/concatenate | solution.py:536
  1.8 0.7 state_send_kernel.1
  2.5 3.3 %collective-permute-start = (f32[584,128]{1,0:T(8,128)S(1)}, f32[584,128]{1,0:T(8,128)S(1)}, u32[]{:S(2)}, u32[]{:S(2)}) collective-permute-start(f32[584,128]{1,0:T(8,128)S(1)} %get-tuple-element.37), channel_id=1, source_target_pairs={{0,4},{4,0},{1,5},{5,1},{2,6},{6,2},{3,7},{7,3},{8,12},{12,8},{9,1... | collective-permute-start | bytes 897032 | tf_op jit(solution)/shard_map/ppermute | solution.py:512
  5.8 0.5 state_keep_kernel.1.own_ref.x_ref.own_x_ref
  6.3 0.8 collective-permute-done.got_ref.got_x_ref
  7.0 0.1 combine_forward_kernel.1
  7.1 19.7 %all_to_all.24 = f32[32,2432,1]{1,2,0:T(1,128)S(1)} all-to-all(f32[32,2432,1]{1,2,0:T(1,128)S(1)} %bitcast.12), channel_id=1, replica_groups=mesh['xh'=2,'xl'=2,'zh'=2,'zm'=2,'zl'=2,'core'=2,'head'=4] {'zl','zm','x..., dimensions={0} | all-to-all | bytes 622592 | tf_op jit(solution)/shard_map/all_to_all | solution.py:518
  26.8 0.1 scan_forward_kernel.1
  26.8 0.0 copy-start.13
  26.8 0.0 copy-start.3
  26.9 16.4 %all_to_all.25 = f32[32,9,2,128]{3,2,1,0:T(2,128)S(1)} all-to-all(f32[32,9,2,128]{3,2,1,0:T(2,128)S(1)} %bitcast.18), channel_id=1, replica_groups=mesh['xh'=2,'xl'=2,'zh'=2,'zm'=2,'zl'=2,'core'=2,'head'=4] {'zl','zm','x..., dimensions={0} | all-to-all | bytes 589824 | tf_op jit(solution)/shard_map/all_to_all | solution.py:518
  43.3 4.0 %collective-permute-start.1 = (f32[576,128]{1,0:T(8,128)S(1)}, f32[576,128]{1,0:T(8,128)S(1)}, u32[]{:S(2)}, u32[]{:S(2)}) collective-permute-start(f32[576,128]{1,0:T(8,128)S(1)} %step_forward_kernel.1), channel_id=1, source_target_pairs={{0,4},{4,0},{1,5},{5,1},{2,6},{6,2},{3,7},{7,3},{8,12},{12,8},{9,1... | collective-permute-start | bytes 884744 | tf_op jit(solution)/shard_map/ppermute | solution.py:512
  47.4 0.0 copy-start.2
  47.4 1.6 %inner_kernel.1 = (f32[128,768]{1,0:T(8,128)S(1)}, f32[128,128]{1,0:T(8,128)S(1)}, f32[128,128]{1,0:T(8,128)S(1)}, f32[128,768]{1,0:T(8,128)S(1)}, f32[128,128]{1,0:T(8,128)S(1)}, /*index=5*/f32[128,128]{1,0:T(8,128)S(1)}) custom-call(s32[1]{0:T(128)} %bitcast.core_ref, bf16[128,1536]{1,0:T(8,128)(2,1)S(1)} %copy-done.3, ...), custom_call_target="tpu_custom_call" | custom-call | flops 2000000000 | bytes 2236420 | tf_op jit(solution)/shard_map/inner_kernel/pallas_call | solution.py:493
  49.0 0.0 collective-permute-done.1.got_ref.other_state_ref
  49.0 0.0 copy-start.6
  49.0 0.8 attention_kernel.1
  49.9 1.4 %collective-permute-start.2 = (f32[2,128]{1,0:T(2,128)S(1)}, f32[2,128]{1,0:T(2,128)S(1)}, u32[]{:S(2)}, u32[]{:S(2)}) collective-permute-start(f32[2,128]{1,0:T(2,128)S(1)} %get-tuple-element.41.sums_0), channel_id=1, source_target_pairs={{0,1},{1,2},{2,3},{3,0},{4,5},{5,6},{6,7},{7,4},{8,9},{9,10},{10,1... | collective-permute-start | bytes 3080 | tf_op jit(solution)/shard_map/ppermute | solution.py:522
  51.2 2.6 %collective-permute-start.3 = (f32[2,128]{1,0:T(2,128)S(1)}, f32[2,128]{1,0:T(2,128)S(1)}, u32[]{:S(2)}, u32[]{:S(2)}) collective-permute-start(f32[2,128]{1,0:T(2,128)S(1)} %get-tuple-element.41.sums_0), channel_id=1, source_target_pairs={{0,2},{1,3},{2,0},{3,1},{4,6},{5,7},{6,4},{7,5},{8,10},{9,11},{10,... | collective-permute-start | bytes 3080 | tf_op jit(solution)/shard_map/ppermute | solution.py:522
  53.9 1.1 %collective-permute-start.4 = (f32[2,128]{1,0:T(2,128)S(1)}, f32[2,128]{1,0:T(2,128)S(1)}, u32[]{:S(2)}, u32[]{:S(2)}) collective-permute-start(f32[2,128]{1,0:T(2,128)S(1)} %get-tuple-element.41.sums_0), channel_id=1, source_target_pairs={{0,3},{1,0},{2,1},{3,2},{4,7},{5,4},{6,5},{7,6},{8,11},{9,8},{10,9... | collective-permute-start | bytes 3080 | tf_op jit(solution)/shard_map/ppermute | solution.py:522
  54.9 0.2 collective-permute-done.3.sums_2
  55.2 1.1 %collective-permute-done.4.sums_3 = f32[2,128]{1,0:T(2,128)S(1)} collective-permute-done((f32[2,128]{1,0:T(2,128)S(1)}, f32[2,128]{1,0:T(2,128)S(1)}, u32[]{:S(2)}, u32[]{:S(2)}) %collective-permute-start.4) | collective-permute-done | bytes 1056 | tf_op jit(solution)/shard_map/ppermute | solution.py:522
  56.3 0.7 norm_kernel.1
  57.0 0.0 copy-start.9
  57.0 1.8 %collective-permute-start.5 = (f32[576,128]{1,0:T(8,128)S(1)}, f32[576,128]{1,0:T(8,128)S(1)}, u32[]{:S(2)}, u32[]{:S(2)}) collective-permute-start(f32[576,128]{1,0:T(8,128)S(1)} %get-tuple-element.46), channel_id=1, source_target_pairs={{0,4},{4,0},{1,5},{5,1},{2,6},{6,2},{3,7},{7,3},{8,12},{12,8},{9,1... | collective-permute-start | bytes 884744 | tf_op jit(solution)/shard_map/ppermute | solution.py:512
  58.8 0.5 carry_keep_kernel.1.own_ref.c_ref
  59.3 0.7 collective-permute-done.5.got_ref.got_c_ref
  60.1 0.8 combine_backward_kernel.1
  60.8 4.3 %all-to-all-start.2 = ((f32[32,9,2,128]{3,2,1,0:T(2,128)}), f32[32,9,2,128]{3,2,1,0:T(2,128)S(1)}, u32[]{:S(2)}, u32[]{:S(2)}) async-start(f32[32,9,2,128]{3,2,1,0:T(2,128)} %bitcast.5), calls=%async_computation.2 | async-start | bytes 589824 | tf_op jit(solution)/shard_map/all_to_all | solution.py:518
  65.1 0.0 copy-start.10
  65.1 1.0 copy-done.10
  66.1 0.9 values_own_kernel.1
  67.0 0.1 copy-done.4
  67.1 0.1 copy-done.7
  67.2 0.1 copy-done.11
  67.3 3.9 %middle_kernel.1 = (bf16[128,1536]{1,0:T(8,128)(2,1)}, f32[128,768]{1,0:T(8,128)S(1)}, f32[128,768]{1,0:T(8,128)S(1)}, f32[8,128]{1,0:T(8,128)S(1)}) custom-call(s32[1]{0:T(128)} %bitcast.core_ref, bf16[128,1536]{1,0:T(8,128)(2,1)S(1)} %copy-done.4, bf16[256,1536]{1,0:T(8,128)(2,1)S(1)} %pad_maximum_fusion.kv_ref, bf16[128,1536]{1,0:T(8,128)(2,1)S(1)} %copy-done.11, ...), custom_call_target="tpu_custom_call" | custom-call | flops 4000000000 | bytes 3653636 | tf_op jit(solution)/shard_map/middle_kernel/pallas_call | solution.py:493
  71.2 0.7 copy-done
  72.0 3.5 %all-to-all-done.2 = f32[32,9,2,128]{3,2,1,0:T(2,128)S(1)} async-done(((f32[32,9,2,128]{3,2,1,0:T(2,128)}), f32[32,9,2,128]{3,2,1,0:T(2,128)S(1)}, u32[]{:S(2)}, u32[]{:S(2)}) %all-to-all-start.2) | async-done | bytes 294944 | tf_op jit(solution)/shard_map/all_to_all | solution.py:518
  75.4 0.1 scan_backward_kernel.1
  75.5 0.0 copy-start.5
  75.5 0.0 copy-start.12
  75.5 16.2 %all_to_all.26 = f32[32,9,2,128]{3,2,1,0:T(2,128)S(1)} all-to-all(f32[32,9,2,128]{3,2,1,0:T(2,128)S(1)} %bitcast.17), channel_id=1, replica_groups=mesh['xh'=2,'xl'=2,'zh'=2,'zm'=2,'zl'=2,'core'=2,'head'=4] {'zl','zm','x..., dimensions={0} | all-to-all | bytes 589824 | tf_op jit(solution)/shard_map/all_to_all | solution.py:518
  91.7 0.1 step_backward_kernel.1
  91.8 0.0 copy-start.1
  91.8 4.0 %collective-permute-start.6 = (f32[576,128]{1,0:T(8,128)S(1)}, f32[576,128]{1,0:T(8,128)S(1)}, u32[]{:S(2)}, u32[]{:S(2)}) collective-permute-start(f32[576,128]{1,0:T(8,128)S(1)} %step_backward_kernel.1), channel_id=1, source_target_pairs={{0,4},{4,0},{1,5},{5,1},{2,6},{6,2},{3,7},{7,3},{8,12},{12,8},{9,1... | collective-permute-start | bytes 884744 | tf_op jit(solution)/shard_map/ppermute | solution.py:512
  95.8 0.9 values_other_kernel.1.gv0_ref
  96.7 0.7 last_own_kernel.1
  97.3 1.4 %last_other_kernel.1 = (bf16[128,1536]{1,0:T(8,128)(2,1)}, bf16[128,1536]{1,0:T(8,128)(2,1)}) custom-call(s32[1]{0:T(128)} %bitcast.core_ref, bf16[256,1536]{1,0:T(8,128)(2,1)S(1)} %pad_maximum_fusion.kv_ref, f32[128,128]{1,0:T(8,128)S(1)} %get-tuple-element.44.tail_ref, f32[128,768]{1,0:T(8,128)S(1)} %get-tuple-element.45.gk0_ref, ...), custom_call_target="tpu_custom_call" | custom-call | flops 500000000 | bytes 3112964 | tf_op jit(solution)/shard_map/last_other_kernel/pallas_call | solution.py:493
  (18 shorter events, 0.1 us)
Async XLA Ops:
  0.6 1.2 %copy-start.8 = (f32[16,128]{1,0:T(8,128)S(1)}, f32[16,128]{1,0:T(8,128)}, u32[]{:S(2)}) copy-start(f32[16,128]{1,0:T(8,128)} %logs_ref) | copy-start | bytes 24580
  2.5 4.5 %collective-permute-start = (f32[584,128]{1,0:T(8,128)S(1)}, f32[584,128]{1,0:T(8,128)S(1)}, u32[]{:S(2)}, u32[]{:S(2)}) collective-permute-start(f32[584,128]{1,0:T(8,128)S(1)} %get-tuple-element.37), channel_id=1, source_target_pairs={{0,4},{4,0},{1,5},{5,1},{2,6},{6,2},{3,7},{7,3},{8,12},{12,8},{9,1... | collective-permute-start | bytes 897032 | tf_op jit(solution)/shard_map/ppermute | solution.py:512
  26.8 20.5 %copy-start.13 = (f32[1536]{0:T(1024)S(1)}, f32[1536]{0:T(1024)}, u32[]{:S(2)}) copy-start(f32[1536]{0:T(1024)} %param.11) | copy-start | bytes 18436
  26.8 20.5 %copy-start.3 = (bf16[128,1536]{1,0:T(8,128)(2,1)S(1)}, bf16[128,1536]{1,0:T(8,128)(2,1)}, u32[]{:S(2)}) copy-start(bf16[128,1536]{1,0:T(8,128)(2,1)} %q_ref.13) | copy-start | bytes 1179652
  43.3 5.7 %collective-permute-start.1 = (f32[576,128]{1,0:T(8,128)S(1)}, f32[576,128]{1,0:T(8,128)S(1)}, u32[]{:S(2)}, u32[]{:S(2)}) collective-permute-start(f32[576,128]{1,0:T(8,128)S(1)} %step_forward_kernel.1), channel_id=1, source_target_pairs={{0,4},{4,0},{1,5},{5,1},{2,6},{6,2},{3,7},{7,3},{8,12},{12,8},{9,1... | collective-permute-start | bytes 884744 | tf_op jit(solution)/shard_map/ppermute | solution.py:512
  47.4 1.7 %copy-start.2 = (bf16[128,1536]{1,0:T(8,128)(2,1)S(1)}, bf16[128,1536]{1,0:T(8,128)(2,1)}, u32[]{:S(2)}) copy-start(bf16[128,1536]{1,0:T(8,128)(2,1)} %y_ref.3) | copy-start | bytes 1179652
  49.0 0.9 copy-start.6
  49.9 5.1 %collective-permute-start.2 = (f32[2,128]{1,0:T(2,128)S(1)}, f32[2,128]{1,0:T(2,128)S(1)}, u32[]{:S(2)}, u32[]{:S(2)}) collective-permute-start(f32[2,128]{1,0:T(2,128)S(1)} %get-tuple-element.41.sums_0), channel_id=1, source_target_pairs={{0,1},{1,2},{2,3},{3,0},{4,5},{5,6},{6,7},{7,4},{8,9},{9,10},{10,1... | collective-permute-start | bytes 3080 | tf_op jit(solution)/shard_map/ppermute | solution.py:522
  51.2 3.9 %collective-permute-start.3 = (f32[2,128]{1,0:T(2,128)S(1)}, f32[2,128]{1,0:T(2,128)S(1)}, u32[]{:S(2)}, u32[]{:S(2)}) collective-permute-start(f32[2,128]{1,0:T(2,128)S(1)} %get-tuple-element.41.sums_0), channel_id=1, source_target_pairs={{0,2},{1,3},{2,0},{3,1},{4,6},{5,7},{6,4},{7,5},{8,10},{9,11},{10,... | collective-permute-start | bytes 3080 | tf_op jit(solution)/shard_map/ppermute | solution.py:522
  53.9 2.4 %collective-permute-start.4 = (f32[2,128]{1,0:T(2,128)S(1)}, f32[2,128]{1,0:T(2,128)S(1)}, u32[]{:S(2)}, u32[]{:S(2)}) collective-permute-start(f32[2,128]{1,0:T(2,128)S(1)} %get-tuple-element.41.sums_0), channel_id=1, source_target_pairs={{0,3},{1,0},{2,1},{3,2},{4,7},{5,4},{6,5},{7,6},{8,11},{9,8},{10,9... | collective-permute-start | bytes 3080 | tf_op jit(solution)/shard_map/ppermute | solution.py:522
  57.0 2.3 %copy-start.9 = (bf16[128,1536]{1,0:T(8,128)(2,1)}, bf16[128,1536]{1,0:T(8,128)(2,1)S(1)}, u32[]{:S(2)}) copy-start(bf16[128,1536]{1,0:T(8,128)(2,1)S(1)} %get-tuple-element.42.back_ref) | copy-start | bytes 1179652
  57.0 3.0 %collective-permute-start.5 = (f32[576,128]{1,0:T(8,128)S(1)}, f32[576,128]{1,0:T(8,128)S(1)}, u32[]{:S(2)}, u32[]{:S(2)}) collective-permute-start(f32[576,128]{1,0:T(8,128)S(1)} %get-tuple-element.46), channel_id=1, source_target_pairs={{0,4},{4,0},{1,5},{5,1},{2,6},{6,2},{3,7},{7,3},{8,12},{12,8},{9,1... | collective-permute-start | bytes 884744 | tf_op jit(solution)/shard_map/ppermute | solution.py:512
  60.8 14.6 %all-to-all-start.2 = ((f32[32,9,2,128]{3,2,1,0:T(2,128)}), f32[32,9,2,128]{3,2,1,0:T(2,128)S(1)}, u32[]{:S(2)}, u32[]{:S(2)}) async-start(f32[32,9,2,128]{3,2,1,0:T(2,128)} %bitcast.5), calls=%async_computation.2 | async-start | bytes 589824 | tf_op jit(solution)/shard_map/all_to_all | solution.py:518
  65.1 1.0 %copy-start.10 = (bf16[128,1536]{1,0:T(8,128)(2,1)S(1)}, bf16[128,1536]{1,0:T(8,128)(2,1)}, u32[]{:S(2)}) copy-start(bf16[128,1536]{1,0:T(8,128)(2,1)} %copy-done.9) | copy-start | bytes 1179652
  66.1 1.0 %copy-start.4 = (bf16[128,1536]{1,0:T(8,128)(2,1)S(1)}, bf16[128,1536]{1,0:T(8,128)(2,1)}, u32[]{:S(2)}) copy-start(bf16[128,1536]{1,0:T(8,128)(2,1)} %q_ref.13) | copy-start | bytes 1179652
  66.1 1.1 %copy-start.7 = (f32[576,128]{1,0:T(8,128)S(1)}, f32[576,128]{1,0:T(8,128)}, u32[]{:S(2)}) copy-start(f32[576,128]{1,0:T(8,128)} %copy-done.6) | copy-start | bytes 884740
  66.1 1.2 %copy-start.11 = (bf16[128,1536]{1,0:T(8,128)(2,1)S(1)}, bf16[128,1536]{1,0:T(8,128)(2,1)}, u32[]{:S(2)}) copy-start(bf16[128,1536]{1,0:T(8,128)(2,1)} %copy-done.9) | copy-start | bytes 1179652
  71.2 0.7 copy-start
  75.5 20.3 %copy-start.5 = (bf16[128,1536]{1,0:T(8,128)(2,1)S(1)}, bf16[128,1536]{1,0:T(8,128)(2,1)}, u32[]{:S(2)}) copy-start(bf16[128,1536]{1,0:T(8,128)(2,1)} %q_ref.13) | copy-start | bytes 1179652
  75.5 20.3 %copy-start.12 = (bf16[128,1536]{1,0:T(8,128)(2,1)S(1)}, bf16[128,1536]{1,0:T(8,128)(2,1)}, u32[]{:S(2)}) copy-start(bf16[128,1536]{1,0:T(8,128)(2,1)} %copy-done.9) | copy-start | bytes 1179652
  91.8 4.9 %copy-start.1 = (f32[128,768]{1,0:T(8,128)S(1)}, f32[128,768]{1,0:T(8,128)}, u32[]{:S(2)}) copy-start(f32[128,768]{1,0:T(8,128)} %copy-done) | copy-start | bytes 1179652
  91.8 5.6 %collective-permute-start.6 = (f32[576,128]{1,0:T(8,128)S(1)}, f32[576,128]{1,0:T(8,128)S(1)}, u32[]{:S(2)}, u32[]{:S(2)}) collective-permute-start(f32[576,128]{1,0:T(8,128)S(1)} %step_backward_kernel.1), channel_id=1, source_target_pairs={{0,4},{4,0},{1,5},{5,1},{2,6},{6,2},{3,7},{7,3},{8,12},{12,8},{9,1... | collective-permute-start | bytes 884744 | tf_op jit(solution)/shard_map/ppermute | solution.py:512

commit v5 on v4

--- a/solution.py
+++ b/solution.py
@@ -156,14 +156,14 @@
     spread_by = wide_column(cols, h) - row
     shape = (TOKENS, LANES)
     keep = lanes_of(shape) <= rows_of(shape)
-    return jnp.where(keep, jnp.exp(jnp.where(keep, spread_by, 0.0)), 0.0)
+    return jnp.exp(jnp.where(keep, spread_by, -jnp.inf))
 
 
 def weight_turned(accum, cols, h):
     spread_by = accum[h : h + 1, :] - wide_column(cols, h)
     shape = (TOKENS, LANES)
     keep = rows_of(shape) <= lanes_of(shape)
-    return jnp.where(keep, jnp.exp(jnp.where(keep, spread_by, 0.0)), 0.0)
+    return jnp.exp(jnp.where(keep, spread_by, -jnp.inf))
 
 
 def outer_states(half, left_ref, scale, right_ref, out_ref):
@@ -505,7 +505,7 @@
 
 SWAP = [(0, 1), (1, 0)]
 CHIP_BITS = ("xh", "xl", "zh", "zm", "zl")
-EXCHANGE = ("zl", "zm", "xl", "xh", "zh")
+EXCHANGE = ("zm", "zh", "xh", "zl", "xl")
 
 
 def swap(value):

time: 99.3 us -> 98.5 us (level)
  blocking collectives: 52.3 us -> 50.8 us
    all_to_all x3, blocking collectives: 52.3 us -> 50.8 us  [exchange(): lax.all_to_all(parts, EXCHANGE, 0, 0, tiled=True).reshape(value.shape)]
where the time goes in v5:
time: 98.5 us; the launch traced here: 98.1 us
  blocking collectives  50.8 us (52%)
  starting transfers between devices  22.6 us (23%)
  Pallas kernels  13.4 us (14%)
  waiting for transfers between devices  6.94 us (7%)
  local copies, waits for them, and re-layouts  2.14 us (2%)
  other arithmetic  1.17 us (1%)
  between operations  1.02 us (1%)
    all_to_all x3, blocking collectives, exchange(): lax.all_to_all(parts, EXCHANGE, 0, 0, tiled=True).reshape(value.shape)  50.8 us
    pallas_call x17, Pallas kernels, call(): pl.pallas_call(kernel, out_shape=shapes, in_specs=specs, out_specs=[pl.Bl...  13.4 us
    ppermute x4, starting transfers between devices, swap(): return lax.ppermute(value, 'core', SWAP)  13.1 us
    ppermute x3, starting transfers between devices, others(): lax.ppermute(value, 'head', [(i, (i + k) % 4) for i in range(4)])  5.06 us
    all_to_all x1, starting transfers between devices, exchange(): lax.all_to_all(parts, EXCHANGE, 0, 0, tiled=True).reshape(value.shape)  4.47 us
    all_to_all x1, waiting for transfers between devices, exchange(): lax.all_to_all(parts, EXCHANGE, 0, 0, tiled=True).reshape(value.shape)  4.09 us
    unnamed x28, local copies, waits for them, and re-layouts  2.13 us
  transfers between devices with their start and end apart: 8, of which 5 were waited for; matrix products, arithmetic and copies ran while one was open for 0% of the time, Pallas kernels for 9%

profile of v5, /device:TPU:1, one launch (start us, length us, event | category | flops | bytes accessed | tf_op | source)
XLA Modules:
  0.0 98.1 jit_solution(1500440313484023446)
XLA Ops:
  0.6 1.2 %pad_maximum_fusion.kv_ref = bf16[256,1536]{1,0:T(8,128)(2,1)S(1)} fusion(bf16[128,1536]{1,0:T(8,128)(2,1)} %param.8, bf16[128,1536]{1,0:T(8,128)(2,1)} %param.7), kind=kLoop, calls=%fused_computation | loop fusion | flops 1572864 | bytes 1572864 | tf_op jit(solution)/shard_map/concatenate | solution.py:536
  1.8 0.7 state_send_kernel.1
  2.5 3.3 %collective-permute-start = (f32[584,128]{1,0:T(8,128)S(1)}, f32[584,128]{1,0:T(8,128)S(1)}, u32[]{:S(2)}, u32[]{:S(2)}) collective-permute-start(f32[584,128]{1,0:T(8,128)S(1)} %get-tuple-element.37), channel_id=1, source_target_pairs={{0,4},{4,0},{1,5},{5,1},{2,6},{6,2},{3,7},{7,3},{8,12},{12,8},{9,1... | collective-permute-start | bytes 897032 | tf_op jit(solution)/shard_map/ppermute | solution.py:512
  5.8 0.5 state_keep_kernel.1.own_ref.x_ref.own_x_ref
  6.3 0.8 collective-permute-done.got_ref.got_x_ref
  7.0 0.1 combine_forward_kernel.1
  7.1 20.4 %all_to_all.24 = f32[32,2432,1]{1,2,0:T(1,128)S(1)} all-to-all(f32[32,2432,1]{1,2,0:T(1,128)S(1)} %bitcast.12), channel_id=1, replica_groups=mesh['xh'=2,'xl'=2,'zh'=2,'zm'=2,'zl'=2,'core'=2,'head'=4] {'zm','zh','x..., dimensions={0} | all-to-all | bytes 622592 | tf_op jit(solution)/shard_map/all_to_all | solution.py:518
  27.5 0.1 scan_forward_kernel.1
  27.6 0.0 copy-start.13
  27.6 0.0 copy-start.3
  27.6 15.2 %all_to_all.25 = f32[32,9,2,128]{3,2,1,0:T(2,128)S(1)} all-to-all(f32[32,9,2,128]{3,2,1,0:T(2,128)S(1)} %bitcast.18), channel_id=1, replica_groups=mesh['xh'=2,'xl'=2,'zh'=2,'zm'=2,'zl'=2,'core'=2,'head'=4] {'zm','zh','x..., dimensions={0} | all-to-all | bytes 589824 | tf_op jit(solution)/shard_map/all_to_all | solution.py:518
  42.8 4.0 %collective-permute-start.1 = (f32[576,128]{1,0:T(8,128)S(1)}, f32[576,128]{1,0:T(8,128)S(1)}, u32[]{:S(2)}, u32[]{:S(2)}) collective-permute-start(f32[576,128]{1,0:T(8,128)S(1)} %step_forward_kernel.1), channel_id=1, source_target_pairs={{0,4},{4,0},{1,5},{5,1},{2,6},{6,2},{3,7},{7,3},{8,12},{12,8},{9,1... | collective-permute-start | bytes 884744 | tf_op jit(solution)/shard_map/ppermute | solution.py:512
  46.9 0.0 copy-start.2
  46.9 1.6 %inner_kernel.1 = (f32[128,768]{1,0:T(8,128)S(1)}, f32[128,128]{1,0:T(8,128)S(1)}, f32[128,128]{1,0:T(8,128)S(1)}, f32[128,768]{1,0:T(8,128)S(1)}, f32[128,128]{1,0:T(8,128)S(1)}, /*index=5*/f32[128,128]{1,0:T(8,128)S(1)}) custom-call(s32[1]{0:T(128)} %bitcast.core_ref, bf16[128,1536]{1,0:T(8,128)(2,1)S(1)} %copy-done.3, ...), custom_call_target="tpu_custom_call" | custom-call | flops 2000000000 | bytes 2236420 | tf_op jit(solution)/shard_map/inner_kernel/pallas_call | solution.py:493
  48.5 0.0 collective-permute-done.1.got_ref.other_state_ref
  48.5 0.0 copy-start.6
  48.6 0.8 attention_kernel.1
  49.4 1.4 %collective-permute-start.2 = (f32[2,128]{1,0:T(2,128)S(1)}, f32[2,128]{1,0:T(2,128)S(1)}, u32[]{:S(2)}, u32[]{:S(2)}) collective-permute-start(f32[2,128]{1,0:T(2,128)S(1)} %get-tuple-element.41.sums_0), channel_id=1, source_target_pairs={{0,1},{1,2},{2,3},{3,0},{4,5},{5,6},{6,7},{7,4},{8,9},{9,10},{10,1... | collective-permute-start | bytes 3080 | tf_op jit(solution)/shard_map/ppermute | solution.py:522
  50.8 2.6 %collective-permute-start.3 = (f32[2,128]{1,0:T(2,128)S(1)}, f32[2,128]{1,0:T(2,128)S(1)}, u32[]{:S(2)}, u32[]{:S(2)}) collective-permute-start(f32[2,128]{1,0:T(2,128)S(1)} %get-tuple-element.41.sums_0), channel_id=1, source_target_pairs={{0,2},{1,3},{2,0},{3,1},{4,6},{5,7},{6,4},{7,5},{8,10},{9,11},{10,... | collective-permute-start | bytes 3080 | tf_op jit(solution)/shard_map/ppermute | solution.py:522
  53.4 1.1 %collective-permute-start.4 = (f32[2,128]{1,0:T(2,128)S(1)}, f32[2,128]{1,0:T(2,128)S(1)}, u32[]{:S(2)}, u32[]{:S(2)}) collective-permute-start(f32[2,128]{1,0:T(2,128)S(1)} %get-tuple-element.41.sums_0), channel_id=1, source_target_pairs={{0,3},{1,0},{2,1},{3,2},{4,7},{5,4},{6,5},{7,6},{8,11},{9,8},{10,9... | collective-permute-start | bytes 3080 | tf_op jit(solution)/shard_map/ppermute | solution.py:522
  54.5 0.2 collective-permute-done.3.sums_2
  54.7 1.1 %collective-permute-done.4.sums_3 = f32[2,128]{1,0:T(2,128)S(1)} collective-permute-done((f32[2,128]{1,0:T(2,128)S(1)}, f32[2,128]{1,0:T(2,128)S(1)}, u32[]{:S(2)}, u32[]{:S(2)}) %collective-permute-start.4) | collective-permute-done | bytes 1056 | tf_op jit(solution)/shard_map/ppermute | solution.py:522
  55.8 0.7 norm_kernel.1
  56.5 0.0 copy-start.9
  56.5 1.8 %collective-permute-start.5 = (f32[576,128]{1,0:T(8,128)S(1)}, f32[576,128]{1,0:T(8,128)S(1)}, u32[]{:S(2)}, u32[]{:S(2)}) collective-permute-start(f32[576,128]{1,0:T(8,128)S(1)} %get-tuple-element.46), channel_id=1, source_target_pairs={{0,4},{4,0},{1,5},{5,1},{2,6},{6,2},{3,7},{7,3},{8,12},{12,8},{9,1... | collective-permute-start | bytes 884744 | tf_op jit(solution)/shard_map/ppermute | solution.py:512
  58.4 0.5 carry_keep_kernel.1.own_ref.c_ref
  58.8 0.7 collective-permute-done.5.got_ref.got_c_ref
  59.6 0.8 combine_backward_kernel.1
  60.3 4.5 %all-to-all-start.2 = ((f32[32,9,2,128]{3,2,1,0:T(2,128)}), f32[32,9,2,128]{3,2,1,0:T(2,128)S(1)}, u32[]{:S(2)}, u32[]{:S(2)}) async-start(f32[32,9,2,128]{3,2,1,0:T(2,128)} %bitcast.5), calls=%async_computation.2 | async-start | bytes 589824 | tf_op jit(solution)/shard_map/all_to_all | solution.py:518
  64.8 0.0 copy-start.10
  64.8 1.0 %copy-done.10 = bf16[128,1536]{1,0:T(8,128)(2,1)S(1)} copy-done((bf16[128,1536]{1,0:T(8,128)(2,1)S(1)}, bf16[128,1536]{1,0:T(8,128)(2,1)}, u32[]{:S(2)}) %copy-start.10) | copy-done | bytes 393240
  65.8 0.9 values_own_kernel.1
  66.7 0.1 copy-done.4
  66.8 0.1 copy-done.7
  66.9 0.1 copy-done.11
  67.0 3.9 %middle_kernel.1 = (bf16[128,1536]{1,0:T(8,128)(2,1)}, f32[128,768]{1,0:T(8,128)S(1)}, f32[128,768]{1,0:T(8,128)S(1)}, f32[8,128]{1,0:T(8,128)S(1)}) custom-call(s32[1]{0:T(128)} %bitcast.core_ref, bf16[128,1536]{1,0:T(8,128)(2,1)S(1)} %copy-done.4, bf16[256,1536]{1,0:T(8,128)(2,1)S(1)} %pad_maximum_fusion.kv_ref, bf16[128,1536]{1,0:T(8,128)(2,1)S(1)} %copy-done.11, ...), custom_call_target="tpu_custom_call" | custom-call | flops 4000000000 | bytes 3653636 | tf_op jit(solution)/shard_map/middle_kernel/pallas_call | solution.py:493
  70.9 0.7 copy-done
  71.6 4.1 %all-to-all-done.2 = f32[32,9,2,128]{3,2,1,0:T(2,128)S(1)} async-done(((f32[32,9,2,128]{3,2,1,0:T(2,128)}), f32[32,9,2,128]{3,2,1,0:T(2,128)S(1)}, u32[]{:S(2)}, u32[]{:S(2)}) %all-to-all-start.2) | async-done | bytes 294944 | tf_op jit(solution)/shard_map/all_to_all | solution.py:518
  75.7 0.1 scan_backward_kernel.1
  75.8 0.0 copy-start.5
  75.8 0.0 copy-start.12
  75.8 15.2 %all_to_all.26 = f32[32,9,2,128]{3,2,1,0:T(2,128)S(1)} all-to-all(f32[32,9,2,128]{3,2,1,0:T(2,128)S(1)} %bitcast.17), channel_id=1, replica_groups=mesh['xh'=2,'xl'=2,'zh'=2,'zm'=2,'zl'=2,'core'=2,'head'=4] {'zm','zh','x..., dimensions={0} | all-to-all | bytes 589824 | tf_op jit(solution)/shard_map/all_to_all | solution.py:518
  91.0 0.1 step_backward_kernel.1
  91.0 0.0 copy-start.1
  91.0 3.9 %collective-permute-start.6 = (f32[576,128]{1,0:T(8,128)S(1)}, f32[576,128]{1,0:T(8,128)S(1)}, u32[]{:S(2)}, u32[]{:S(2)}) collective-permute-start(f32[576,128]{1,0:T(8,128)S(1)} %step_backward_kernel.1), channel_id=1, source_target_pairs={{0,4},{4,0},{1,5},{5,1},{2,6},{6,2},{3,7},{7,3},{8,12},{12,8},{9,1... | collective-permute-start | bytes 884744 | tf_op jit(solution)/shard_map/ppermute | solution.py:512
  95.0 0.9 values_other_kernel.1.gv0_ref
  95.9 0.7 last_own_kernel.1
  96.5 1.4 %last_other_kernel.1 = (bf16[128,1536]{1,0:T(8,128)(2,1)}, bf16[128,1536]{1,0:T(8,128)(2,1)}) custom-call(s32[1]{0:T(128)} %bitcast.core_ref, bf16[256,1536]{1,0:T(8,128)(2,1)S(1)} %pad_maximum_fusion.kv_ref, f32[128,128]{1,0:T(8,128)S(1)} %get-tuple-element.44.tail_ref, f32[128,768]{1,0:T(8,128)S(1)} %get-tuple-element.45.gk0_ref, ...), custom_call_target="tpu_custom_call" | custom-call | flops 500000000 | bytes 3112964 | tf_op jit(solution)/shard_map/last_other_kernel/pallas_call | solution.py:493
  (18 shorter events, 0.1 us)
Async XLA Ops:
  0.6 1.2 %copy-start.8 = (f32[16,128]{1,0:T(8,128)S(1)}, f32[16,128]{1,0:T(8,128)}, u32[]{:S(2)}) copy-start(f32[16,128]{1,0:T(8,128)} %logs_ref) | copy-start | bytes 24580
  2.5 4.5 %collective-permute-start = (f32[584,128]{1,0:T(8,128)S(1)}, f32[584,128]{1,0:T(8,128)S(1)}, u32[]{:S(2)}, u32[]{:S(2)}) collective-permute-start(f32[584,128]{1,0:T(8,128)S(1)} %get-tuple-element.37), channel_id=1, source_target_pairs={{0,4},{4,0},{1,5},{5,1},{2,6},{6,2},{3,7},{7,3},{8,12},{12,8},{9,1... | collective-permute-start | bytes 897032 | tf_op jit(solution)/shard_map/ppermute | solution.py:512
  27.6 19.3 %copy-start.13 = (f32[1536]{0:T(1024)S(1)}, f32[1536]{0:T(1024)}, u32[]{:S(2)}) copy-start(f32[1536]{0:T(1024)} %param.11) | copy-start | bytes 18436
  27.6 19.3 %copy-start.3 = (bf16[128,1536]{1,0:T(8,128)(2,1)S(1)}, bf16[128,1536]{1,0:T(8,128)(2,1)}, u32[]{:S(2)}) copy-start(bf16[128,1536]{1,0:T(8,128)(2,1)} %q_ref.13) | copy-start | bytes 1179652
  42.8 5.7 %collective-permute-start.1 = (f32[576,128]{1,0:T(8,128)S(1)}, f32[576,128]{1,0:T(8,128)S(1)}, u32[]{:S(2)}, u32[]{:S(2)}) collective-permute-start(f32[576,128]{1,0:T(8,128)S(1)} %step_forward_kernel.1), channel_id=1, source_target_pairs={{0,4},{4,0},{1,5},{5,1},{2,6},{6,2},{3,7},{7,3},{8,12},{12,8},{9,1... | collective-permute-start | bytes 884744 | tf_op jit(solution)/shard_map/ppermute | solution.py:512
  46.9 1.7 %copy-start.2 = (bf16[128,1536]{1,0:T(8,128)(2,1)S(1)}, bf16[128,1536]{1,0:T(8,128)(2,1)}, u32[]{:S(2)}) copy-start(bf16[128,1536]{1,0:T(8,128)(2,1)} %y_ref.3) | copy-start | bytes 1179652
  48.5 0.9 copy-start.6
  49.4 5.1 %collective-permute-start.2 = (f32[2,128]{1,0:T(2,128)S(1)}, f32[2,128]{1,0:T(2,128)S(1)}, u32[]{:S(2)}, u32[]{:S(2)}) collective-permute-start(f32[2,128]{1,0:T(2,128)S(1)} %get-tuple-element.41.sums_0), channel_id=1, source_target_pairs={{0,1},{1,2},{2,3},{3,0},{4,5},{5,6},{6,7},{7,4},{8,9},{9,10},{10,1... | collective-permute-start | bytes 3080 | tf_op jit(solution)/shard_map/ppermute | solution.py:522
  50.8 3.9 %collective-permute-start.3 = (f32[2,128]{1,0:T(2,128)S(1)}, f32[2,128]{1,0:T(2,128)S(1)}, u32[]{:S(2)}, u32[]{:S(2)}) collective-permute-start(f32[2,128]{1,0:T(2,128)S(1)} %get-tuple-element.41.sums_0), channel_id=1, source_target_pairs={{0,2},{1,3},{2,0},{3,1},{4,6},{5,7},{6,4},{7,5},{8,10},{9,11},{10,... | collective-permute-start | bytes 3080 | tf_op jit(solution)/shard_map/ppermute | solution.py:522
  53.4 2.4 %collective-permute-start.4 = (f32[2,128]{1,0:T(2,128)S(1)}, f32[2,128]{1,0:T(2,128)S(1)}, u32[]{:S(2)}, u32[]{:S(2)}) collective-permute-start(f32[2,128]{1,0:T(2,128)S(1)} %get-tuple-element.41.sums_0), channel_id=1, source_target_pairs={{0,3},{1,0},{2,1},{3,2},{4,7},{5,4},{6,5},{7,6},{8,11},{9,8},{10,9... | collective-permute-start | bytes 3080 | tf_op jit(solution)/shard_map/ppermute | solution.py:522
  56.5 2.3 %copy-start.9 = (bf16[128,1536]{1,0:T(8,128)(2,1)}, bf16[128,1536]{1,0:T(8,128)(2,1)S(1)}, u32[]{:S(2)}) copy-start(bf16[128,1536]{1,0:T(8,128)(2,1)S(1)} %get-tuple-element.42.back_ref) | copy-start | bytes 1179652
  56.5 3.0 %collective-permute-start.5 = (f32[576,128]{1,0:T(8,128)S(1)}, f32[576,128]{1,0:T(8,128)S(1)}, u32[]{:S(2)}, u32[]{:S(2)}) collective-permute-start(f32[576,128]{1,0:T(8,128)S(1)} %get-tuple-element.46), channel_id=1, source_target_pairs={{0,4},{4,0},{1,5},{5,1},{2,6},{6,2},{3,7},{7,3},{8,12},{12,8},{9,1... | collective-permute-start | bytes 884744 | tf_op jit(solution)/shard_map/ppermute | solution.py:512
  60.3 15.4 %all-to-all-start.2 = ((f32[32,9,2,128]{3,2,1,0:T(2,128)}), f32[32,9,2,128]{3,2,1,0:T(2,128)S(1)}, u32[]{:S(2)}, u32[]{:S(2)}) async-start(f32[32,9,2,128]{3,2,1,0:T(2,128)} %bitcast.5), calls=%async_computation.2 | async-start | bytes 589824 | tf_op jit(solution)/shard_map/all_to_all | solution.py:518
  64.8 1.0 %copy-start.10 = (bf16[128,1536]{1,0:T(8,128)(2,1)S(1)}, bf16[128,1536]{1,0:T(8,128)(2,1)}, u32[]{:S(2)}) copy-start(bf16[128,1536]{1,0:T(8,128)(2,1)} %copy-done.9) | copy-start | bytes 1179652
  65.8 1.0 %copy-start.4 = (bf16[128,1536]{1,0:T(8,128)(2,1)S(1)}, bf16[128,1536]{1,0:T(8,128)(2,1)}, u32[]{:S(2)}) copy-start(bf16[128,1536]{1,0:T(8,128)(2,1)} %q_ref.13) | copy-start | bytes 1179652
  65.8 1.1 %copy-start.7 = (f32[576,128]{1,0:T(8,128)S(1)}, f32[576,128]{1,0:T(8,128)}, u32[]{:S(2)}) copy-start(f32[576,128]{1,0:T(8,128)} %copy-done.6) | copy-start | bytes 884740
  65.8 1.2 %copy-start.11 = (bf16[128,1536]{1,0:T(8,128)(2,1)S(1)}, bf16[128,1536]{1,0:T(8,128)(2,1)}, u32[]{:S(2)}) copy-start(bf16[128,1536]{1,0:T(8,128)(2,1)} %copy-done.9) | copy-start | bytes 1179652
  70.9 0.7 copy-start
  75.8 19.2 %copy-start.5 = (bf16[128,1536]{1,0:T(8,128)(2,1)S(1)}, bf16[128,1536]{1,0:T(8,128)(2,1)}, u32[]{:S(2)}) copy-start(bf16[128,1536]{1,0:T(8,128)(2,1)} %q_ref.13) | copy-start | bytes 1179652
  75.8 19.2 %copy-start.12 = (bf16[128,1536]{1,0:T(8,128)(2,1)S(1)}, bf16[128,1536]{1,0:T(8,128)(2,1)}, u32[]{:S(2)}) copy-start(bf16[128,1536]{1,0:T(8,128)(2,1)} %copy-done.9) | copy-start | bytes 1179652
  91.0 4.8 %copy-start.1 = (f32[128,768]{1,0:T(8,128)S(1)}, f32[128,768]{1,0:T(8,128)}, u32[]{:S(2)}) copy-start(f32[128,768]{1,0:T(8,128)} %copy-done) | copy-start | bytes 1179652
  91.0 5.5 %collective-permute-start.6 = (f32[576,128]{1,0:T(8,128)S(1)}, f32[576,128]{1,0:T(8,128)S(1)}, u32[]{:S(2)}, u32[]{:S(2)}) collective-permute-start(f32[576,128]{1,0:T(8,128)S(1)} %step_backward_kernel.1), channel_id=1, source_target_pairs={{0,4},{4,0},{1,5},{5,1},{2,6},{6,2},{3,7},{7,3},{8,12},{12,8},{9,1... | collective-permute-start | bytes 884744 | tf_op jit(solution)/shard_map/ppermute | solution.py:512

commit v6 on v5

--- a/solution.py
+++ b/solution.py
@@ -297,11 +297,10 @@
     return at_lanes(384 * (2 * half + i), 0, 384)
 
 
-def inner_half(half, q_ref, kv_ref, accum_ref, inner_ref, start_ref, tail_ref):
+def inner_half(half, q_ref, kv_ref, accum_ref, inner_ref, start_ref):
     accum = half_rows(accum_ref, half)
     cols = columns(accum)
     start_ref[...] = jnp.exp(cols)
-    tail_ref[...] = columns(jnp.exp(accum[:, LANES - 1 :] - accum))
     k_ref, v_ref = keys_of(kv_ref), values_of(kv_ref)
     for i in range(2):
         g = 2 * half + i
@@ -316,11 +315,11 @@
 
 def inner_kernel(
     core_ref, q_ref, kv_ref, accum_ref,
-    own_inner_ref, own_start_ref, own_tail_ref, inner_ref, start_ref, tail_ref,
+    own_inner_ref, own_start_ref, inner_ref, start_ref,
 ):
     core = core_ref[0]
-    inner_half(core, q_ref, kv_ref, accum_ref, own_inner_ref, own_start_ref, own_tail_ref)
-    inner_half(1 - core, q_ref, kv_ref, accum_ref, inner_ref, start_ref, tail_ref)
+    inner_half(core, q_ref, kv_ref, accum_ref, own_inner_ref, own_start_ref)
+    inner_half(1 - core, q_ref, kv_ref, accum_ref, inner_ref, start_ref)
 
 
 def attention_half(half, q_ref, y_ref, gain_ref, start_ref, inner_ref, state_ref, o_ref, squares, crossed):
@@ -380,8 +379,9 @@
     outer_states(half, q_ref, jnp.exp(half_rows(accum_ref, half)), back_ref, c_ref)
 
 
-def middle_half(half, q_ref, kv_ref, back_ref, accum_ref, state_ref, gq_ref, gk_ref):
+def middle_half(half, q_ref, kv_ref, back_ref, accum_ref, state_ref, gq_ref, gk_ref, tail_ref):
     accum = half_rows(accum_ref, half)
+    tail_ref[...] = columns(jnp.exp(accum[:, LANES - 1 :] - accum))
     cols = columns(accum)
     start = jnp.exp(cols)
     k_ref, v_ref = keys_of(kv_ref), values_of(kv_ref)
@@ -408,13 +408,13 @@
 
 def middle_kernel(
     core_ref, q_ref, kv_ref, back_ref, accum_ref, own_ref, got_x_ref, other_state_ref,
-    gq_ref, own_gk_ref, other_gk_ref, done_ref, own_state_ref,
+    gq_ref, own_gk_ref, other_gk_ref, own_tail_ref, tail_ref, done_ref, own_state_ref,
 ):
     done_ref[...] = accum_ref[0:8, :]
     core = core_ref[0]
     own_states(core, 1, own_ref, got_x_ref, got_x_ref, own_state_ref)
-    middle_half(core, q_ref, kv_ref, back_ref, accum_ref, own_state_ref, gq_ref, own_gk_ref)
-    middle_half(1 - core, q_ref, kv_ref, back_ref, accum_ref, other_state_ref, gq_ref, other_gk_ref)
+    middle_half(core, q_ref, kv_ref, back_ref, accum_ref, own_state_ref, gq_ref, own_gk_ref, own_tail_ref)
+    middle_half(1 - core, q_ref, kv_ref, back_ref, accum_ref, other_state_ref, gq_ref, other_gk_ref, tail_ref)
 
 
 def values_half(half, q_ref, kv_ref, back_ref, accum_ref, gv_ref):
@@ -544,8 +544,8 @@
     entering, decays = call(scan_forward_kernel, [half, ((CHIPS, LANES), F32)], 0, payload)
     entering = exchange(entering)
     got_entering = swap(call(step_forward_kernel, [half], 1, core, entering, x_keep))
-    own_inner, own_start, own_tail, inner, start, tail = call(
-        inner_kernel, [half_wide, cols, cols, half_wide, cols, cols], 1, core, q, kv, accum, flops=2 * 10**9
+    own_inner, own_start, inner, start = call(
+        inner_kernel, [half_wide, cols, half_wide, cols], 1, core, q, kv, accum, flops=2 * 10**9
     )
     half_scratch = pltpu.VMEM((HALF_ROWS, LANES), F32)
     own_o, other_o, sums = call(
@@ -566,9 +566,9 @@
     own_gv, values_done = call(values_own_kernel, [half_wide, token], 1, core, q, kv, back, accum, flops=10**9)
     payload = call(combine_backward_kernel, [half], 1, core, c_keep, got_c, x_keep, got_x)
     payload = exchange(payload)
-    gq, own_gk, other_gk, middle_done = call(
+    gq, own_gk, other_gk, own_tail, tail, middle_done = call(
         middle_kernel,
-        [(wide, BF16), half_wide, half_wide, token],
+        [(wide, BF16), half_wide, half_wide, cols, cols, token],
         1, core, q, kv, back, accum, entering, got_x, got_entering,
         scratch=[half_scratch],
         flops=4 * 10**9,

time: 98.5 us -> 98.5 us (level)
  no operation moved by 1% of the time
where the time goes in v6:
time: 98.5 us; the launch traced here: 98.1 us
  blocking collectives  50.8 us (52%)
  starting transfers between devices  22.6 us (23%)
  Pallas kernels  13.4 us (14%)
  waiting for transfers between devices  6.89 us (7%)
  local copies, waits for them, and re-layouts  2.13 us (2%)
  other arithmetic  1.17 us (1%)
  between operations  1.02 us (1%)
    all_to_all x3, blocking collectives, exchange(): lax.all_to_all(parts, EXCHANGE, 0, 0, tiled=True).reshape(value.shape)  50.8 us
    pallas_call x17, Pallas kernels, call(): pl.pallas_call(kernel, out_shape=shapes, in_specs=specs, out_specs=[pl.Bl...  13.4 us
    ppermute x4, starting transfers between devices, swap(): return lax.ppermute(value, 'core', SWAP)  13.1 us
    ppermute x3, starting transfers between devices, others(): lax.ppermute(value, 'head', [(i, (i + k) % 4) for i in range(4)])  5.06 us
    all_to_all x1, starting transfers between devices, exchange(): lax.all_to_all(parts, EXCHANGE, 0, 0, tiled=True).reshape(value.shape)  4.47 us
    all_to_all x1, waiting for transfers between devices, exchange(): lax.all_to_all(parts, EXCHANGE, 0, 0, tiled=True).reshape(value.shape)  4.05 us
    unnamed x28, local copies, waits for them, and re-layouts  2.13 us
  transfers between devices with their start and end apart: 8, of which 5 were waited for; matrix products, arithmetic and copies ran while one was open for 0% of the time, Pallas kernels for 9%

profile of v6, /device:TPU:1, one launch (start us, length us, event | category | flops | bytes accessed | tf_op | source)
XLA Modules:
  0.0 98.1 jit_solution(3147236904958330468)
XLA Ops:
  0.6 1.2 %pad_maximum_fusion.kv_ref = bf16[256,1536]{1,0:T(8,128)(2,1)S(1)} fusion(bf16[128,1536]{1,0:T(8,128)(2,1)} %param.8, bf16[128,1536]{1,0:T(8,128)(2,1)} %param.7), kind=kLoop, calls=%fused_computation | loop fusion | flops 1572864 | bytes 1572864 | tf_op jit(solution)/shard_map/concatenate | solution.py:536
  1.8 0.7 state_send_kernel.1
  2.5 3.3 %collective-permute-start = (f32[584,128]{1,0:T(8,128)S(1)}, f32[584,128]{1,0:T(8,128)S(1)}, u32[]{:S(2)}, u32[]{:S(2)}) collective-permute-start(f32[584,128]{1,0:T(8,128)S(1)} %get-tuple-element.37), channel_id=1, source_target_pairs={{0,4},{4,0},{1,5},{5,1},{2,6},{6,2},{3,7},{7,3},{8,12},{12,8},{9,1... | collective-permute-start | bytes 897032 | tf_op jit(solution)/shard_map/ppermute | solution.py:512
  5.8 0.5 state_keep_kernel.1.own_ref.x_ref.own_x_ref
  6.3 0.8 collective-permute-done.got_ref.got_x_ref
  7.0 0.1 combine_forward_kernel.1
  7.1 20.4 %all_to_all.24 = f32[32,2432,1]{1,2,0:T(1,128)S(1)} all-to-all(f32[32,2432,1]{1,2,0:T(1,128)S(1)} %bitcast.12), channel_id=1, replica_groups=mesh['xh'=2,'xl'=2,'zh'=2,'zm'=2,'zl'=2,'core'=2,'head'=4] {'zm','zh','x..., dimensions={0} | all-to-all | bytes 622592 | tf_op jit(solution)/shard_map/all_to_all | solution.py:518
  27.5 0.1 scan_forward_kernel.1
  27.6 0.0 copy-start.13
  27.6 0.0 copy-start.3
  27.6 15.2 %all_to_all.25 = f32[32,9,2,128]{3,2,1,0:T(2,128)S(1)} all-to-all(f32[32,9,2,128]{3,2,1,0:T(2,128)S(1)} %bitcast.18), channel_id=1, replica_groups=mesh['xh'=2,'xl'=2,'zh'=2,'zm'=2,'zl'=2,'core'=2,'head'=4] {'zm','zh','x..., dimensions={0} | all-to-all | bytes 589824 | tf_op jit(solution)/shard_map/all_to_all | solution.py:518
  42.8 4.0 %collective-permute-start.1 = (f32[576,128]{1,0:T(8,128)S(1)}, f32[576,128]{1,0:T(8,128)S(1)}, u32[]{:S(2)}, u32[]{:S(2)}) collective-permute-start(f32[576,128]{1,0:T(8,128)S(1)} %step_forward_kernel.1), channel_id=1, source_target_pairs={{0,4},{4,0},{1,5},{5,1},{2,6},{6,2},{3,7},{7,3},{8,12},{12,8},{9,1... | collective-permute-start | bytes 884744 | tf_op jit(solution)/shard_map/ppermute | solution.py:512
  46.9 0.0 copy-start.2
  46.9 1.6 %inner_kernel.1 = (f32[128,768]{1,0:T(8,128)S(1)}, f32[128,128]{1,0:T(8,128)S(1)}, f32[128,768]{1,0:T(8,128)S(1)}, f32[128,128]{1,0:T(8,128)S(1)}) custom-call(s32[1]{0:T(128)} %bitcast.core_ref, bf16[128,1536]{1,0:T(8,128)(2,1)S(1)} %copy-done.3, bf16[256,1536]{1,0:T(8,128)(2,1)S(1)} %pad_maximum_fusion.kv_ref, f32[16,128]{1,0:T(8,128)S(1)} %get-tuple-element.32.accum_ref), custom_call_target="tpu_custom_call" | custom-call | flops 2000000000 | bytes 2105348 | tf_op jit(solution)/shard_map/inner_kernel/pallas_call | solution.py:493
  48.5 0.0 collective-permute-done.1.got_ref.other_state_ref
  48.5 0.0 copy-start.6
  48.5 0.8 attention_kernel.1
  49.4 1.4 %collective-permute-start.2 = (f32[2,128]{1,0:T(2,128)S(1)}, f32[2,128]{1,0:T(2,128)S(1)}, u32[]{:S(2)}, u32[]{:S(2)}) collective-permute-start(f32[2,128]{1,0:T(2,128)S(1)} %get-tuple-element.41.sums_0), channel_id=1, source_target_pairs={{0,1},{1,2},{2,3},{3,0},{4,5},{5,6},{6,7},{7,4},{8,9},{9,10},{10,1... | collective-permute-start | bytes 3080 | tf_op jit(solution)/shard_map/ppermute | solution.py:522
  50.7 2.6 %collective-permute-start.3 = (f32[2,128]{1,0:T(2,128)S(1)}, f32[2,128]{1,0:T(2,128)S(1)}, u32[]{:S(2)}, u32[]{:S(2)}) collective-permute-start(f32[2,128]{1,0:T(2,128)S(1)} %get-tuple-element.41.sums_0), channel_id=1, source_target_pairs={{0,2},{1,3},{2,0},{3,1},{4,6},{5,7},{6,4},{7,5},{8,10},{9,11},{10,... | collective-permute-start | bytes 3080 | tf_op jit(solution)/shard_map/ppermute | solution.py:522
  53.4 1.1 %collective-permute-start.4 = (f32[2,128]{1,0:T(2,128)S(1)}, f32[2,128]{1,0:T(2,128)S(1)}, u32[]{:S(2)}, u32[]{:S(2)}) collective-permute-start(f32[2,128]{1,0:T(2,128)S(1)} %get-tuple-element.41.sums_0), channel_id=1, source_target_pairs={{0,3},{1,0},{2,1},{3,2},{4,7},{5,4},{6,5},{7,6},{8,11},{9,8},{10,9... | collective-permute-start | bytes 3080 | tf_op jit(solution)/shard_map/ppermute | solution.py:522
  54.4 0.2 collective-permute-done.3.sums_2
  54.7 1.1 %collective-permute-done.4.sums_3 = f32[2,128]{1,0:T(2,128)S(1)} collective-permute-done((f32[2,128]{1,0:T(2,128)S(1)}, f32[2,128]{1,0:T(2,128)S(1)}, u32[]{:S(2)}, u32[]{:S(2)}) %collective-permute-start.4) | collective-permute-done | bytes 1056 | tf_op jit(solution)/shard_map/ppermute | solution.py:522
  55.8 0.7 norm_kernel.1
  56.5 0.0 copy-start.9
  56.5 1.8 %collective-permute-start.5 = (f32[576,128]{1,0:T(8,128)S(1)}, f32[576,128]{1,0:T(8,128)S(1)}, u32[]{:S(2)}, u32[]{:S(2)}) collective-permute-start(f32[576,128]{1,0:T(8,128)S(1)} %get-tuple-element.46), channel_id=1, source_target_pairs={{0,4},{4,0},{1,5},{5,1},{2,6},{6,2},{3,7},{7,3},{8,12},{12,8},{9,1... | collective-permute-start | bytes 884744 | tf_op jit(solution)/shard_map/ppermute | solution.py:512
  58.3 0.5 carry_keep_kernel.1.own_ref.c_ref
  58.8 0.7 collective-permute-done.5.got_ref.got_c_ref
  59.5 0.8 combine_backward_kernel.1
  60.3 4.5 %all-to-all-start.2 = ((f32[32,9,2,128]{3,2,1,0:T(2,128)}), f32[32,9,2,128]{3,2,1,0:T(2,128)S(1)}, u32[]{:S(2)}, u32[]{:S(2)}) async-start(f32[32,9,2,128]{3,2,1,0:T(2,128)} %bitcast.5), calls=%async_computation.2 | async-start | bytes 589824 | tf_op jit(solution)/shard_map/all_to_all | solution.py:518
  64.8 0.0 copy-start.10
  64.8 1.0 %copy-done.10 = bf16[128,1536]{1,0:T(8,128)(2,1)S(1)} copy-done((bf16[128,1536]{1,0:T(8,128)(2,1)S(1)}, bf16[128,1536]{1,0:T(8,128)(2,1)}, u32[]{:S(2)}) %copy-start.10) | copy-done | bytes 393240
  65.8 0.9 values_own_kernel.1
  66.6 0.1 copy-done.4
  66.8 0.1 copy-done.7
  66.9 0.1 copy-done.11
  67.0 3.9 %middle_kernel.1 = (bf16[128,1536]{1,0:T(8,128)(2,1)}, f32[128,768]{1,0:T(8,128)S(1)}, f32[128,768]{1,0:T(8,128)S(1)}, f32[128,128]{1,0:T(8,128)S(1)}, f32[128,128]{1,0:T(8,128)S(1)}, /*index=5*/f32[8,128]{1,0:T(8,128)S(1)}) custom-call(s32[1]{0:T(128)} %bitcast.core_ref, bf16[128,1536]{1,0:T(8,128)(2,1)S(1)} %copy-done.4, ...), custom_call_target="tpu_custom_call" | custom-call | flops 4000000000 | bytes 3784708 | tf_op jit(solution)/shard_map/middle_kernel/pallas_call | solution.py:493
  70.9 0.7 copy-done
  71.6 4.1 %all-to-all-done.2 = f32[32,9,2,128]{3,2,1,0:T(2,128)S(1)} async-done(((f32[32,9,2,128]{3,2,1,0:T(2,128)}), f32[32,9,2,128]{3,2,1,0:T(2,128)S(1)}, u32[]{:S(2)}, u32[]{:S(2)}) %all-to-all-start.2) | async-done | bytes 294944 | tf_op jit(solution)/shard_map/all_to_all | solution.py:518
  75.7 0.1 scan_backward_kernel.1
  75.7 0.0 copy-start.5
  75.8 0.0 copy-start.12
  75.8 15.2 %all_to_all.26 = f32[32,9,2,128]{3,2,1,0:T(2,128)S(1)} all-to-all(f32[32,9,2,128]{3,2,1,0:T(2,128)S(1)} %bitcast.17), channel_id=1, replica_groups=mesh['xh'=2,'xl'=2,'zh'=2,'zm'=2,'zl'=2,'core'=2,'head'=4] {'zm','zh','x..., dimensions={0} | all-to-all | bytes 589824 | tf_op jit(solution)/shard_map/all_to_all | solution.py:518
  90.9 0.1 step_backward_kernel.1
  91.0 0.0 copy-start.1
  91.0 3.9 %collective-permute-start.6 = (f32[576,128]{1,0:T(8,128)S(1)}, f32[576,128]{1,0:T(8,128)S(1)}, u32[]{:S(2)}, u32[]{:S(2)}) collective-permute-start(f32[576,128]{1,0:T(8,128)S(1)} %step_backward_kernel.1), channel_id=1, source_target_pairs={{0,4},{4,0},{1,5},{5,1},{2,6},{6,2},{3,7},{7,3},{8,12},{12,8},{9,1... | collective-permute-start | bytes 884744 | tf_op jit(solution)/shard_map/ppermute | solution.py:512
  95.0 0.9 values_other_kernel.1.gv0_ref
  95.8 0.7 last_own_kernel.1
  96.5 1.4 %last_other_kernel.1 = (bf16[128,1536]{1,0:T(8,128)(2,1)}, bf16[128,1536]{1,0:T(8,128)(2,1)}) custom-call(s32[1]{0:T(128)} %bitcast.core_ref, bf16[256,1536]{1,0:T(8,128)(2,1)S(1)} %pad_maximum_fusion.kv_ref, f32[128,128]{1,0:T(8,128)S(1)} %get-tuple-element.44.tail_ref, f32[128,768]{1,0:T(8,128)S(1)} %get-tuple-element.45.gk0_ref, ...), custom_call_target="tpu_custom_call" | custom-call | flops 500000000 | bytes 3112964 | tf_op jit(solution)/shard_map/last_other_kernel/pallas_call | solution.py:493
  (18 shorter events, 0.1 us)
Async XLA Ops:
  0.6 1.2 %copy-start.8 = (f32[16,128]{1,0:T(8,128)S(1)}, f32[16,128]{1,0:T(8,128)}, u32[]{:S(2)}) copy-start(f32[16,128]{1,0:T(8,128)} %logs_ref) | copy-start | bytes 24580
  2.5 4.5 %collective-permute-start = (f32[584,128]{1,0:T(8,128)S(1)}, f32[584,128]{1,0:T(8,128)S(1)}, u32[]{:S(2)}, u32[]{:S(2)}) collective-permute-start(f32[584,128]{1,0:T(8,128)S(1)} %get-tuple-element.37), channel_id=1, source_target_pairs={{0,4},{4,0},{1,5},{5,1},{2,6},{6,2},{3,7},{7,3},{8,12},{12,8},{9,1... | collective-permute-start | bytes 897032 | tf_op jit(solution)/shard_map/ppermute | solution.py:512
  27.6 19.3 %copy-start.13 = (f32[1536]{0:T(1024)S(1)}, f32[1536]{0:T(1024)}, u32[]{:S(2)}) copy-start(f32[1536]{0:T(1024)} %param.11) | copy-start | bytes 18436
  27.6 19.3 %copy-start.3 = (bf16[128,1536]{1,0:T(8,128)(2,1)S(1)}, bf16[128,1536]{1,0:T(8,128)(2,1)}, u32[]{:S(2)}) copy-start(bf16[128,1536]{1,0:T(8,128)(2,1)} %q_ref.13) | copy-start | bytes 1179652
  42.8 5.6 %collective-permute-start.1 = (f32[576,128]{1,0:T(8,128)S(1)}, f32[576,128]{1,0:T(8,128)S(1)}, u32[]{:S(2)}, u32[]{:S(2)}) collective-permute-start(f32[576,128]{1,0:T(8,128)S(1)} %step_forward_kernel.1), channel_id=1, source_target_pairs={{0,4},{4,0},{1,5},{5,1},{2,6},{6,2},{3,7},{7,3},{8,12},{12,8},{9,1... | collective-permute-start | bytes 884744 | tf_op jit(solution)/shard_map/ppermute | solution.py:512
  46.9 1.6 %copy-start.2 = (bf16[128,1536]{1,0:T(8,128)(2,1)S(1)}, bf16[128,1536]{1,0:T(8,128)(2,1)}, u32[]{:S(2)}) copy-start(bf16[128,1536]{1,0:T(8,128)(2,1)} %y_ref.3) | copy-start | bytes 1179652
  48.5 0.9 copy-start.6
  49.4 5.1 %collective-permute-start.2 = (f32[2,128]{1,0:T(2,128)S(1)}, f32[2,128]{1,0:T(2,128)S(1)}, u32[]{:S(2)}, u32[]{:S(2)}) collective-permute-start(f32[2,128]{1,0:T(2,128)S(1)} %get-tuple-element.41.sums_0), channel_id=1, source_target_pairs={{0,1},{1,2},{2,3},{3,0},{4,5},{5,6},{6,7},{7,4},{8,9},{9,10},{10,1... | collective-permute-start | bytes 3080 | tf_op jit(solution)/shard_map/ppermute | solution.py:522
  50.7 3.9 %collective-permute-start.3 = (f32[2,128]{1,0:T(2,128)S(1)}, f32[2,128]{1,0:T(2,128)S(1)}, u32[]{:S(2)}, u32[]{:S(2)}) collective-permute-start(f32[2,128]{1,0:T(2,128)S(1)} %get-tuple-element.41.sums_0), channel_id=1, source_target_pairs={{0,2},{1,3},{2,0},{3,1},{4,6},{5,7},{6,4},{7,5},{8,10},{9,11},{10,... | collective-permute-start | bytes 3080 | tf_op jit(solution)/shard_map/ppermute | solution.py:522
  53.4 2.4 %collective-permute-start.4 = (f32[2,128]{1,0:T(2,128)S(1)}, f32[2,128]{1,0:T(2,128)S(1)}, u32[]{:S(2)}, u32[]{:S(2)}) collective-permute-start(f32[2,128]{1,0:T(2,128)S(1)} %get-tuple-element.41.sums_0), channel_id=1, source_target_pairs={{0,3},{1,0},{2,1},{3,2},{4,7},{5,4},{6,5},{7,6},{8,11},{9,8},{10,9... | collective-permute-start | bytes 3080 | tf_op jit(solution)/shard_map/ppermute | solution.py:522
  56.5 2.3 %copy-start.9 = (bf16[128,1536]{1,0:T(8,128)(2,1)}, bf16[128,1536]{1,0:T(8,128)(2,1)S(1)}, u32[]{:S(2)}) copy-start(bf16[128,1536]{1,0:T(8,128)(2,1)S(1)} %get-tuple-element.42.back_ref) | copy-start | bytes 1179652
  56.5 3.0 %collective-permute-start.5 = (f32[576,128]{1,0:T(8,128)S(1)}, f32[576,128]{1,0:T(8,128)S(1)}, u32[]{:S(2)}, u32[]{:S(2)}) collective-permute-start(f32[576,128]{1,0:T(8,128)S(1)} %get-tuple-element.46), channel_id=1, source_target_pairs={{0,4},{4,0},{1,5},{5,1},{2,6},{6,2},{3,7},{7,3},{8,12},{12,8},{9,1... | collective-permute-start | bytes 884744 | tf_op jit(solution)/shard_map/ppermute | solution.py:512
  60.3 15.4 %all-to-all-start.2 = ((f32[32,9,2,128]{3,2,1,0:T(2,128)}), f32[32,9,2,128]{3,2,1,0:T(2,128)S(1)}, u32[]{:S(2)}, u32[]{:S(2)}) async-start(f32[32,9,2,128]{3,2,1,0:T(2,128)} %bitcast.5), calls=%async_computation.2 | async-start | bytes 589824 | tf_op jit(solution)/shard_map/all_to_all | solution.py:518
  64.8 1.0 %copy-start.10 = (bf16[128,1536]{1,0:T(8,128)(2,1)S(1)}, bf16[128,1536]{1,0:T(8,128)(2,1)}, u32[]{:S(2)}) copy-start(bf16[128,1536]{1,0:T(8,128)(2,1)} %copy-done.9) | copy-start | bytes 1179652
  65.8 1.0 %copy-start.4 = (bf16[128,1536]{1,0:T(8,128)(2,1)S(1)}, bf16[128,1536]{1,0:T(8,128)(2,1)}, u32[]{:S(2)}) copy-start(bf16[128,1536]{1,0:T(8,128)(2,1)} %q_ref.13) | copy-start | bytes 1179652
  65.8 1.1 %copy-start.7 = (f32[576,128]{1,0:T(8,128)S(1)}, f32[576,128]{1,0:T(8,128)}, u32[]{:S(2)}) copy-start(f32[576,128]{1,0:T(8,128)} %copy-done.6) | copy-start | bytes 884740
  65.8 1.2 %copy-start.11 = (bf16[128,1536]{1,0:T(8,128)(2,1)S(1)}, bf16[128,1536]{1,0:T(8,128)(2,1)}, u32[]{:S(2)}) copy-start(bf16[128,1536]{1,0:T(8,128)(2,1)} %copy-done.9) | copy-start | bytes 1179652
  70.9 0.7 copy-start
  75.7 19.2 %copy-start.5 = (bf16[128,1536]{1,0:T(8,128)(2,1)S(1)}, bf16[128,1536]{1,0:T(8,128)(2,1)}, u32[]{:S(2)}) copy-start(bf16[128,1536]{1,0:T(8,128)(2,1)} %q_ref.13) | copy-start | bytes 1179652
  75.8 19.2 %copy-start.12 = (bf16[128,1536]{1,0:T(8,128)(2,1)S(1)}, bf16[128,1536]{1,0:T(8,128)(2,1)}, u32[]{:S(2)}) copy-start(bf16[128,1536]{1,0:T(8,128)(2,1)} %copy-done.9) | copy-start | bytes 1179652
  91.0 4.8 %copy-start.1 = (f32[128,768]{1,0:T(8,128)S(1)}, f32[128,768]{1,0:T(8,128)}, u32[]{:S(2)}) copy-start(f32[128,768]{1,0:T(8,128)} %copy-done) | copy-start | bytes 1179652
  91.0 5.5 %collective-permute-start.6 = (f32[576,128]{1,0:T(8,128)S(1)}, f32[576,128]{1,0:T(8,128)S(1)}, u32[]{:S(2)}, u32[]{:S(2)}) collective-permute-start(f32[576,128]{1,0:T(8,128)S(1)} %step_backward_kernel.1), channel_id=1, source_target_pairs={{0,4},{4,0},{1,5},{5,1},{2,6},{6,2},{3,7},{7,3},{8,12},{12,8},{9,1... | collective-permute-start | bytes 884744 | tf_op jit(solution)/shard_map/ppermute | solution.py:512

commit v7 on v6

--- a/solution.py
+++ b/solution.py
@@ -519,7 +519,7 @@
 
 
 def others(value):
-    return [lax.ppermute(value, "head", [(i, (i + k) % 4) for i in range(4)]) for k in (1, 2, 3)]
+    return [lax.ppermute(value, "head", [(i, i ^ k) for i in range(4)]) for k in (2, 1, 3)]
 
 
 def local(q, k, v, y, logs, gain):

time: 98.5 us -> 98.9 us (level)
  waiting for transfers between devices: 6.89 us -> 8.97 us
  starting transfers between devices: 22.6 us -> 21.2 us
    ppermute x3, waiting for transfers between devices: 1.35 us -> 3.25 us  [others(): lax.ppermute(value, 'head', [(i, i ^ k) for i in range(4)])]
    ppermute x3, starting transfers between devices: 5.06 us -> 3.78 us  [others(): lax.ppermute(value, 'head', [(i, i ^ k) for i in range(4)])]
  transfers between devices with their start and end apart: 8 -> 8, of which waited for: 5 -> 6; matrix products, arithmetic and copies ran while one was open for 0% -> 0% of each run, Pallas kernels for 9% -> 9%
where the time goes in v7:
time: 98.9 us; the launch traced here: 98.5 us
  blocking collectives  50.8 us (51%)
  starting transfers between devices  21.2 us (21%)
  Pallas kernels  13.4 us (14%)
  waiting for transfers between devices  8.97 us (9%)
  local copies, waits for them, and re-layouts  2.13 us (2%)
  other arithmetic  1.17 us (1%)
    all_to_all x3, blocking collectives, exchange(): lax.all_to_all(parts, EXCHANGE, 0, 0, tiled=True).reshape(value.shape)  50.8 us
    pallas_call x17, Pallas kernels, call(): pl.pallas_call(kernel, out_shape=shapes, in_specs=specs, out_specs=[pl.Bl...  13.4 us
    ppermute x4, starting transfers between devices, swap(): return lax.ppermute(value, 'core', SWAP)  13.1 us
    all_to_all x1, starting transfers between devices, exchange(): lax.all_to_all(parts, EXCHANGE, 0, 0, tiled=True).reshape(value.shape)  4.28 us
    all_to_all x1, waiting for transfers between devices, exchange(): lax.all_to_all(parts, EXCHANGE, 0, 0, tiled=True).reshape(value.shape)  4.24 us
    ppermute x3, starting transfers between devices, others(): lax.ppermute(value, 'head', [(i, i ^ k) for i in range(4)])  3.78 us
    ppermute x3, waiting for transfers between devices, others(): lax.ppermute(value, 'head', [(i, i ^ k) for i in range(4)])  3.25 us
    unnamed x28, local copies, waits for them, and re-layouts  2.13 us
  transfers between devices with their start and end apart: 8, of which 6 were waited for; matrix products, arithmetic and copies ran while one was open for 0% of the time, Pallas kernels for 9%

profile of v7, /device:TPU:1, one launch (start us, length us, event | category | flops | bytes accessed | tf_op | source)
XLA Modules:
  0.0 98.5 jit_solution(15343492480995184706)
XLA Ops:
  0.6 1.2 %pad_maximum_fusion.kv_ref = bf16[256,1536]{1,0:T(8,128)(2,1)S(1)} fusion(bf16[128,1536]{1,0:T(8,128)(2,1)} %param.8, bf16[128,1536]{1,0:T(8,128)(2,1)} %param.7), kind=kLoop, calls=%fused_computation | loop fusion | flops 1572864 | bytes 1572864 | tf_op jit(solution)/shard_map/concatenate | solution.py:536
  1.8 0.7 state_send_kernel.1
  2.5 3.3 %collective-permute-start = (f32[584,128]{1,0:T(8,128)S(1)}, f32[584,128]{1,0:T(8,128)S(1)}, u32[]{:S(2)}, u32[]{:S(2)}) collective-permute-start(f32[584,128]{1,0:T(8,128)S(1)} %get-tuple-element.37), channel_id=1, source_target_pairs={{0,4},{4,0},{1,5},{5,1},{2,6},{6,2},{3,7},{7,3},{8,12},{12,8},{9,1... | collective-permute-start | bytes 897032 | tf_op jit(solution)/shard_map/ppermute | solution.py:512
  5.8 0.5 state_keep_kernel.1.own_ref.x_ref.own_x_ref
  6.3 0.8 collective-permute-done.got_ref.got_x_ref
  7.0 0.1 combine_forward_kernel.1
  7.1 20.4 %all_to_all.24 = f32[32,2432,1]{1,2,0:T(1,128)S(1)} all-to-all(f32[32,2432,1]{1,2,0:T(1,128)S(1)} %bitcast.12), channel_id=1, replica_groups=mesh['xh'=2,'xl'=2,'zh'=2,'zm'=2,'zl'=2,'core'=2,'head'=4] {'zm','zh','x..., dimensions={0} | all-to-all | bytes 622592 | tf_op jit(solution)/shard_map/all_to_all | solution.py:518
  27.5 0.1 scan_forward_kernel.1
  27.6 0.0 copy-start.13
  27.6 0.0 copy-start.3
  27.6 15.2 %all_to_all.25 = f32[32,9,2,128]{3,2,1,0:T(2,128)S(1)} all-to-all(f32[32,9,2,128]{3,2,1,0:T(2,128)S(1)} %bitcast.18), channel_id=1, replica_groups=mesh['xh'=2,'xl'=2,'zh'=2,'zm'=2,'zl'=2,'core'=2,'head'=4] {'zm','zh','x..., dimensions={0} | all-to-all | bytes 589824 | tf_op jit(solution)/shard_map/all_to_all | solution.py:518
  42.8 4.0 %collective-permute-start.1 = (f32[576,128]{1,0:T(8,128)S(1)}, f32[576,128]{1,0:T(8,128)S(1)}, u32[]{:S(2)}, u32[]{:S(2)}) collective-permute-start(f32[576,128]{1,0:T(8,128)S(1)} %step_forward_kernel.1), channel_id=1, source_target_pairs={{0,4},{4,0},{1,5},{5,1},{2,6},{6,2},{3,7},{7,3},{8,12},{12,8},{9,1... | collective-permute-start | bytes 884744 | tf_op jit(solution)/shard_map/ppermute | solution.py:512
  46.9 0.0 copy-start.2
  46.9 1.6 %inner_kernel.1 = (f32[128,768]{1,0:T(8,128)S(1)}, f32[128,128]{1,0:T(8,128)S(1)}, f32[128,768]{1,0:T(8,128)S(1)}, f32[128,128]{1,0:T(8,128)S(1)}) custom-call(s32[1]{0:T(128)} %bitcast.core_ref, bf16[128,1536]{1,0:T(8,128)(2,1)S(1)} %copy-done.3, bf16[256,1536]{1,0:T(8,128)(2,1)S(1)} %pad_maximum_fusion.kv_ref, f32[16,128]{1,0:T(8,128)S(1)} %get-tuple-element.32.accum_ref), custom_call_target="tpu_custom_call" | custom-call | flops 2000000000 | bytes 2105348 | tf_op jit(solution)/shard_map/inner_kernel/pallas_call | solution.py:493
  48.5 0.0 copy-start.6
  48.5 0.8 attention_kernel.1
  49.4 3.0 %collective-permute-start.2 = (f32[2,128]{1,0:T(2,128)S(1)}, f32[2,128]{1,0:T(2,128)S(1)}, u32[]{:S(2)}, u32[]{:S(2)}) collective-permute-start(f32[2,128]{1,0:T(2,128)S(1)} %get-tuple-element.41.sums_0), channel_id=1, source_target_pairs={{0,2},{1,3},{2,0},{3,1},{4,6},{5,7},{6,4},{7,5},{8,10},{9,11},{10,... | collective-permute-start | bytes 3080 | tf_op jit(solution)/shard_map/ppermute | solution.py:522
  52.4 0.4 collective-permute-start.3
  52.8 0.4 collective-permute-start.4
  53.1 0.2 collective-permute-done.2.sums_1
  53.4 1.4 %collective-permute-done.3.sums_2 = f32[2,128]{1,0:T(2,128)S(1)} collective-permute-done((f32[2,128]{1,0:T(2,128)S(1)}, f32[2,128]{1,0:T(2,128)S(1)}, u32[]{:S(2)}, u32[]{:S(2)}) %collective-permute-start.3) | collective-permute-done | bytes 1056 | tf_op jit(solution)/shard_map/ppermute | solution.py:522
  54.8 1.6 %collective-permute-done.4.sums_3 = f32[2,128]{1,0:T(2,128)S(1)} collective-permute-done((f32[2,128]{1,0:T(2,128)S(1)}, f32[2,128]{1,0:T(2,128)S(1)}, u32[]{:S(2)}, u32[]{:S(2)}) %collective-permute-start.4) | collective-permute-done | bytes 1056 | tf_op jit(solution)/shard_map/ppermute | solution.py:522
  56.4 0.7 norm_kernel.1
  57.1 0.0 copy-start.9
  57.1 1.8 %collective-permute-start.5 = (f32[576,128]{1,0:T(8,128)S(1)}, f32[576,128]{1,0:T(8,128)S(1)}, u32[]{:S(2)}, u32[]{:S(2)}) collective-permute-start(f32[576,128]{1,0:T(8,128)S(1)} %get-tuple-element.46), channel_id=1, source_target_pairs={{0,4},{4,0},{1,5},{5,1},{2,6},{6,2},{3,7},{7,3},{8,12},{12,8},{9,1... | collective-permute-start | bytes 884744 | tf_op jit(solution)/shard_map/ppermute | solution.py:512
  59.0 0.5 carry_keep_kernel.1.own_ref.c_ref
  59.4 0.7 collective-permute-done.5.got_ref.got_c_ref
  60.2 0.8 combine_backward_kernel.1
  60.9 4.3 %all-to-all-start.2 = ((f32[32,9,2,128]{3,2,1,0:T(2,128)}), f32[32,9,2,128]{3,2,1,0:T(2,128)S(1)}, u32[]{:S(2)}, u32[]{:S(2)}) async-start(f32[32,9,2,128]{3,2,1,0:T(2,128)} %bitcast.5), calls=%async_computation.2 | async-start | bytes 589824 | tf_op jit(solution)/shard_map/all_to_all | solution.py:518
  65.2 0.0 copy-start.10
  65.2 1.0 %copy-done.10 = bf16[128,1536]{1,0:T(8,128)(2,1)S(1)} copy-done((bf16[128,1536]{1,0:T(8,128)(2,1)S(1)}, bf16[128,1536]{1,0:T(8,128)(2,1)}, u32[]{:S(2)}) %copy-start.10) | copy-done | bytes 393240
  66.2 0.9 values_own_kernel.1
  67.1 0.1 copy-done.4
  67.2 0.1 copy-done.7
  67.3 0.1 copy-done.11
  67.4 3.9 %middle_kernel.1 = (bf16[128,1536]{1,0:T(8,128)(2,1)}, f32[128,768]{1,0:T(8,128)S(1)}, f32[128,768]{1,0:T(8,128)S(1)}, f32[128,128]{1,0:T(8,128)S(1)}, f32[128,128]{1,0:T(8,128)S(1)}, /*index=5*/f32[8,128]{1,0:T(8,128)S(1)}) custom-call(s32[1]{0:T(128)} %bitcast.core_ref, bf16[128,1536]{1,0:T(8,128)(2,1)S(1)} %copy-done.4, ...), custom_call_target="tpu_custom_call" | custom-call | flops 4000000000 | bytes 3784708 | tf_op jit(solution)/shard_map/middle_kernel/pallas_call | solution.py:493
  71.3 0.7 copy-done
  72.0 4.2 %all-to-all-done.2 = f32[32,9,2,128]{3,2,1,0:T(2,128)S(1)} async-done(((f32[32,9,2,128]{3,2,1,0:T(2,128)}), f32[32,9,2,128]{3,2,1,0:T(2,128)S(1)}, u32[]{:S(2)}, u32[]{:S(2)}) %all-to-all-start.2) | async-done | bytes 294944 | tf_op jit(solution)/shard_map/all_to_all | solution.py:518
  76.3 0.1 scan_backward_kernel.1
  76.4 0.0 copy-start.5
  76.4 0.0 copy-start.12
  76.4 15.2 %all_to_all.26 = f32[32,9,2,128]{3,2,1,0:T(2,128)S(1)} all-to-all(f32[32,9,2,128]{3,2,1,0:T(2,128)S(1)} %bitcast.17), channel_id=1, replica_groups=mesh['xh'=2,'xl'=2,'zh'=2,'zm'=2,'zl'=2,'core'=2,'head'=4] {'zm','zh','x..., dimensions={0} | all-to-all | bytes 589824 | tf_op jit(solution)/shard_map/all_to_all | solution.py:518
  91.5 0.1 step_backward_kernel.1
  91.6 0.0 copy-start.1
  91.6 3.9 %collective-permute-start.6 = (f32[576,128]{1,0:T(8,128)S(1)}, f32[576,128]{1,0:T(8,128)S(1)}, u32[]{:S(2)}, u32[]{:S(2)}) collective-permute-start(f32[576,128]{1,0:T(8,128)S(1)} %step_backward_kernel.1), channel_id=1, source_target_pairs={{0,4},{4,0},{1,5},{5,1},{2,6},{6,2},{3,7},{7,3},{8,12},{12,8},{9,1... | collective-permute-start | bytes 884744 | tf_op jit(solution)/shard_map/ppermute | solution.py:512
  95.6 0.9 values_other_kernel.1.gv0_ref
  96.4 0.7 last_own_kernel.1
  97.1 1.4 %last_other_kernel.1 = (bf16[128,1536]{1,0:T(8,128)(2,1)}, bf16[128,1536]{1,0:T(8,128)(2,1)}) custom-call(s32[1]{0:T(128)} %bitcast.core_ref, bf16[256,1536]{1,0:T(8,128)(2,1)S(1)} %pad_maximum_fusion.kv_ref, f32[128,128]{1,0:T(8,128)S(1)} %get-tuple-element.44.tail_ref, f32[128,768]{1,0:T(8,128)S(1)} %get-tuple-element.45.gk0_ref, ...), custom_call_target="tpu_custom_call" | custom-call | flops 500000000 | bytes 3112964 | tf_op jit(solution)/shard_map/last_other_kernel/pallas_call | solution.py:493
  (18 shorter events, 0.1 us)
Async XLA Ops:
  0.6 1.2 %copy-start.8 = (f32[16,128]{1,0:T(8,128)S(1)}, f32[16,128]{1,0:T(8,128)}, u32[]{:S(2)}) copy-start(f32[16,128]{1,0:T(8,128)} %logs_ref) | copy-start | bytes 24580
  2.5 4.5 %collective-permute-start = (f32[584,128]{1,0:T(8,128)S(1)}, f32[584,128]{1,0:T(8,128)S(1)}, u32[]{:S(2)}, u32[]{:S(2)}) collective-permute-start(f32[584,128]{1,0:T(8,128)S(1)} %get-tuple-element.37), channel_id=1, source_target_pairs={{0,4},{4,0},{1,5},{5,1},{2,6},{6,2},{3,7},{7,3},{8,12},{12,8},{9,1... | collective-permute-start | bytes 897032 | tf_op jit(solution)/shard_map/ppermute | solution.py:512
  27.6 19.3 %copy-start.13 = (f32[1536]{0:T(1024)S(1)}, f32[1536]{0:T(1024)}, u32[]{:S(2)}) copy-start(f32[1536]{0:T(1024)} %param.11) | copy-start | bytes 18436
  27.6 19.3 %copy-start.3 = (bf16[128,1536]{1,0:T(8,128)(2,1)S(1)}, bf16[128,1536]{1,0:T(8,128)(2,1)}, u32[]{:S(2)}) copy-start(bf16[128,1536]{1,0:T(8,128)(2,1)} %q_ref.13) | copy-start | bytes 1179652
  42.8 5.6 %collective-permute-start.1 = (f32[576,128]{1,0:T(8,128)S(1)}, f32[576,128]{1,0:T(8,128)S(1)}, u32[]{:S(2)}, u32[]{:S(2)}) collective-permute-start(f32[576,128]{1,0:T(8,128)S(1)} %step_forward_kernel.1), channel_id=1, source_target_pairs={{0,4},{4,0},{1,5},{5,1},{2,6},{6,2},{3,7},{7,3},{8,12},{12,8},{9,1... | collective-permute-start | bytes 884744 | tf_op jit(solution)/shard_map/ppermute | solution.py:512
  46.9 1.6 %copy-start.2 = (bf16[128,1536]{1,0:T(8,128)(2,1)S(1)}, bf16[128,1536]{1,0:T(8,128)(2,1)}, u32[]{:S(2)}) copy-start(bf16[128,1536]{1,0:T(8,128)(2,1)} %y_ref.3) | copy-start | bytes 1179652
  48.5 0.9 copy-start.6
  49.4 4.0 %collective-permute-start.2 = (f32[2,128]{1,0:T(2,128)S(1)}, f32[2,128]{1,0:T(2,128)S(1)}, u32[]{:S(2)}, u32[]{:S(2)}) collective-permute-start(f32[2,128]{1,0:T(2,128)S(1)} %get-tuple-element.41.sums_0), channel_id=1, source_target_pairs={{0,2},{1,3},{2,0},{3,1},{4,6},{5,7},{6,4},{7,5},{8,10},{9,11},{10,... | collective-permute-start | bytes 3080 | tf_op jit(solution)/shard_map/ppermute | solution.py:522
  52.4 2.4 %collective-permute-start.3 = (f32[2,128]{1,0:T(2,128)S(1)}, f32[2,128]{1,0:T(2,128)S(1)}, u32[]{:S(2)}, u32[]{:S(2)}) collective-permute-start(f32[2,128]{1,0:T(2,128)S(1)} %get-tuple-element.41.sums_0), channel_id=1, source_target_pairs={{0,1},{1,0},{2,3},{3,2},{4,5},{5,4},{6,7},{7,6},{8,9},{9,8},{10,11... | collective-permute-start | bytes 3080 | tf_op jit(solution)/shard_map/ppermute | solution.py:522
  52.8 3.6 %collective-permute-start.4 = (f32[2,128]{1,0:T(2,128)S(1)}, f32[2,128]{1,0:T(2,128)S(1)}, u32[]{:S(2)}, u32[]{:S(2)}) collective-permute-start(f32[2,128]{1,0:T(2,128)S(1)} %get-tuple-element.41.sums_0), channel_id=1, source_target_pairs={{0,3},{1,2},{2,1},{3,0},{4,7},{5,6},{6,5},{7,4},{8,11},{9,10},{10,... | collective-permute-start | bytes 3080 | tf_op jit(solution)/shard_map/ppermute | solution.py:522
  57.1 2.3 %copy-start.9 = (bf16[128,1536]{1,0:T(8,128)(2,1)}, bf16[128,1536]{1,0:T(8,128)(2,1)S(1)}, u32[]{:S(2)}) copy-start(bf16[128,1536]{1,0:T(8,128)(2,1)S(1)} %get-tuple-element.42.back_ref) | copy-start | bytes 1179652
  57.1 3.0 %collective-permute-start.5 = (f32[576,128]{1,0:T(8,128)S(1)}, f32[576,128]{1,0:T(8,128)S(1)}, u32[]{:S(2)}, u32[]{:S(2)}) collective-permute-start(f32[576,128]{1,0:T(8,128)S(1)} %get-tuple-element.46), channel_id=1, source_target_pairs={{0,4},{4,0},{1,5},{5,1},{2,6},{6,2},{3,7},{7,3},{8,12},{12,8},{9,1... | collective-permute-start | bytes 884744 | tf_op jit(solution)/shard_map/ppermute | solution.py:512
  60.9 15.4 %all-to-all-start.2 = ((f32[32,9,2,128]{3,2,1,0:T(2,128)}), f32[32,9,2,128]{3,2,1,0:T(2,128)S(1)}, u32[]{:S(2)}, u32[]{:S(2)}) async-start(f32[32,9,2,128]{3,2,1,0:T(2,128)} %bitcast.5), calls=%async_computation.2 | async-start | bytes 589824 | tf_op jit(solution)/shard_map/all_to_all | solution.py:518
  65.2 1.0 %copy-start.10 = (bf16[128,1536]{1,0:T(8,128)(2,1)S(1)}, bf16[128,1536]{1,0:T(8,128)(2,1)}, u32[]{:S(2)}) copy-start(bf16[128,1536]{1,0:T(8,128)(2,1)} %copy-done.9) | copy-start | bytes 1179652
  66.2 1.0 %copy-start.4 = (bf16[128,1536]{1,0:T(8,128)(2,1)S(1)}, bf16[128,1536]{1,0:T(8,128)(2,1)}, u32[]{:S(2)}) copy-start(bf16[128,1536]{1,0:T(8,128)(2,1)} %q_ref.13) | copy-start | bytes 1179652
  66.2 1.1 %copy-start.7 = (f32[576,128]{1,0:T(8,128)S(1)}, f32[576,128]{1,0:T(8,128)}, u32[]{:S(2)}) copy-start(f32[576,128]{1,0:T(8,128)} %copy-done.6) | copy-start | bytes 884740
  66.2 1.2 %copy-start.11 = (bf16[128,1536]{1,0:T(8,128)(2,1)S(1)}, bf16[128,1536]{1,0:T(8,128)(2,1)}, u32[]{:S(2)}) copy-start(bf16[128,1536]{1,0:T(8,128)(2,1)} %copy-done.9) | copy-start | bytes 1179652
  71.3 0.7 copy-start
  76.4 19.2 %copy-start.5 = (bf16[128,1536]{1,0:T(8,128)(2,1)S(1)}, bf16[128,1536]{1,0:T(8,128)(2,1)}, u32[]{:S(2)}) copy-start(bf16[128,1536]{1,0:T(8,128)(2,1)} %q_ref.13) | copy-start | bytes 1179652
  76.4 19.2 %copy-start.12 = (bf16[128,1536]{1,0:T(8,128)(2,1)S(1)}, bf16[128,1536]{1,0:T(8,128)(2,1)}, u32[]{:S(2)}) copy-start(bf16[128,1536]{1,0:T(8,128)(2,1)} %copy-done.9) | copy-start | bytes 1179652
  91.6 4.8 %copy-start.1 = (f32[128,768]{1,0:T(8,128)S(1)}, f32[128,768]{1,0:T(8,128)}, u32[]{:S(2)}) copy-start(f32[128,768]{1,0:T(8,128)} %copy-done) | copy-start | bytes 1179652
  91.6 5.5 %collective-permute-start.6 = (f32[576,128]{1,0:T(8,128)S(1)}, f32[576,128]{1,0:T(8,128)S(1)}, u32[]{:S(2)}, u32[]{:S(2)}) collective-permute-start(f32[576,128]{1,0:T(8,128)S(1)} %step_backward_kernel.1), channel_id=1, source_target_pairs={{0,4},{4,0},{1,5},{5,1},{2,6},{6,2},{3,7},{7,3},{8,12},{12,8},{9,1... | collective-permute-start | bytes 884744 | tf_op jit(solution)/shard_map/ppermute | solution.py:512
